TPU v7x, 128 devices: a whole 4x4x4 slice. The times are simulated.
128 devices in a mesh: py: 8 (over x, y_lo), pz: 16 (over z, y_hi, core).
Axes of the slice: x: 4, y: 4 (y_hi: 2, y_lo: 2; y = y_hi * 2 + y_lo), z: 4, core: 2. Of those that a mesh axis runs over, the one named last changes fastest.
Arguments:
- adjoint: bfloat16 [5, 256, 512, 512], P(None, 'pz', 'py'), may hold values from -6 to 6
- state: bfloat16 [5, 256, 512, 512], P(None, 'pz', 'py'), may hold values from -1.5 to 4, as said below
- metric: bfloat16 [3, 256, 512, 512], P(None, 'pz', 'py'), may hold values from 0.5 to 2
- deriv_x: bfloat16 [512, 512], replicated, may hold values from -0.25 to 0.25
- deriv_y: bfloat16 [512, 512], replicated, may hold values from -0.25 to 0.25
- deriv_z: bfloat16 [256, 256], replicated, may hold values from -0.375 to 0.375
- surf_cells: int32 [512, 128], P(('py', 'pz')), may hold values from 0 to 524287, as said below
- surf_normal: bfloat16 [512, 3, 128], P(('py', 'pz')), may hold values from -5 to 5
- shape_basis: bfloat16 [65536, 256], P(('py', 'pz')), may hold values from -16 to 16
Outputs:
- adjoint_out: bfloat16 [5, 256, 512, 512], P(None, 'pz', 'py')
- shape_grad: float32 [256], replicated
Inputs may be any that keep to these rules, and one draw needn't show every extreme that they name: `surf_cells`: each entry of rows r * 4 to (r + 1) * 4 - 1 is z_in * 64 * 512 + y_in * 512 + x for a cell of tile r as the steps define it. `state`: field 0 (density) lies in 0.6 to 1.6 and field 4 (energy) in 2 to 4.
All inputs are finite; a program needn't handle non-finite values.
Results may differ from a plain program's by a relative error of at most 0.0055.
Values may be sent and summed in bfloat16 or wider, within the bound.
No kernel may reach another device: no remote copies, remote signals or barrier semaphores. Data moves between devices by JAX's collectives and lax.ppermute only.
A program may use at most 320 MiB of HBM per device.

v0:
```python
import jax
import jax.numpy as jnp
from jax import lax
from jax.experimental import pallas as pl
from jax.experimental.pallas import tpu as pltpu
from jax.sharding import PartitionSpec as P

gamma_less = 0.4
section_step = 0.5
FIELDS, CZ, CY, NX, NZ = 5, 16, 64, 512, 256
CELLS = 512
BF, F32 = jnp.bfloat16, jnp.float32
VMEM_LIMIT = 48 * 1024 * 1024


def params():
    return pltpu.CompilerParams(vmem_limit_bytes=VMEM_LIMIT)


def cost(flops, nbytes):
    return pl.CostEstimate(flops=int(flops), bytes_accessed=int(nbytes), transcendentals=0)


def line_y_kernel(in_ref, op_ref, out_ref):
    line = in_ref[...].reshape(512, NX)
    out = jnp.dot(op_ref[...], line, preferred_element_type=F32)
    out_ref[...] = out.astype(BF).reshape(out_ref.shape)


def line_y(lines, deriv_t):
    n, f, z = lines.shape[:3]
    spec = pl.BlockSpec((n, 1, 1, CY, NX), lambda i, j: (0, i, j, 0, 0))
    return pl.pallas_call(
        line_y_kernel,
        grid=(f, z),
        in_specs=[spec, pl.BlockSpec((512, 512), lambda i, j: (0, 0))],
        out_specs=spec,
        out_shape=jax.ShapeDtypeStruct(lines.shape, BF),
        compiler_params=params(),
        cost_estimate=cost(2 * lines.size * 512, 4 * lines.size),
        name="line_y",
    )(lines, deriv_t)


def line_z_kernel(in_ref, op_ref, *rest):
    outs, (wide, prod) = rest[:-2], rest[-2:]
    wide[...] = in_ref[...].reshape(NZ * 16, 128).astype(F32)
    for row in range(0, 16, 2):
        pair = [wide[pl.ds(row + i, NZ, stride=16), :].astype(BF) for i in range(2)]
        out = jnp.dot(op_ref[...], jnp.concatenate(pair, axis=1), preferred_element_type=F32)
        for i in range(2):
            prod[pl.ds(row + i, NZ, stride=16), :] = out[:, 128 * i : 128 * (i + 1)]
    whole = prod[...].astype(BF).reshape(16, CZ, 16, 128)
    depth = CZ // len(outs)
    for i, out_ref in enumerate(outs):
        out_ref[...] = whole[:, i * depth : (i + 1) * depth].reshape(out_ref.shape)


def line_z(lines, deriv_t, parts):
    f = lines.shape[1]
    depth = CZ // parts
    return pl.pallas_call(
        line_z_kernel,
        grid=(f,),
        in_specs=[
            pl.BlockSpec((16, 1, CZ, 16, 128), lambda i: (0, i, 0, 0, 0)),
            pl.BlockSpec((NZ, NZ), lambda i: (0, 0)),
        ],
        out_specs=[pl.BlockSpec((16, 1, depth, 16, 128), lambda i: (0, i, 0, 0, 0))] * parts,
        out_shape=[jax.ShapeDtypeStruct((16, f, depth, 16, 128), BF)] * parts,
        scratch_shapes=[pltpu.VMEM((NZ * 16, 128), F32), pltpu.VMEM((NZ * 16, 128), F32)],
        compiler_params=params(),
        cost_estimate=cost(2 * lines.size * NZ, 4 * lines.size),
        name="line_z",
    )(lines, deriv_t)


def update(adj, state, metric, alongs):
    recip = 1.0 / state[0]
    vel = [state[1 + i] * recip for i in range(3)]
    speed_sq = vel[0] * vel[0] + vel[1] * vel[1] + vel[2] * vel[2]
    kinetic = 0.5 * (state[1] * vel[0] + state[2] * vel[1] + state[3] * vel[2])
    enthalpy = (state[4] + gamma_less * (state[4] - kinetic)) * recip
    press = energy = back = None
    mom = [None] * 3
    turn = [None] * 3
    plus = lambda a, b: b if a is None else a + b
    for d in range(3):
        weight, along = metric[d], alongs[d]
        weighted_vel = weight * vel[d]
        turn[d] = weight * (
            along[4] * enthalpy + along[1] * vel[0] + along[2] * vel[1] + along[3] * vel[2]
        )
        back = plus(back, turn[d] * vel[d])
        mom[d] = plus(mom[d], weight * along[0])
        for m in range(3):
            mom[m] = plus(mom[m], weighted_vel * along[1 + m])
        work = weighted_vel * along[4]
        energy = plus(energy, work)
        press = plus(press, weight * along[1 + d] + work)
    press = gamma_less * press
    pulled = [0.5 * speed_sq * press - back]
    pulled += [mom[m] + turn[m] - vel[m] * press for m in range(3)]
    pulled += [energy + press]
    return [adj[f] - section_step * pulled[f] for f in range(5)]


def update_kernel(adj_ref, state_ref, metric_ref, op_ref, y_ref, z_ref, *rest):
    out_ref, along_x = rest[-2:]
    along_x[...] = jnp.dot(
        adj_ref[...].reshape(FIELDS * CY, NX), op_ref[...], preferred_element_type=F32
    ).reshape(FIELDS, CY, NX)

    def body(a, carry):
        rows = pl.ds(pl.multiple_of(a * 16, 16), 16)
        for b in range(4):
            cols = slice(128 * b, 128 * b + 128)
            adj = [adj_ref[f, 0, rows, cols].astype(F32) for f in range(5)]
            state = [state_ref[f, 0, rows, cols].astype(F32) for f in range(5)]
            metric = [metric_ref[d, 0, rows, cols].astype(F32) for d in range(3)]
            alongs = [
                [along_x[f, rows, cols] for f in range(5)],
                [y_ref[0, f, 0, rows, cols].astype(F32) for f in range(5)],
                [z_ref[a * 4 + b, f, 0].astype(F32) for f in range(5)],
            ]
            new = update(adj, state, metric, alongs)
            for f in range(5):
                out_ref[f, 0, rows, cols] = new[f].astype(BF)
        return carry

    lax.fori_loop(0, 4, body, 0)


def update_part(adjoint, state, metric, deriv_x, along_y, along_z, first, old):
    depth = along_z.shape[2]
    plane = lambda n: pl.BlockSpec((n, 1, CY, NX), lambda i: (0, i + first, 0, 0))
    in_specs = [
        plane(5),
        plane(5),
        plane(3),
        pl.BlockSpec((NX, NX), lambda i: (0, 0)),
        pl.BlockSpec((1, 5, 1, CY, NX), lambda i: ((i + first) // 2, 0, (i + first) % 2, 0, 0)),
        pl.BlockSpec((16, 5, 1, 16, 128), lambda i: (0, 0, i, 0, 0)),
    ]
    operands = [adjoint, state, metric, deriv_x, along_y, along_z]
    aliases = {}
    if old is not None:
        in_specs.append(pl.BlockSpec(memory_space=pl.ANY))
        aliases = {len(operands): 0}
        operands.append(old)
    cells = depth * CY * NX
    return pl.pallas_call(
        update_kernel,
        grid=(depth,),
        in_specs=in_specs,
        out_specs=plane(5),
        out_shape=jax.ShapeDtypeStruct(adjoint.shape, BF),
        scratch_shapes=[pltpu.VMEM((FIELDS, CY, NX), F32)],
        input_output_aliases=aliases,
        compiler_params=params(),
        cost_estimate=cost(cells * 2 * 5 * NX + cells * 2000, cells * 56),
        name="update",
    )(*operands)


def pick(field, onehot, x_of):
    rows = jnp.dot(onehot, field, preferred_element_type=F32)
    lane = lax.broadcasted_iota(jnp.int32, (CELLS, NX), 1)
    return jnp.sum(jnp.where(lane == x_of, rows, 0.0), axis=1, keepdims=True)


def pick_kernel(cell_ref, field_ref, out_ref, onehot):
    f = pl.program_id(0)
    cell = cell_ref[:, 0:1]

    @pl.when(f == 0)
    def _():
        row = lax.broadcasted_iota(jnp.int32, (CELLS, CZ * CY), 1)
        onehot[...] = (row == cell // NX).astype(F32).astype(BF)

    value = pick(field_ref[...].reshape(CZ * CY, NX), onehot[...], cell % NX)
    lane = lax.broadcasted_iota(jnp.int32, (CELLS, 128), 1)
    old = jnp.where(f == 0, 0.0, out_ref[...])
    out_ref[...] = jnp.where(lane == f, value, old)


def pick_cells(cells, fields, first, count):
    return pl.pallas_call(
        pick_kernel,
        grid=(count,),
        in_specs=[
            pl.BlockSpec((CELLS, 128), lambda f: (0, 0)),
            pl.BlockSpec((1, CZ, CY, NX), lambda f: (f + first, 0, 0, 0)),
        ],
        out_specs=pl.BlockSpec((CELLS, 128), lambda f: (0, 0)),
        out_shape=jax.ShapeDtypeStruct((CELLS, 128), F32),
        scratch_shapes=[pltpu.VMEM((CELLS, CZ * CY), BF)],
        compiler_params=params(),
        cost_estimate=cost(2 * count * CELLS * CZ * CY * NX, count * CZ * CY * NX * 2),
        name="pick_cells",
    )(cells, fields)


def gradient_kernel(picked_ref, state_ref, normal_ref, basis_ref, out_ref):
    state = [state_ref[:, f : f + 1] for f in range(5)]
    work = sum(state[1 + i] * (state[1 + i] / state[0]) for i in range(3))
    press = gamma_less * (state[4] - 0.5 * work)
    force = sum(normal_ref[:, i : i + 1] * picked_ref[:, i : i + 1] for i in range(3))
    sens = (press * force).astype(BF).astype(F32)
    out_ref[...] = jnp.sum(sens * basis_ref[...].astype(F32), axis=0, keepdims=True)


def gradient_terms(picked, state, normals, basis):
    return pl.pallas_call(
        gradient_kernel,
        out_shape=jax.ShapeDtypeStruct((1, 256), F32),
        compiler_params=params(),
        cost_estimate=cost(4 * basis.size, 2 * basis.size),
        name="gradient_terms",
    )(picked, state, normals, basis)


def shift(value, dx=0, yl=0, dz=0, yh=0, core=0):
    pairs = []
    for device in range(128):
        py, pz = divmod(device, 16)
        x, y_lo = divmod(py, 2)
        z, rest = divmod(pz, 4)
        y_hi, c = divmod(rest, 2)
        to_py = (x + dx) % 4 * 2 + (y_lo ^ yl)
        to_pz = (z + dz) % 4 * 4 + (y_hi ^ yh) * 2 + (c ^ core)
        pairs.append((device, to_py * 16 + to_pz))
    return lax.ppermute(value, ("py", "pz"), pairs)


def sum_devices(value):
    for step in ({"core": 1}, {"yl": 1}, {"yh": 1}):
        value = value + shift(value, **step)
    for axis in ("dx", "dz"):
        one, two, three = [shift(value, **{axis: n}) for n in (1, 2, 3)]
        value = (value + two) + (one + three)
    return value


def on_device(
    adjoint, state, metric, deriv_x, deriv_y, deriv_z, surf_cells, surf_normal, shape_basis
):
    to_y = jnp.transpose(adjoint.reshape(5, 8, 2, CY, NX), (1, 0, 2, 3, 4))
    lines_y = lax.all_to_all(to_y, "py", 0, 0)
    to_z = jnp.transpose(adjoint.reshape(5, CZ, 4, 16, 4, 128), (2, 4, 0, 1, 3, 5))
    lines_z = lax.all_to_all(to_z.reshape(16, 5, CZ, 16, 128), "pz", 0, 0)
    back_y = lax.all_to_all(line_y(lines_y, deriv_y.T), "py", 0, 0)
    parts = line_z(lines_z, deriv_z.T, 2)
    back_z = [lax.all_to_all(part, "pz", 0, 0) for part in parts]

    cells = jnp.broadcast_to(surf_cells.reshape(CELLS, 1), (CELLS, 128))
    normals = jnp.transpose(surf_normal, (0, 2, 1)).reshape(CELLS, 3).astype(F32)
    normals = jnp.pad(normals, ((0, 0), (0, 125)))
    picked_state = pick_cells(cells, state, 0, 5)

    result = None
    for i, part in enumerate(back_z):
        result = update_part(
            adjoint, state, metric, deriv_x, back_y, part, i * CZ // 2, result
        )
    picked_out = pick_cells(cells, result, 1, 3)
    partial_grad = gradient_terms(picked_out, picked_state, normals, shape_basis)
    summed_grad = sum_devices(partial_grad)[0]
    gradient_out = summed_grad / jnp.sqrt(jnp.mean(summed_grad * summed_grad) + 1e-06)
    return (result, gradient_out)


def solution(mesh):
    return jax.shard_map(
        on_device,
        mesh=mesh,
        in_specs=(
            P(None, "pz", "py", None),
            P(None, "pz", "py", None),
            P(None, "pz", "py", None),
            P(),
            P(),
            P(),
            P(("py", "pz"), None),
            P(("py", "pz"), None, None),
            P(("py", "pz"), None),
        ),
        out_specs=(P(None, "pz", "py", None), P()),
        check_vma=False,
    )
```

profile of v0, /device:TPU:1, one launch (start us, length us, event | category | flops | bytes accessed | tf_op | source)
XLA Modules:
  0.0 346.3 jit_solution(11920855708673496432)
XLA Ops:
  0.6 8.3 %reshape.22 = bf16[5,16,4,16,4,128]{5,4,3,2,1,0:T(4,128)(2,1)} reshape(bf16[5,16,64,512]{3,2,1,0:T(8,128)(2,1)} %adj_ref.3) | data formatting | bytes 10485760 | tf_op jit(solution)/shard_map/reshape | solution.py:250
  8.9 6.1 %copy.18 = bf16[5,16,4,16,4,128]{5,3,1,0,4,2:T(8,128)(2,1)} copy(bf16[5,16,4,16,4,128]{5,4,3,2,1,0:T(4,128)(2,1)} %reshape.22) | data formatting | bytes 10485760 | tf_op jit(solution)/shard_map/reshape | solution.py:250
  15.0 9.5 %all-to-all-start.2 = ((bf16[16,5,16,16,128]{4,3,2,1,0:T(8,128)(2,1)}), bf16[16,5,16,16,128]{4,3,2,1,0:T(8,128)(2,1)}, u32[]{:S(2)}, u32[]{:S(2)}) async-start(bf16[16,5,16,16,128]{4,3,2,1,0:T(8,128)(2,1)} %bitcast.19), calls=%async_computation.2 | async-start | bytes 10485760 | tf_op jit(solution)/shard_map/all_to_all | solution.py:251
  24.5 5.5 %copy.22 = bf16[5,8,2,64,512]{4,3,2,0,1:T(8,128)(2,1)} copy(bf16[5,8,2,64,512]{4,3,2,1,0:T(8,128)(2,1)} %bitcast.17) | data formatting | bytes 10485760 | tf_op jit(solution)/shard_map/reshape | solution.py:248
  30.0 56.8 %all-to-all-done.2.in_ref = bf16[16,5,16,16,128]{4,3,2,1,0:T(8,128)(2,1)} async-done(((bf16[16,5,16,16,128]{4,3,2,1,0:T(8,128)(2,1)}), bf16[16,5,16,16,128]{4,3,2,1,0:T(8,128)(2,1)}, u32[]{:S(2)}, u32[]{:S(2)}) %all-to-all-start.2) | async-done | bytes 5242912 | tf_op jit(solution)/shard_map/all_to_all | solution.py:251
  86.8 4.8 %all-to-all-start = ((bf16[8,5,2,64,512]{4,3,2,1,0:T(8,128)(2,1)}), bf16[8,5,2,64,512]{4,3,2,1,0:T(8,128)(2,1)}, u32[]{:S(2)}, u32[]{:S(2)}) async-start(bf16[8,5,2,64,512]{4,3,2,1,0:T(8,128)(2,1)} %bitcast.18), calls=%async_computation | async-start | bytes 10485760 | tf_op jit(solution)/shard_map/all_to_all | solution.py:249
  91.7 8.9 %line_z.1 = (bf16[16,5,8,16,128]{4,3,2,1,0:T(8,128)(2,1)S(1)}, bf16[16,5,8,16,128]{4,3,2,1,0:T(8,128)(2,1)S(1)}) custom-call(bf16[16,5,16,16,128]{4,3,2,1,0:T(8,128)(2,1)} %all-to-all-done.2.in_ref, bf16[256,256]{1,0:T(8,128)(2,1)S(1)} %bitcast.16), custom_call_target="tpu_custom_call" | custom-call | flops 1342177280 | bytes 10485760 | tf_op jit(solution)/shard_map/line_z/pallas_call | solution.py:62
  100.7 1.5 copy-done.3
  102.2 1.6 copy-done.4
  103.8 60.8 %all-to-all-done.in_ref = bf16[8,5,2,64,512]{4,3,2,1,0:T(8,128)(2,1)} async-done(((bf16[8,5,2,64,512]{4,3,2,1,0:T(8,128)(2,1)}), bf16[8,5,2,64,512]{4,3,2,1,0:T(8,128)(2,1)}, u32[]{:S(2)}, u32[]{:S(2)}) %all-to-all-start) | async-done | bytes 5242912 | tf_op jit(solution)/shard_map/all_to_all | solution.py:249
  164.6 5.1 %all-to-all-start.4 = ((bf16[16,5,8,16,128]{4,3,2,1,0:T(8,128)(2,1)}), bf16[16,5,8,16,128]{4,3,2,1,0:T(8,128)(2,1)S(1)}, u32[]{:S(2)}, u32[]{:S(2)}) async-start(bf16[16,5,8,16,128]{4,3,2,1,0:T(8,128)(2,1)} %copy-done.4), calls=%async_computation.4 | async-start | bytes 5242880 | tf_op jit(solution)/shard_map/all_to_all | solution.py:254
  169.7 1.3 copy.17
  170.9 8.2 %line_y.1 = bf16[8,5,2,64,512]{4,3,2,1,0:T(8,128)(2,1)S(1)} custom-call(bf16[8,5,2,64,512]{4,3,2,1,0:T(8,128)(2,1)} %all-to-all-done.in_ref, bf16[512,512]{1,0:T(8,128)(2,1)S(1)} %bitcast.15), custom_call_target="tpu_custom_call" | custom-call | flops 2684354560 | bytes 10485760 | tf_op jit(solution)/shard_map/line_y/pallas_call | solution.py:33
  179.2 2.3 copy-done.2
  181.5 22.4 %all-to-all-done.4.z_ref = bf16[16,5,8,16,128]{4,3,2,1,0:T(8,128)(2,1)S(1)} async-done(((bf16[16,5,8,16,128]{4,3,2,1,0:T(8,128)(2,1)}), bf16[16,5,8,16,128]{4,3,2,1,0:T(8,128)(2,1)S(1)}, u32[]{:S(2)}, u32[]{:S(2)}) %all-to-all-start.4) | async-done | bytes 2621472 | tf_op jit(solution)/shard_map/all_to_all | solution.py:254
  203.9 64.5 %all_to_all.25.y_ref = bf16[8,5,2,64,512]{4,3,2,1,0:T(8,128)(2,1)} all-to-all(bf16[8,5,2,64,512]{4,3,2,1,0:T(8,128)(2,1)} %copy-done.2), channel_id=1, replica_groups=mesh['py'=8,'pz'=16] {'py'}, dimensions={0} | all-to-all | bytes 10485760 | tf_op jit(solution)/shard_map/all_to_all | solution.py:252
  268.4 6.2 %all-to-all-start.3 = ((bf16[16,5,8,16,128]{4,3,2,1,0:T(8,128)(2,1)}), bf16[16,5,8,16,128]{4,3,2,1,0:T(8,128)(2,1)}, u32[]{:S(2)}, u32[]{:S(2)}) async-start(bf16[16,5,8,16,128]{4,3,2,1,0:T(8,128)(2,1)} %copy-done.3), calls=%async_computation.3 | async-start | bytes 5242880 | tf_op jit(solution)/shard_map/all_to_all | solution.py:254
  274.9 2.5 copy-done
  277.4 4.3 %pick_cells.3.state_ref = f32[512,128]{1,0:T(8,128)S(1)} custom-call(s32[512,128]{1,0:T(8,128)S(1)} %broadcast_in_dim.8.cell_ref, bf16[5,16,64,512]{3,2,1,0:T(8,128)(2,1)S(1)} %copy-done), custom_call_target="tpu_custom_call" | custom-call | flops 2684354560 | bytes 5242880 | tf_op jit(solution)/shard_map/pick_cells/pallas_call | solution.py:188
  282.5 11.4 %update.2.rest_0_ = bf16[5,16,64,512]{3,2,1,0:T(8,128)(2,1)} custom-call(bf16[5,16,64,512]{3,2,1,0:T(8,128)(2,1)} %adj_ref.3, bf16[5,16,64,512]{3,2,1,0:T(8,128)(2,1)} %field_ref.1, bf16[3,16,64,512]{3,2,1,0:T(8,128)(2,1)} %metric_ref.3, bf16[512,512]{1,0:T(8,128)(2,1)S(1)} %copy-done.5, bf16[8,5,2,64,512]{4,3,2,1,0:T(8,128)(2,1)} %all_to_all.25.y_ref, ...), custom_call_target="tpu_custom_call" | custom-call | flops 1866465280 | bytes 14680064 | tf_op jit(solution)/shard_map/update/pallas_call | solution.py:152
  293.9 15.0 %all-to-all-done.3.z_ref = bf16[16,5,8,16,128]{4,3,2,1,0:T(8,128)(2,1)} async-done(((bf16[16,5,8,16,128]{4,3,2,1,0:T(8,128)(2,1)}), bf16[16,5,8,16,128]{4,3,2,1,0:T(8,128)(2,1)}, u32[]{:S(2)}, u32[]{:S(2)}) %all-to-all-start.3) | async-done | bytes 2621472 | tf_op jit(solution)/shard_map/all_to_all | solution.py:254
  308.9 11.9 %update.3.field_ref = bf16[5,16,64,512]{3,2,1,0:T(8,128)(2,1)} custom-call(bf16[5,16,64,512]{3,2,1,0:T(8,128)(2,1)} %adj_ref.3, bf16[5,16,64,512]{3,2,1,0:T(8,128)(2,1)} %field_ref.1, bf16[3,16,64,512]{3,2,1,0:T(8,128)(2,1)} %metric_ref.3, bf16[512,512]{1,0:T(8,128)(2,1)S(1)} %copy-done.5, ...), custom_call_target="tpu_custom_call", output_to_operand_aliasing={{}: (6, {})} | custom-call | flops 1866465280 | bytes 14680064 | tf_op jit(solution)/shard_map/update/pallas_call | solution.py:152
  320.8 2.5 copy-done.1
  323.3 2.7 pick_cells.2.picked_ref
  326.8 1.0 collective-permute-start
  328.6 1.3 collective-permute-start.1
  329.9 1.1 collective-permute-done.1
  331.8 3.2 collective-permute-done.2
  335.0 1.5 collective-permute-start.3
  336.6 2.5 collective-permute-start.5
  340.7 1.3 collective-permute-start.7
  342.0 1.4 collective-permute-start.8
  (44 shorter events, 7.4 us)
Async XLA Ops:
  15.0 71.8 %all-to-all-start.2 = ((bf16[16,5,16,16,128]{4,3,2,1,0:T(8,128)(2,1)}), bf16[16,5,16,16,128]{4,3,2,1,0:T(8,128)(2,1)}, u32[]{:S(2)}, u32[]{:S(2)}) async-start(bf16[16,5,16,16,128]{4,3,2,1,0:T(8,128)(2,1)} %bitcast.19), calls=%async_computation.2 | async-start | bytes 10485760 | tf_op jit(solution)/shard_map/all_to_all | solution.py:251
  86.8 4.8 %copy-start.11 = (bf16[256,256]{1,0:T(8,128)(2,1)S(1)}, bf16[256,256]{1,0:T(8,128)(2,1)}, u32[]{:S(2)}) copy-start(bf16[256,256]{1,0:T(8,128)(2,1)} %param.14) | copy-start | bytes 393220
  86.8 77.7 %all-to-all-start = ((bf16[8,5,2,64,512]{4,3,2,1,0:T(8,128)(2,1)}), bf16[8,5,2,64,512]{4,3,2,1,0:T(8,128)(2,1)}, u32[]{:S(2)}, u32[]{:S(2)}) async-start(bf16[8,5,2,64,512]{4,3,2,1,0:T(8,128)(2,1)} %bitcast.18), calls=%async_computation | async-start | bytes 10485760 | tf_op jit(solution)/shard_map/all_to_all | solution.py:249
  100.7 1.5 copy-start.3
  102.2 1.6 copy-start.4
  164.6 39.3 %all-to-all-start.4 = ((bf16[16,5,8,16,128]{4,3,2,1,0:T(8,128)(2,1)}), bf16[16,5,8,16,128]{4,3,2,1,0:T(8,128)(2,1)S(1)}, u32[]{:S(2)}, u32[]{:S(2)}) async-start(bf16[16,5,8,16,128]{4,3,2,1,0:T(8,128)(2,1)} %copy-done.4), calls=%async_computation.4 | async-start | bytes 5242880 | tf_op jit(solution)/shard_map/all_to_all | solution.py:254
  179.2 2.4 copy-start.2
  268.4 6.2 %copy-start.12 = (bf16[4,3,128]{2,0,1:T(4,128)(2,1)S(1)}, bf16[4,3,128]{2,0,1:T(4,128)(2,1)}, u32[]{:S(2)}) copy-start(bf16[4,3,128]{2,0,1:T(4,128)(2,1)} %param.16) | copy-start | bytes 9220
  268.4 6.4 %copy-start.13 = (s32[4,128]{1,0:T(4,128)S(1)}, s32[4,128]{1,0:T(4,128)}, u32[]{:S(2)}) copy-start(s32[4,128]{1,0:T(4,128)} %param.15) | copy-start | bytes 6148
  268.4 40.5 %all-to-all-start.3 = ((bf16[16,5,8,16,128]{4,3,2,1,0:T(8,128)(2,1)}), bf16[16,5,8,16,128]{4,3,2,1,0:T(8,128)(2,1)}, u32[]{:S(2)}, u32[]{:S(2)}) async-start(bf16[16,5,8,16,128]{4,3,2,1,0:T(8,128)(2,1)} %copy-done.3), calls=%async_computation.3 | async-start | bytes 5242880 | tf_op jit(solution)/shard_map/all_to_all | solution.py:254
  274.7 7.7 %copy-start.5 = (bf16[512,512]{1,0:T(8,128)(2,1)S(1)}, bf16[512,512]{1,0:T(8,128)(2,1)}, u32[]{:S(2)}) copy-start(bf16[512,512]{1,0:T(8,128)(2,1)} %op_ref.3) | copy-start | bytes 1572868
  274.9 2.5 copy-start
  277.4 4.3 %copy-start.9 = (s32[512,128]{1,0:T(8,128)}, s32[512,128]{1,0:T(8,128)S(1)}, u32[]{:S(2)}) copy-start(s32[512,128]{1,0:T(8,128)S(1)} %broadcast_in_dim.8.cell_ref) | copy-start | bytes 786436
  281.8 0.7 copy-start.7
  293.9 26.9 %copy-start.10 = (s32[512,128]{1,0:T(8,128)S(1)}, s32[512,128]{1,0:T(8,128)}, u32[]{:S(2)}) copy-start(s32[512,128]{1,0:T(8,128)} %copy-done.9) | copy-start | bytes 786436
  320.8 2.5 copy-start.1
  323.3 2.7 copy-start.6
  323.3 2.8 copy-start.8
  326.8 1.8 collective-permute-start
  328.6 2.4 collective-permute-start.1
  331.0 3.9 %collective-permute-start.2 = (f32[1,256]{1,0:T(1,128)S(1)}, f32[1,256]{1,0:T(1,128)S(1)}, u32[]{:S(2)}, u32[]{:S(2)}) collective-permute-start(f32[1,256]{1,0:T(1,128)S(1)} %add.33), channel_id=1, source_target_pairs={{0,2},{1,3},{2,0},{3,1},{4,6},{5,7},{6,4},{7,5},{8,10},{9,11},{10,... | collective-permute-start | bytes 3080 | tf_op jit(solution)/shard_map/ppermute | solution.py:233
  335.0 4.2 %collective-permute-start.3 = (f32[1,256]{1,0:T(1,128)S(1)}, f32[1,256]{1,0:T(1,128)S(1)}, u32[]{:S(2)}, u32[]{:S(2)}) collective-permute-start(f32[1,256]{1,0:T(1,128)S(1)} %add.34), channel_id=1, source_target_pairs={{0,64},{1,65},{2,66},{3,67},{4,68},{5,69},{6,70},{7,71},{8,72},{9,... | collective-permute-start | bytes 3080 | tf_op jit(solution)/shard_map/ppermute | solution.py:233
  336.5 3.6 %collective-permute-start.4 = (f32[1,256]{1,0:T(1,128)S(1)}, f32[1,256]{1,0:T(1,128)S(1)}, u32[]{:S(2)}, u32[]{:S(2)}) collective-permute-start(f32[1,256]{1,0:T(1,128)S(1)} %add.34), channel_id=1, source_target_pairs={{0,32},{1,33},{2,34},{3,35},{4,36},{5,37},{6,38},{7,39},{8,40},{9,... | collective-permute-start | bytes 3080 | tf_op jit(solution)/shard_map/ppermute | solution.py:233
  336.6 3.5 %collective-permute-start.5 = (f32[1,256]{1,0:T(1,128)S(1)}, f32[1,256]{1,0:T(1,128)S(1)}, u32[]{:S(2)}, u32[]{:S(2)}) collective-permute-start(f32[1,256]{1,0:T(1,128)S(1)} %add.34), channel_id=1, source_target_pairs={{0,96},{1,97},{2,98},{3,99},{4,100},{5,101},{6,102},{7,103},{8,104... | collective-permute-start | bytes 3080 | tf_op jit(solution)/shard_map/ppermute | solution.py:233
  340.1 4.0 %collective-permute-start.6 = (f32[1,256]{1,0:T(1,128)S(1)}, f32[1,256]{1,0:T(1,128)S(1)}, u32[]{:S(2)}, u32[]{:S(2)}) collective-permute-start(f32[1,256]{1,0:T(1,128)S(1)} %add_add_fusion.1), channel_id=1, source_target_pairs={{0,8},{1,9},{2,10},{3,11},{4,12},{5,13},{6,14},{7,15},{8,0},{9,1},... | collective-permute-start | bytes 3080 | tf_op jit(solution)/shard_map/ppermute | solution.py:233
  340.7 3.6 %collective-permute-start.7 = (f32[1,256]{1,0:T(1,128)S(1)}, f32[1,256]{1,0:T(1,128)S(1)}, u32[]{:S(2)}, u32[]{:S(2)}) collective-permute-start(f32[1,256]{1,0:T(1,128)S(1)} %add_add_fusion.1), channel_id=1, source_target_pairs={{0,4},{1,5},{2,6},{3,7},{4,8},{5,9},{6,10},{7,11},{8,12},{9,13},{1... | collective-permute-start | bytes 3080 | tf_op jit(solution)/shard_map/ppermute | solution.py:233
  342.0 2.4 collective-permute-start.8
where the time goes:
time: 352 us; the launch traced here: 346 us
  waiting for transfers between devices  162 us (46%)
  blocking collectives  64.5 us (18%)
  Pallas kernels  48.3 us (14%)
  starting transfers between devices  36 us (10%)
  local copies, waits for them, and re-layouts  32.7 us (9%)
    all_to_all x1, blocking collectives, on_device(): back_y = lax.all_to_all(line_y(lines_y, deriv_y.T), 'py', 0, 0)  64.5 us
    all_to_all x1, waiting for transfers between devices, on_device(): lines_y = lax.all_to_all(to_y, 'py', 0, 0)  60.8 us
    all_to_all x1, waiting for transfers between devices, on_device(): lines_z = lax.all_to_all(to_z.reshape(16, 5, CZ, 16, 128), 'pz', 0, 0)  56.8 us
    all_to_all x2, waiting for transfers between devices, on_device(): back_z = [lax.all_to_all(part, 'pz', 0, 0) for part in parts]  37.3 us
    pallas_call x2, Pallas kernels, update_part(): pl.pallas_call(update_kernel, grid=(depth,), in_specs=in_specs, out_specs...  23.3 us
    reshape x2, local copies, waits for them, and re-layouts, on_device(): adjoint.reshape(5, CZ, 4, 16, 4, 128)  14.4 us
    unnamed x30, local copies, waits for them, and re-layouts  12.5 us
    all_to_all x2, starting transfers between devices, on_device(): back_z = [lax.all_to_all(part, 'pz', 0, 0) for part in parts]  11.3 us
  transfers between devices with their start and end apart: 13, of which 11 were waited for; matrix products, arithmetic and copies ran while one was open for 2% of the time, Pallas kernels for 10%

commit v1 on v0

--- a/solution.py
+++ b/solution.py
@@ -40,6 +40,33 @@
         cost_estimate=cost(2 * lines.size * 512, 4 * lines.size),
         name="line_y",
     )(lines, deriv_t)
+
+
+def pieces_kernel(in_ref, y_ref, z_ref):
+    y_ref[:, 0] = in_ref[0].reshape(y_ref.shape[0], 2, CY, NX)
+    for a in range(4):
+        for b in range(4):
+            z_ref[4 * a + b, 0] = in_ref[0, :, 16 * a : 16 * a + 16, 128 * b : 128 * b + 128]
+
+
+def pieces(adjoint):
+    depth = 8
+    return pl.pallas_call(
+        pieces_kernel,
+        grid=(FIELDS, CZ // depth),
+        in_specs=[pl.BlockSpec((1, depth, CY, NX), lambda f, i: (f, i, 0, 0))],
+        out_specs=[
+            pl.BlockSpec((depth // 2, 1, 2, CY, NX), lambda f, i: (i, f, 0, 0, 0)),
+            pl.BlockSpec((16, 1, depth, 16, 128), lambda f, i: (0, f, i, 0, 0)),
+        ],
+        out_shape=[
+            jax.ShapeDtypeStruct((8, FIELDS, 2, CY, NX), BF),
+            jax.ShapeDtypeStruct((16, FIELDS, CZ, 16, 128), BF),
+        ],
+        compiler_params=params(),
+        cost_estimate=cost(adjoint.size, 6 * adjoint.size),
+        name="pieces",
+    )(adjoint)
 
 
 def line_z_kernel(in_ref, op_ref, *rest):
@@ -131,8 +158,7 @@
     lax.fori_loop(0, 4, body, 0)
 
 
-def update_part(adjoint, state, metric, deriv_x, along_y, along_z, first, old):
-    depth = along_z.shape[2]
+def update_part(adjoint, state, metric, deriv_x, along_y, along_z, first, depth, old, after):
     plane = lambda n: pl.BlockSpec((n, 1, CY, NX), lambda i: (0, i + first, 0, 0))
     in_specs = [
         plane(5),
@@ -140,14 +166,16 @@
         plane(3),
         pl.BlockSpec((NX, NX), lambda i: (0, 0)),
         pl.BlockSpec((1, 5, 1, CY, NX), lambda i: ((i + first) // 2, 0, (i + first) % 2, 0, 0)),
-        pl.BlockSpec((16, 5, 1, 16, 128), lambda i: (0, 0, i, 0, 0)),
+        pl.BlockSpec((16, 5, 1, 16, 128), lambda i: (0, 0, i + first, 0, 0)),
     ]
     operands = [adjoint, state, metric, deriv_x, along_y, along_z]
     aliases = {}
     if old is not None:
-        in_specs.append(pl.BlockSpec(memory_space=pl.ANY))
         aliases = {len(operands): 0}
         operands.append(old)
+    if after is not None:
+        operands.append(after)
+    in_specs += [pl.BlockSpec(memory_space=pl.ANY)] * (len(operands) - len(in_specs))
     cells = depth * CY * NX
     return pl.pallas_call(
         update_kernel,
@@ -158,114 +186,197 @@
         scratch_shapes=[pltpu.VMEM((FIELDS, CY, NX), F32)],
         input_output_aliases=aliases,
         compiler_params=params(),
-        cost_estimate=cost(cells * 2 * 5 * NX + cells * 2000, cells * 56),
+        cost_estimate=cost(cells * 2 * 5 * NX + cells * 10000, cells * 56),
         name="update",
     )(*operands)
 
 
-def pick(field, onehot, x_of):
-    rows = jnp.dot(onehot, field, preferred_element_type=F32)
-    lane = lax.broadcasted_iota(jnp.int32, (CELLS, NX), 1)
-    return jnp.sum(jnp.where(lane == x_of, rows, 0.0), axis=1, keepdims=True)
-
-
-def pick_kernel(cell_ref, field_ref, out_ref, onehot):
+def pick_rows(onehot_ref, row, f):
+    @pl.when(f == 0)
+    def _():
+        count = onehot_ref.shape[1]
+        at = lax.broadcasted_iota(jnp.int32, (CELLS, count), 1)
+        onehot_ref[...] = jnp.where(at == row, 1.0, 0.0).astype(BF)
+
+    return onehot_ref[...]
+
+
+def pick_lane(rows, lane):
+    at = lax.broadcasted_iota(jnp.int32, rows.shape, 1)
+    return jnp.sum(jnp.where(at == lane, rows, 0.0), axis=1, keepdims=True)
+
+
+def keep(held, value, f):
+    lane = lax.broadcasted_iota(jnp.int32, (CELLS, 128), 1)
+    held[...] = jnp.where(lane == f, value, held[...])
+
+
+def pick_kernel(cell_ref, field_ref, out_ref, onehot_ref, held):
     f = pl.program_id(0)
     cell = cell_ref[:, 0:1]
+    onehot = pick_rows(onehot_ref, cell // NX, f)
 
     @pl.when(f == 0)
     def _():
-        row = lax.broadcasted_iota(jnp.int32, (CELLS, CZ * CY), 1)
-        onehot[...] = (row == cell // NX).astype(F32).astype(BF)
-
-    value = pick(field_ref[...].reshape(CZ * CY, NX), onehot[...], cell % NX)
-    lane = lax.broadcasted_iota(jnp.int32, (CELLS, 128), 1)
-    old = jnp.where(f == 0, 0.0, out_ref[...])
-    out_ref[...] = jnp.where(lane == f, value, old)
-
-
-def pick_cells(cells, fields, first, count):
+        held[...] = jnp.zeros_like(held)
+
+    rows = jnp.dot(onehot, field_ref[...].reshape(CZ * CY, NX), preferred_element_type=F32)
+    keep(held, pick_lane(rows, cell % NX), f)
+
+    @pl.when(f == pl.num_programs(0) - 1)
+    def _():
+        out_ref[...] = held[...].T[0:8]
+
+
+def pick_cells(cells, fields, spec, count):
     return pl.pallas_call(
         pick_kernel,
         grid=(count,),
-        in_specs=[
-            pl.BlockSpec((CELLS, 128), lambda f: (0, 0)),
-            pl.BlockSpec((1, CZ, CY, NX), lambda f: (f + first, 0, 0, 0)),
-        ],
-        out_specs=pl.BlockSpec((CELLS, 128), lambda f: (0, 0)),
-        out_shape=jax.ShapeDtypeStruct((CELLS, 128), F32),
-        scratch_shapes=[pltpu.VMEM((CELLS, CZ * CY), BF)],
+        in_specs=[pl.BlockSpec((CELLS, 128), lambda f: (0, 0)), spec],
+        out_specs=pl.BlockSpec((8, CELLS), lambda f: (0, 0)),
+        out_shape=jax.ShapeDtypeStruct((8, CELLS), F32),
+        scratch_shapes=[pltpu.VMEM((CELLS, CZ * CY), BF), pltpu.VMEM((CELLS, 128), F32)],
         compiler_params=params(),
         cost_estimate=cost(2 * count * CELLS * CZ * CY * NX, count * CZ * CY * NX * 2),
         name="pick_cells",
     )(cells, fields)
 
 
-def gradient_kernel(picked_ref, state_ref, normal_ref, basis_ref, out_ref):
-    state = [state_ref[:, f : f + 1] for f in range(5)]
-    work = sum(state[1 + i] * (state[1 + i] / state[0]) for i in range(3))
-    press = gamma_less * (state[4] - 0.5 * work)
-    force = sum(normal_ref[:, i : i + 1] * picked_ref[:, i : i + 1] for i in range(3))
-    sens = (press * force).astype(BF).astype(F32)
-    out_ref[...] = jnp.sum(sens * basis_ref[...].astype(F32), axis=0, keepdims=True)
-
-
-def gradient_terms(picked, state, normals, basis):
-    return pl.pallas_call(
-        gradient_kernel,
-        out_shape=jax.ShapeDtypeStruct((1, 256), F32),
-        compiler_params=params(),
-        cost_estimate=cost(4 * basis.size, 2 * basis.size),
-        name="gradient_terms",
-    )(picked, state, normals, basis)
-
-
-def shift(value, dx=0, yl=0, dz=0, yh=0, core=0):
-    pairs = []
-    for device in range(128):
-        py, pz = divmod(device, 16)
-        x, y_lo = divmod(py, 2)
-        z, rest = divmod(pz, 4)
-        y_hi, c = divmod(rest, 2)
-        to_py = (x + dx) % 4 * 2 + (y_lo ^ yl)
-        to_pz = (z + dz) % 4 * 4 + (y_hi ^ yh) * 2 + (c ^ core)
-        pairs.append((device, to_py * 16 + to_pz))
-    return lax.ppermute(value, ("py", "pz"), pairs)
-
-
-def sum_devices(value):
-    for step in ({"core": 1}, {"yl": 1}, {"yh": 1}):
-        value = value + shift(value, **step)
-    for axis in ("dx", "dz"):
-        one, two, three = [shift(value, **{axis: n}) for n in (1, 2, 3)]
-        value = (value + two) + (one + three)
-    return value
+def pick_x_kernel(cell_ref, field_ref, op_ref, adj_out, along_out, onehot_ref, column, held, along):
+    f = pl.program_id(0)
+    cell = cell_ref[:, 0:1]
+    x = cell % NX
+    onehot = pick_rows(onehot_ref, cell // NX, f)
+
+    @pl.when(f == 0)
+    def _():
+        at = lax.broadcasted_iota(jnp.int32, (CELLS, NX), 1)
+        pick_x = jnp.where(at == x, 1.0, 0.0).astype(BF)
+        column[...] = jnp.dot(pick_x, op_ref[...], preferred_element_type=F32)
+        held[...] = jnp.zeros_like(held)
+        along[...] = jnp.zeros_like(along)
+
+    rows = jnp.dot(onehot, field_ref[...].reshape(CZ * CY, NX), preferred_element_type=F32)
+    keep(held, pick_lane(rows, x), f)
+    keep(along, jnp.sum(rows * column[...], axis=1, keepdims=True), f)
+
+    @pl.when(f == pl.num_programs(0) - 1)
+    def _():
+        adj_out[...] = held[...].T[0:8]
+        along_out[...] = along[...].T[0:8]
+
+
+def pick_x(cells, adjoint, deriv_t):
+    return pl.pallas_call(
+        pick_x_kernel,
+        grid=(FIELDS,),
+        in_specs=[
+            pl.BlockSpec((CELLS, 128), lambda f: (0, 0)),
+            pl.BlockSpec((1, CZ, CY, NX), lambda f: (f, 0, 0, 0)),
+            pl.BlockSpec((NX, NX), lambda f: (0, 0)),
+        ],
+        out_specs=[pl.BlockSpec((8, CELLS), lambda f: (0, 0))] * 2,
+        out_shape=[jax.ShapeDtypeStruct((8, CELLS), F32)] * 2,
+        scratch_shapes=[
+            pltpu.VMEM((CELLS, CZ * CY), BF),
+            pltpu.VMEM((CELLS, NX), F32),
+            pltpu.VMEM((CELLS, 128), F32),
+            pltpu.VMEM((CELLS, 128), F32),
+        ],
+        compiler_params=params(),
+        cost_estimate=cost(2 * 5 * CELLS * CZ * CY * NX, 5 * CZ * CY * NX * 2),
+        name="pick_x",
+    )(cells, adjoint, deriv_t)
+
+
+def surface_kernel(
+    cell_ref, z_ref, adj_ref, x_ref, y_ref, state_ref, metric_ref, normal_ref, basis_ref, out_ref,
+    onehot_ref, held,
+):
+    f = pl.program_id(0)
+    cell = cell_ref[:, 0:1]
+    x, y, z = cell % NX, cell // NX % CY, cell // (NX * CY)
+    row = ((y // 16 * 4 + x // 128) * CZ + z) * 16 + y % 16
+    onehot = pick_rows(onehot_ref, row, f)
+
+    @pl.when(f == 0)
+    def _():
+        held[...] = jnp.zeros_like(held)
+
+    rows = jnp.dot(onehot, z_ref[...].reshape(16 * CZ * 16, 128), preferred_element_type=F32)
+    keep(held, pick_lane(rows, x % 128), f)
+
+    @pl.when(f == FIELDS - 1)
+    def _():
+        lines = lambda ref, n: [ref[i : i + 1, :] for i in range(n)]
+        picked = held[...].T
+        along_z = [picked[i : i + 1, :] for i in range(5)]
+        state = lines(state_ref, 5)
+        new = update(
+            lines(adj_ref, 5), state, lines(metric_ref, 3),
+            [lines(x_ref, 5), lines(y_ref, 5), along_z],
+        )
+        work = sum(state[1 + i] * (state[1 + i] / state[0]) for i in range(3))
+        press = gamma_less * (state[4] - 0.5 * work)
+        normal = lines(normal_ref, 3)
+        force = sum(normal[i] * new[1 + i].astype(BF).astype(F32) for i in range(3))
+        sens = jnp.broadcast_to((press * force).astype(BF), (16, CELLS))
+        out_ref[...] = jnp.dot(sens, basis_ref[...], preferred_element_type=F32)[0:8]
+
+
+def surface_terms(cells, along_z, adj, along_x, along_y, state, metric, normals, basis):
+    small = pl.BlockSpec((8, CELLS), lambda f: (0, 0))
+    return pl.pallas_call(
+        surface_kernel,
+        grid=(FIELDS,),
+        in_specs=[
+            pl.BlockSpec((CELLS, 128), lambda f: (0, 0)),
+            pl.BlockSpec((16, 1, CZ, 16, 128), lambda f: (0, f, 0, 0, 0)),
+            small, small, small, small, small, small,
+            pl.BlockSpec((CELLS, 256), lambda f: (0, 0)),
+        ],
+        out_specs=pl.BlockSpec((8, 256), lambda f: (0, 0)),
+        out_shape=jax.ShapeDtypeStruct((8, 256), F32),
+        scratch_shapes=[pltpu.VMEM((CELLS, 16 * CZ * 16), BF), pltpu.VMEM((CELLS, 128), F32)],
+        compiler_params=params(),
+        cost_estimate=cost(2 * 5 * CELLS * CZ * CY * NX, 5 * CZ * CY * NX * 2),
+        name="surface_terms",
+    )(cells, along_z, adj, along_x, along_y, state, metric, normals, basis)
 
 
 def on_device(
     adjoint, state, metric, deriv_x, deriv_y, deriv_z, surf_cells, surf_normal, shape_basis
 ):
-    to_y = jnp.transpose(adjoint.reshape(5, 8, 2, CY, NX), (1, 0, 2, 3, 4))
+    to_y, to_z = pieces(adjoint)
     lines_y = lax.all_to_all(to_y, "py", 0, 0)
-    to_z = jnp.transpose(adjoint.reshape(5, CZ, 4, 16, 4, 128), (2, 4, 0, 1, 3, 5))
-    lines_z = lax.all_to_all(to_z.reshape(16, 5, CZ, 16, 128), "pz", 0, 0)
-    back_y = lax.all_to_all(line_y(lines_y, deriv_y.T), "py", 0, 0)
-    parts = line_z(lines_z, deriv_z.T, 2)
-    back_z = [lax.all_to_all(part, "pz", 0, 0) for part in parts]
+    surf_cells, to_z, lines_y = lax.optimization_barrier((surf_cells, to_z, lines_y))
+    lines_z = lax.all_to_all(to_z, "pz", 0, 0)
+    products_y, lines_z = lax.optimization_barrier((line_y(lines_y, deriv_y.T), lines_z))
+    back_y = lax.all_to_all(products_y, "py", 0, 0)
+    (products_z,) = line_z(lines_z, deriv_z.T, 1)
 
     cells = jnp.broadcast_to(surf_cells.reshape(CELLS, 1), (CELLS, 128))
-    normals = jnp.transpose(surf_normal, (0, 2, 1)).reshape(CELLS, 3).astype(F32)
-    normals = jnp.pad(normals, ((0, 0), (0, 125)))
-    picked_state = pick_cells(cells, state, 0, 5)
-
-    result = None
-    for i, part in enumerate(back_z):
-        result = update_part(
-            adjoint, state, metric, deriv_x, back_y, part, i * CZ // 2, result
-        )
-    picked_out = pick_cells(cells, result, 1, 3)
-    partial_grad = gradient_terms(picked_out, picked_state, normals, shape_basis)
-    summed_grad = sum_devices(partial_grad)[0]
+    normals = jnp.transpose(surf_normal, (1, 0, 2)).reshape(3, CELLS).astype(F32)
+    normals = jnp.pad(normals, ((0, 5), (0, 0)))
+    plain = pl.BlockSpec((1, CZ, CY, NX), lambda f: (f, 0, 0, 0))
+    picked_state = pick_cells(cells, state, plain, 5)
+    picked_metric = pick_cells(cells, metric, plain, 3)
+    picked_adj, picked_x = pick_x(cells, adjoint, deriv_x.T)
+
+    products_z, back_y = lax.optimization_barrier((products_z, back_y))
+    back_z = lax.all_to_all(products_z, "pz", 0, 0)
+    lines = pl.BlockSpec((8, 1, 2, CY, NX), lambda f: (0, f, 0, 0, 0))
+    picked_y = pick_cells(cells, back_y, lines, 5)
+
+    terms = surface_terms(
+        cells, back_z, picked_adj, picked_x, picked_y, picked_state, picked_metric, normals,
+        shape_basis,
+    )[0:1]
+    result = update_part(
+        adjoint, state, metric, deriv_x, back_y, back_z, 0, CZ, None, terms
+    )
+    all_terms = lax.all_to_all(jnp.broadcast_to(terms, (128, 1, 256)), ("py", "pz"), 0, 0)
+    summed_grad = jnp.sum(all_terms, axis=(0, 1))
     gradient_out = summed_grad / jnp.sqrt(jnp.mean(summed_grad * summed_grad) + 1e-06)
     return (result, gradient_out)
 

time: 352 us -> 340 us (0.966); the launches traced: 346 us -> 338 us
  Pallas kernels: 48.3 us -> 83.6 us
  local copies, waits for them, and re-layouts: 32.7 us -> 12.5 us
  waiting for transfers between devices: 162 us -> 149 us
  starting transfers between devices: 36 us -> 25.2 us
    pallas_call x1 -> x3, Pallas kernels: 0.78 us -> 29.2 us  [the longest x1 14.5 us: surface_terms(): pl.pallas_call(surface_kernel, grid=(FIELDS,), in_specs=[pl.BlockSpec((CE...]
    reshape x3 -> x0, local copies, waits for them, and re-layouts: 19.9 us -> none  [the longest x2 14.4 us: on_device(): adjoint.reshape(5, CZ, 4, 16, 4, 128)]
    ppermute x9 -> x0, starting transfers between devices: 10.5 us -> none  [shift(): return lax.ppermute(value, ('py', 'pz'), pairs)]
    pallas_call x2 -> x3, Pallas kernels: 7.06 us -> 15.7 us  [pick_cells(): pl.pallas_call(pick_kernel, grid=(count,), in_specs=[pl.BlockSpec((CELLS,...]
    ppermute x9 -> x0, waiting for transfers between devices: 7.13 us -> none  [shift(): return lax.ppermute(value, ('py', 'pz'), pairs)]
    all_to_all x4, waiting for transfers between devices: 155 us -> 149 us  [the longest x1 61.5 us: on_device(): back_y = lax.all_to_all(products_y, 'py', 0, 0)]
    pallas_call x2 -> x1, Pallas kernels: 23.3 us -> 21.5 us  [update_part(): pl.pallas_call(update_kernel, grid=(depth,), in_specs=in_specs, out_specs...]
    unnamed x30 -> x32, local copies, waits for them, and re-layouts: 12.5 us -> 11.6 us
  transfers between devices with their start and end apart: 13 -> 4, of which waited for: 11 -> 3; matrix products, arithmetic and copies ran while one was open for 2% -> 0% of each run, Pallas kernels for 10% -> 18%
where the time goes in v1:
time: 340 us; the launch traced here: 338 us
  waiting for transfers between devices  149 us (44%)
  Pallas kernels  83.6 us (25%)
  blocking collectives  65.7 us (19%)
  starting transfers between devices  25.2 us (7%)
  local copies, waits for them, and re-layouts  12.5 us (4%)
    all_to_all x1, blocking collectives, on_device(): lines_y = lax.all_to_all(to_y, 'py', 0, 0)  65.7 us
    all_to_all x1, waiting for transfers between devices, on_device(): back_y = lax.all_to_all(products_y, 'py', 0, 0)  61.5 us
    all_to_all x1, waiting for transfers between devices, on_device(): lines_z = lax.all_to_all(to_z, 'pz', 0, 0)  51.5 us
    all_to_all x1, waiting for transfers between devices, on_device(): back_z = lax.all_to_all(products_z, 'pz', 0, 0)  35.6 us
    pallas_call x1, Pallas kernels, update_part(): pl.pallas_call(update_kernel, grid=(depth,), in_specs=in_specs, out_specs...  21.5 us
    pallas_call x3, Pallas kernels, pick_cells(): pl.pallas_call(pick_kernel, grid=(count,), in_specs=[pl.BlockSpec((CELLS,...  15.7 us
    pallas_call x1, Pallas kernels, surface_terms(): pl.pallas_call(surface_kernel, grid=(FIELDS,), in_specs=[pl.BlockSpec((CE...  14.5 us
    unnamed x32, local copies, waits for them, and re-layouts  11.6 us
  transfers between devices with their start and end apart: 4, of which 3 were waited for; matrix products, arithmetic and copies ran while one was open for 0% of the time, Pallas kernels for 18%

profile of v1, /device:TPU:1, one launch (start us, length us, event | category | flops | bytes accessed | tf_op | source)
XLA Modules:
  0.0 338.5 jit_solution(1475518200056643886)
XLA Ops:
  0.6 8.5 %pieces.1 = (bf16[8,5,2,64,512]{4,3,2,1,0:T(8,128)(2,1)S(1)}, bf16[16,5,16,16,128]{4,3,2,1,0:T(8,128)(2,1)}) custom-call(bf16[5,16,64,512]{3,2,1,0:T(8,128)(2,1)} %adj_ref.1), custom_call_target="tpu_custom_call" | custom-call | flops 2621440 | bytes 15728640 | tf_op jit(solution)/shard_map/pieces/pallas_call | solution.py:54
  9.2 65.7 %all_to_all.25.in_ref = bf16[8,5,2,64,512]{4,3,2,1,0:T(8,128)(2,1)} all-to-all(bf16[8,5,2,64,512]{4,3,2,1,0:T(8,128)(2,1)S(1)} %get-tuple-element.14), channel_id=1, replica_groups=mesh['py'=8,'pz'=16] {'py'}, dimensions={0} | all-to-all | bytes 10485760 | tf_op jit(solution)/shard_map/all_to_all | solution.py:351
  74.8 9.7 %all-to-all-start.1 = ((bf16[16,5,16,16,128]{4,3,2,1,0:T(8,128)(2,1)}), bf16[16,5,16,16,128]{4,3,2,1,0:T(8,128)(2,1)}, u32[]{:S(2)}, u32[]{:S(2)}) async-start(bf16[16,5,16,16,128]{4,3,2,1,0:T(8,128)(2,1)} %get-tuple-element.16), calls=%async_computation.1 | async-start | bytes 10485760 | tf_op jit(solution)/shard_map/all_to_all | solution.py:353
  84.5 0.2 copy.17
  84.7 8.2 %line_y.1 = bf16[8,5,2,64,512]{4,3,2,1,0:T(8,128)(2,1)S(1)} custom-call(bf16[8,5,2,64,512]{4,3,2,1,0:T(8,128)(2,1)} %all_to_all.25.in_ref, bf16[512,512]{1,0:T(8,128)(2,1)S(1)} %bitcast.12), custom_call_target="tpu_custom_call" | custom-call | flops 2684354560 | bytes 10485760 | tf_op jit(solution)/shard_map/line_y/pallas_call | solution.py:33
  93.0 2.3 copy-done.1
  95.3 51.5 %all-to-all-done.1.in_ref = bf16[16,5,16,16,128]{4,3,2,1,0:T(8,128)(2,1)} async-done(((bf16[16,5,16,16,128]{4,3,2,1,0:T(8,128)(2,1)}), bf16[16,5,16,16,128]{4,3,2,1,0:T(8,128)(2,1)}, u32[]{:S(2)}, u32[]{:S(2)}) %all-to-all-start.1) | async-done | bytes 5242912 | tf_op jit(solution)/shard_map/all_to_all | solution.py:353
  146.8 4.7 %all-to-all-start.2 = ((bf16[8,5,2,64,512]{4,3,2,1,0:T(8,128)(2,1)}), bf16[8,5,2,64,512]{4,3,2,1,0:T(8,128)(2,1)}, u32[]{:S(2)}, u32[]{:S(2)}) async-start(bf16[8,5,2,64,512]{4,3,2,1,0:T(8,128)(2,1)} %copy-done.1), calls=%async_computation.2 | async-start | bytes 10485760 | tf_op jit(solution)/shard_map/all_to_all | solution.py:355
  151.5 0.1 copy.18
  151.6 8.9 %line_z.1 = bf16[16,5,16,16,128]{4,3,2,1,0:T(8,128)(2,1)S(1)} custom-call(bf16[16,5,16,16,128]{4,3,2,1,0:T(8,128)(2,1)} %all-to-all-done.1.in_ref, bf16[256,256]{1,0:T(8,128)(2,1)S(1)} %bitcast.14), custom_call_target="tpu_custom_call" | custom-call | flops 1342177280 | bytes 10485760 | tf_op jit(solution)/shard_map/line_z/pallas_call | solution.py:89
  160.5 2.3 copy-done
  162.9 61.5 %all-to-all-done.2.field_ref.y_ref = bf16[8,5,2,64,512]{4,3,2,1,0:T(8,128)(2,1)} async-done(((bf16[8,5,2,64,512]{4,3,2,1,0:T(8,128)(2,1)}), bf16[8,5,2,64,512]{4,3,2,1,0:T(8,128)(2,1)}, u32[]{:S(2)}, u32[]{:S(2)}) %all-to-all-start.2) | async-done | bytes 5242912 | tf_op jit(solution)/shard_map/all_to_all | solution.py:355
  224.4 5.9 %all-to-all-start.3 = ((bf16[16,5,16,16,128]{4,3,2,1,0:T(8,128)(2,1)}), bf16[16,5,16,16,128]{4,3,2,1,0:T(8,128)(2,1)}, u32[]{:S(2)}, u32[]{:S(2)}) async-start(bf16[16,5,16,16,128]{4,3,2,1,0:T(8,128)(2,1)} %copy-done), calls=%async_computation.3 | async-start | bytes 10485760 | tf_op jit(solution)/shard_map/all_to_all | solution.py:367
  230.4 0.0 slice-start
  230.4 0.2 copy.19
  230.6 0.1 broadcast_in_dim.11.cell_ref
  230.8 1.9 copy-done.3
  232.7 3.3 pick_cells.5.metric_ref
  236.0 2.5 copy-done.2
  238.5 6.3 %pick_x.1 = (f32[8,512]{1,0:T(8,128)S(1)}, f32[8,512]{1,0:T(8,128)S(1)}) custom-call(s32[512,128]{1,0:T(8,128)S(1)} %broadcast_in_dim.11.cell_ref, bf16[5,16,64,512]{3,2,1,0:T(8,128)(2,1)S(1)} %copy-done.2, bf16[512,512]{1,0:T(8,128)(2,1)S(1)} %bitcast.13), custom_call_target="tpu_custom_call" | custom-call | flops 2684354560 | bytes 5242880 | tf_op jit(solution)/shard_map/pick_x/pallas_call | solution.py:270
  244.8 5.3 %pick_cells.4.state_ref = f32[8,512]{1,0:T(8,128)S(1)} custom-call(s32[512,128]{1,0:T(8,128)S(1)} %broadcast_in_dim.11.cell_ref, bf16[5,16,64,512]{3,2,1,0:T(8,128)(2,1)S(1)} %bitcast.11), custom_call_target="tpu_custom_call" | custom-call | flops 2684354560 | bytes 5242880 | tf_op jit(solution)/shard_map/pick_cells/pallas_call | solution.py:232
  250.1 7.0 %pick_cells.3.y_ref = f32[8,512]{1,0:T(8,128)S(1)} custom-call(s32[512,128]{1,0:T(8,128)S(1)} %broadcast_in_dim.11.cell_ref, bf16[8,5,2,64,512]{4,3,2,1,0:T(8,128)(2,1)} %all-to-all-done.2.field_ref.y_ref), custom_call_target="tpu_custom_call" | custom-call | flops 2684354560 | bytes 5242880 | tf_op jit(solution)/shard_map/pick_cells/pallas_call | solution.py:232
  257.1 35.6 %all-to-all-done.3.z_ref = bf16[16,5,16,16,128]{4,3,2,1,0:T(8,128)(2,1)} async-done(((bf16[16,5,16,16,128]{4,3,2,1,0:T(8,128)(2,1)}), bf16[16,5,16,16,128]{4,3,2,1,0:T(8,128)(2,1)}, u32[]{:S(2)}, u32[]{:S(2)}) %all-to-all-start.3) | async-done | bytes 5242912 | tf_op jit(solution)/shard_map/all_to_all | solution.py:367
  292.8 0.9 copy-done.7
  293.7 14.5 %surface_terms.1 = f32[8,256]{1,0:T(8,128)S(1)} custom-call(s32[512,128]{1,0:T(8,128)S(1)} %broadcast_in_dim.11.cell_ref, bf16[16,5,16,16,128]{4,3,2,1,0:T(8,128)(2,1)} %all-to-all-done.3.z_ref, f32[8,512]{1,0:T(8,128)S(1)} %get-tuple-element.22.adj_ref, f32[8,512]{1,0:T(8,128)S(1)} %get-tuple-element.23.x_ref, f32[8,512]{1,0:T(8,128)S(1)} %pick_cells.3.y_ref, ...), custom_call_target="tpu_custom_call" | custom-call | flops 2684354560 | bytes 5242880 | tf_op jit(solution)/shard_map/surface_terms/pallas_call | solution.py:329
  308.2 0.7 broadcast_in_dim.12
  308.9 5.0 %all-to-all-start.4 = ((f32[128,1,256]{2,1,0:T(1,128)}), f32[128,1,256]{2,1,0:T(1,128)S(1)}, u32[]{:S(2)}, u32[]{:S(2)}) async-start(f32[128,1,256]{2,1,0:T(1,128)} %broadcast_in_dim.12), calls=%async_computation.4 | async-start | bytes 262144 | tf_op jit(solution)/shard_map/all_to_all | solution.py:378
  313.9 1.0 copy-done.6
  315.0 21.5 %update.1 = bf16[5,16,64,512]{3,2,1,0:T(8,128)(2,1)} custom-call(bf16[5,16,64,512]{3,2,1,0:T(8,128)(2,1)} %adj_ref.1, bf16[5,16,64,512]{3,2,1,0:T(8,128)(2,1)} %state_ref.1, bf16[3,16,64,512]{3,2,1,0:T(8,128)(2,1)S(1)} %copy-done.4, bf16[512,512]{1,0:T(8,128)(2,1)S(1)} %copy-done.6, bf16[8,5,2,64,512]{4,3,2,1,0:T(8,128)(2,1)} %all-to-all-done.2.field_ref.y_ref, ...), custom_call_target="tpu_custom_call" | custom-call | flops 7927234560 | bytes 29360128 | tf_op jit(solution)/shard_map/update/pallas_call | solution.py:180
  336.5 0.2 reduce_sum.18
  336.6 0.6 multiply_reduce_fusion
  337.9 0.6 broadcast_divide_fusion
  (26 shorter events, 0.1 us)
Async XLA Ops:
  74.8 9.7 %copy-start.8 = (bf16[512,512]{1,0:T(8,128)(2,1)S(1)}, bf16[512,512]{1,0:T(8,128)(2,1)}, u32[]{:S(2)}) copy-start(bf16[512,512]{1,0:T(8,128)(2,1)} %param.13) | copy-start | bytes 1572868
  74.8 72.0 %all-to-all-start.1 = ((bf16[16,5,16,16,128]{4,3,2,1,0:T(8,128)(2,1)}), bf16[16,5,16,16,128]{4,3,2,1,0:T(8,128)(2,1)}, u32[]{:S(2)}, u32[]{:S(2)}) async-start(bf16[16,5,16,16,128]{4,3,2,1,0:T(8,128)(2,1)} %get-tuple-element.16), calls=%async_computation.1 | async-start | bytes 10485760 | tf_op jit(solution)/shard_map/all_to_all | solution.py:353
  93.0 2.4 copy-start.1
  95.3 56.2 %copy-start.9 = (bf16[256,256]{1,0:T(8,128)(2,1)S(1)}, bf16[256,256]{1,0:T(8,128)(2,1)}, u32[]{:S(2)}) copy-start(bf16[256,256]{1,0:T(8,128)(2,1)} %param.14) | copy-start | bytes 393220
  146.8 77.6 %all-to-all-start.2 = ((bf16[8,5,2,64,512]{4,3,2,1,0:T(8,128)(2,1)}), bf16[8,5,2,64,512]{4,3,2,1,0:T(8,128)(2,1)}, u32[]{:S(2)}, u32[]{:S(2)}) async-start(bf16[8,5,2,64,512]{4,3,2,1,0:T(8,128)(2,1)} %copy-done.1), calls=%async_computation.2 | async-start | bytes 10485760 | tf_op jit(solution)/shard_map/all_to_all | solution.py:355
  160.5 2.4 copy-start
  162.9 67.5 %copy-start.5 = (bf16[512,512]{1,0:T(8,128)(2,1)S(1)}, bf16[512,512]{1,0:T(8,128)(2,1)}, u32[]{:S(2)}) copy-start(bf16[512,512]{1,0:T(8,128)(2,1)} %op_ref.1) | copy-start | bytes 1572868
  162.9 67.7 %copy-start.10 = (bf16[4,3,128]{2,0,1:T(4,128)(2,1)S(1)}, bf16[4,3,128]{2,0,1:T(4,128)(2,1)}, u32[]{:S(2)}) copy-start(bf16[4,3,128]{2,0,1:T(4,128)(2,1)} %param.16) | copy-start | bytes 9220
  162.9 67.7 %copy-start.11 = (s32[4,128]{1,0:T(4,128)S(1)}, s32[4,128]{1,0:T(4,128)}, u32[]{:S(2)}) copy-start(s32[4,128]{1,0:T(4,128)} %param.15) | copy-start | bytes 6148
  224.4 68.4 %all-to-all-start.3 = ((bf16[16,5,16,16,128]{4,3,2,1,0:T(8,128)(2,1)}), bf16[16,5,16,16,128]{4,3,2,1,0:T(8,128)(2,1)}, u32[]{:S(2)}, u32[]{:S(2)}) async-start(bf16[16,5,16,16,128]{4,3,2,1,0:T(8,128)(2,1)} %copy-done), calls=%async_computation.3 | async-start | bytes 10485760 | tf_op jit(solution)/shard_map/all_to_all | solution.py:367
  230.4 14.4 %slice-start = ((s8[5242880]{0:T(1024)(128)(4,1)}), s8[1048576]{0:T(1024)(128)(4,1)S(1)}, s32[]{:S(2)}) async-start(s8[5242880]{0:T(1024)(128)(4,1)} %bitcast.10), calls=%async_computation.5 | async-start | bytes 2097152
  230.8 1.9 copy-start.3
  236.0 2.5 copy-start.2
  238.5 6.3 %slice-start.1 = ((s8[5242880]{0:T(1024)(128)(4,1)}), s8[4194304]{0:T(1024)(128)(4,1)S(1)}, s32[]{:S(2)}) async-start(s8[5242880]{0:T(1024)(128)(4,1)} %bitcast.10), calls=%async_computation.6 | async-start | bytes 8388608
  257.1 56.8 %copy-start.4 = (bf16[3,16,64,512]{3,2,1,0:T(8,128)(2,1)S(1)}, bf16[3,16,64,512]{3,2,1,0:T(8,128)(2,1)}, u32[]{:S(2)}) copy-start(bf16[3,16,64,512]{3,2,1,0:T(8,128)(2,1)} %metric_ref.1) | copy-start | bytes 9437188
  292.8 1.0 copy-start.7
  308.9 27.6 %all-to-all-start.4 = ((f32[128,1,256]{2,1,0:T(1,128)}), f32[128,1,256]{2,1,0:T(1,128)S(1)}, u32[]{:S(2)}, u32[]{:S(2)}) async-start(f32[128,1,256]{2,1,0:T(1,128)} %broadcast_in_dim.12), calls=%async_computation.4 | async-start | bytes 262144 | tf_op jit(solution)/shard_map/all_to_all | solution.py:378
  313.9 1.0 copy-start.6

commit v2 on v1

--- a/solution.py
+++ b/solution.py
@@ -102,7 +102,7 @@
     )(lines, deriv_t)
 
 
-def update(adj, state, metric, alongs):
+def update(before, state, metric, alongs, directions=(0, 1, 2)):
     recip = 1.0 / state[0]
     vel = [state[1 + i] * recip for i in range(3)]
     speed_sq = vel[0] * vel[0] + vel[1] * vel[1] + vel[2] * vel[2]
@@ -110,16 +110,15 @@
     enthalpy = (state[4] + gamma_less * (state[4] - kinetic)) * recip
     press = energy = back = None
     mom = [None] * 3
-    turn = [None] * 3
     plus = lambda a, b: b if a is None else a + b
-    for d in range(3):
+    for d in directions:
         weight, along = metric[d], alongs[d]
         weighted_vel = weight * vel[d]
-        turn[d] = weight * (
+        turn = weight * (
             along[4] * enthalpy + along[1] * vel[0] + along[2] * vel[1] + along[3] * vel[2]
         )
-        back = plus(back, turn[d] * vel[d])
-        mom[d] = plus(mom[d], weight * along[0])
+        back = plus(back, turn * vel[d])
+        mom[d] = plus(mom[d], weight * along[0] + turn)
         for m in range(3):
             mom[m] = plus(mom[m], weighted_vel * along[1 + m])
         work = weighted_vel * along[4]
@@ -127,68 +126,93 @@
         press = plus(press, weight * along[1 + d] + work)
     press = gamma_less * press
     pulled = [0.5 * speed_sq * press - back]
-    pulled += [mom[m] + turn[m] - vel[m] * press for m in range(3)]
+    pulled += [mom[m] - vel[m] * press for m in range(3)]
     pulled += [energy + press]
-    return [adj[f] - section_step * pulled[f] for f in range(5)]
-
-
-def update_kernel(adj_ref, state_ref, metric_ref, op_ref, y_ref, z_ref, *rest):
-    out_ref, along_x = rest[-2:]
+    return [before[f] - section_step * pulled[f] for f in range(5)]
+
+
+def chunks(body):
+    def step(a, carry):
+        rows = pl.ds(pl.multiple_of(a * 16, 16), 16)
+        for b in range(4):
+            body(a * 4 + b, rows, slice(128 * b, 128 * b + 128))
+        return carry
+
+    lax.fori_loop(0, 4, step, 0)
+
+
+def update_xy_kernel(adj_ref, state_ref, metric_ref, op_ref, y_ref, out_ref, along_x):
     along_x[...] = jnp.dot(
         adj_ref[...].reshape(FIELDS * CY, NX), op_ref[...], preferred_element_type=F32
     ).reshape(FIELDS, CY, NX)
 
-    def body(a, carry):
-        rows = pl.ds(pl.multiple_of(a * 16, 16), 16)
-        for b in range(4):
-            cols = slice(128 * b, 128 * b + 128)
-            adj = [adj_ref[f, 0, rows, cols].astype(F32) for f in range(5)]
-            state = [state_ref[f, 0, rows, cols].astype(F32) for f in range(5)]
-            metric = [metric_ref[d, 0, rows, cols].astype(F32) for d in range(3)]
-            alongs = [
-                [along_x[f, rows, cols] for f in range(5)],
-                [y_ref[0, f, 0, rows, cols].astype(F32) for f in range(5)],
-                [z_ref[a * 4 + b, f, 0].astype(F32) for f in range(5)],
-            ]
-            new = update(adj, state, metric, alongs)
-            for f in range(5):
-                out_ref[f, 0, rows, cols] = new[f].astype(BF)
-        return carry
-
-    lax.fori_loop(0, 4, body, 0)
-
-
-def update_part(adjoint, state, metric, deriv_x, along_y, along_z, first, depth, old, after):
-    plane = lambda n: pl.BlockSpec((n, 1, CY, NX), lambda i: (0, i + first, 0, 0))
-    in_specs = [
-        plane(5),
-        plane(5),
-        plane(3),
-        pl.BlockSpec((NX, NX), lambda i: (0, 0)),
-        pl.BlockSpec((1, 5, 1, CY, NX), lambda i: ((i + first) // 2, 0, (i + first) % 2, 0, 0)),
-        pl.BlockSpec((16, 5, 1, 16, 128), lambda i: (0, 0, i + first, 0, 0)),
-    ]
-    operands = [adjoint, state, metric, deriv_x, along_y, along_z]
-    aliases = {}
-    if old is not None:
-        aliases = {len(operands): 0}
-        operands.append(old)
-    if after is not None:
-        operands.append(after)
-    in_specs += [pl.BlockSpec(memory_space=pl.ANY)] * (len(operands) - len(in_specs))
-    cells = depth * CY * NX
-    return pl.pallas_call(
-        update_kernel,
-        grid=(depth,),
-        in_specs=in_specs,
+    def body(piece, rows, cols):
+        load = lambda ref, n: [ref[f, 0, rows, cols].astype(F32) for f in range(n)]
+        alongs = [
+            [along_x[f, rows, cols] for f in range(5)],
+            [y_ref[0, f, 0, rows, cols].astype(F32) for f in range(5)],
+        ]
+        new = update(load(adj_ref, 5), load(state_ref, 5), load(metric_ref, 2), alongs, (0, 1))
+        for f in range(5):
+            out_ref[f, 0, rows, cols] = new[f]
+
+    chunks(body)
+
+
+def update_xy(adjoint, state, metric, deriv_x, along_y):
+    plane = lambda n: pl.BlockSpec((n, 1, CY, NX), lambda i: (0, i, 0, 0))
+    cells = CZ * CY * NX
+    return pl.pallas_call(
+        update_xy_kernel,
+        grid=(CZ,),
+        in_specs=[
+            plane(5),
+            plane(5),
+            plane(2),
+            pl.BlockSpec((NX, NX), lambda i: (0, 0)),
+            pl.BlockSpec((1, 5, 1, CY, NX), lambda i: (i // 2, 0, i % 2, 0, 0)),
+        ],
         out_specs=plane(5),
-        out_shape=jax.ShapeDtypeStruct(adjoint.shape, BF),
+        out_shape=jax.ShapeDtypeStruct(adjoint.shape, F32),
         scratch_shapes=[pltpu.VMEM((FIELDS, CY, NX), F32)],
-        input_output_aliases=aliases,
-        compiler_params=params(),
-        cost_estimate=cost(cells * 2 * 5 * NX + cells * 10000, cells * 56),
-        name="update",
-    )(*operands)
+        compiler_params=params(),
+        cost_estimate=cost(cells * 2 * 5 * NX + cells * 10000, cells * 54),
+        name="update_xy",
+    )(adjoint, state, metric, deriv_x, along_y)
+
+
+def update_z_kernel(before_ref, state_ref, metric_ref, z_ref, after_ref, out_ref):
+    def body(piece, rows, cols):
+        before = [before_ref[f, 0, rows, cols] for f in range(5)]
+        state = [state_ref[f, 0, rows, cols].astype(F32) for f in range(5)]
+        metric = {2: metric_ref[0, 0, rows, cols].astype(F32)}
+        along = {2: [z_ref[piece, f, 0].astype(F32) for f in range(5)]}
+        new = update(before, state, metric, along, (2,))
+        for f in range(5):
+            out_ref[f, 0, rows, cols] = new[f].astype(BF)
+
+    chunks(body)
+
+
+def update_z(before, state, metric, along_z, after):
+    plane = lambda n: pl.BlockSpec((n, 1, CY, NX), lambda i: (0, i, 0, 0))
+    cells = CZ * CY * NX
+    return pl.pallas_call(
+        update_z_kernel,
+        grid=(CZ,),
+        in_specs=[
+            plane(5),
+            plane(5),
+            pl.BlockSpec((1, 1, CY, NX), lambda i: (2, i, 0, 0)),
+            pl.BlockSpec((16, 5, 1, 16, 128), lambda i: (0, 0, i, 0, 0)),
+            pl.BlockSpec(memory_space=pl.ANY),
+        ],
+        out_specs=plane(5),
+        out_shape=jax.ShapeDtypeStruct(state.shape, BF),
+        compiler_params=params(),
+        cost_estimate=cost(cells * 10000, cells * 52),
+        name="update_z",
+    )(before, state, metric, along_z, after)
 
 
 def pick_rows(onehot_ref, row, f):
@@ -289,27 +313,52 @@
     )(cells, adjoint, deriv_t)
 
 
-def surface_kernel(
-    cell_ref, z_ref, adj_ref, x_ref, y_ref, state_ref, metric_ref, normal_ref, basis_ref, out_ref,
-    onehot_ref, held,
-):
-    f = pl.program_id(0)
+def rows_z_kernel(cell_ref, out_ref):
     cell = cell_ref[:, 0:1]
     x, y, z = cell % NX, cell // NX % CY, cell // (NX * CY)
-    row = ((y // 16 * 4 + x // 128) * CZ + z) * 16 + y % 16
-    onehot = pick_rows(onehot_ref, row, f)
-
-    @pl.when(f == 0)
-    def _():
-        held[...] = jnp.zeros_like(held)
-
-    rows = jnp.dot(onehot, z_ref[...].reshape(16 * CZ * 16, 128), preferred_element_type=F32)
-    keep(held, pick_lane(rows, x % 128), f)
-
-    @pl.when(f == FIELDS - 1)
-    def _():
+    row = ((y // 16 * 4 + x // 128) * CZ + z) * 16 + y % 16 - pl.program_id(0) * 1024
+    at = lax.broadcasted_iota(jnp.int32, (CELLS, 1024), 1)
+    out_ref[...] = jnp.where(at == row, 1.0, 0.0).astype(BF)
+
+
+def rows_z(cells):
+    return pl.pallas_call(
+        rows_z_kernel,
+        grid=(4,),
+        in_specs=[pl.BlockSpec((CELLS, 128), lambda i: (0, 0))],
+        out_specs=pl.BlockSpec((CELLS, 1024), lambda i: (0, i)),
+        out_shape=jax.ShapeDtypeStruct((CELLS, 4096), BF),
+        compiler_params=params(),
+        cost_estimate=cost(CELLS * 4096 * 10, CELLS * 4096 * 2),
+        name="rows_z",
+    )(cells)
+
+
+def surface_kernel(
+    cell_ref, onehot_ref, z_ref, adj_ref, x_ref, y_ref, state_ref, metric_ref, normal_ref,
+    basis_ref, out_ref, total,
+):
+    step = pl.program_id(0)
+
+    @pl.when(step == 0)
+    def _():
+        total[...] = jnp.zeros_like(total)
+
+    fields = [z_ref[:, f].reshape(1024, 128) for f in range(FIELDS)]
+    total[...] += jnp.dot(
+        onehot_ref[...], jnp.concatenate(fields, axis=1), preferred_element_type=F32
+    )
+
+    @pl.when(step == pl.num_programs(0) - 1)
+    def _():
+        lane = lax.broadcasted_iota(jnp.int32, (CELLS, 128), 1)
+        here = lane == cell_ref[:, 0:1] % 128
+        held = jnp.zeros((CELLS, 128), F32)
+        for f in range(FIELDS):
+            value = jnp.where(here, total[:, 128 * f : 128 * (f + 1)], 0.0)
+            held = jnp.where(lane == f, jnp.sum(value, axis=1, keepdims=True), held)
         lines = lambda ref, n: [ref[i : i + 1, :] for i in range(n)]
-        picked = held[...].T
+        picked = held.T
         along_z = [picked[i : i + 1, :] for i in range(5)]
         state = lines(state_ref, 5)
         new = update(
@@ -324,24 +373,25 @@
         out_ref[...] = jnp.dot(sens, basis_ref[...], preferred_element_type=F32)[0:8]
 
 
-def surface_terms(cells, along_z, adj, along_x, along_y, state, metric, normals, basis):
-    small = pl.BlockSpec((8, CELLS), lambda f: (0, 0))
+def surface_terms(cells, onehot, along_z, adj, along_x, along_y, state, metric, normals, basis):
+    small = pl.BlockSpec((8, CELLS), lambda i: (0, 0))
     return pl.pallas_call(
         surface_kernel,
-        grid=(FIELDS,),
+        grid=(4,),
         in_specs=[
-            pl.BlockSpec((CELLS, 128), lambda f: (0, 0)),
-            pl.BlockSpec((16, 1, CZ, 16, 128), lambda f: (0, f, 0, 0, 0)),
+            pl.BlockSpec((CELLS, 128), lambda i: (0, 0)),
+            pl.BlockSpec((CELLS, 1024), lambda i: (0, i)),
+            pl.BlockSpec((4, FIELDS, CZ, 16, 128), lambda i: (i, 0, 0, 0, 0)),
             small, small, small, small, small, small,
-            pl.BlockSpec((CELLS, 256), lambda f: (0, 0)),
-        ],
-        out_specs=pl.BlockSpec((8, 256), lambda f: (0, 0)),
+            pl.BlockSpec((CELLS, 256), lambda i: (0, 0)),
+        ],
+        out_specs=pl.BlockSpec((8, 256), lambda i: (0, 0)),
         out_shape=jax.ShapeDtypeStruct((8, 256), F32),
-        scratch_shapes=[pltpu.VMEM((CELLS, 16 * CZ * 16), BF), pltpu.VMEM((CELLS, 128), F32)],
+        scratch_shapes=[pltpu.VMEM((CELLS, FIELDS * 128), F32)],
         compiler_params=params(),
         cost_estimate=cost(2 * 5 * CELLS * CZ * CY * NX, 5 * CZ * CY * NX * 2),
         name="surface_terms",
-    )(cells, along_z, adj, along_x, along_y, state, metric, normals, basis)
+    )(cells, onehot, along_z, adj, along_x, along_y, state, metric, normals, basis)
 
 
 def on_device(
@@ -367,14 +417,16 @@
     back_z = lax.all_to_all(products_z, "pz", 0, 0)
     lines = pl.BlockSpec((8, 1, 2, CY, NX), lambda f: (0, f, 0, 0, 0))
     picked_y = pick_cells(cells, back_y, lines, 5)
-
+    before = update_xy(adjoint, state, metric, deriv_x, back_y)
+
+    back_z, before, onehot, picked_y = lax.optimization_barrier(
+        (back_z, before, rows_z(cells), picked_y)
+    )
     terms = surface_terms(
-        cells, back_z, picked_adj, picked_x, picked_y, picked_state, picked_metric, normals,
-        shape_basis,
+        cells, onehot, back_z, picked_adj, picked_x, picked_y, picked_state,
+        picked_metric, normals, shape_basis,
     )[0:1]
-    result = update_part(
-        adjoint, state, metric, deriv_x, back_y, back_z, 0, CZ, None, terms
-    )
+    result = update_z(before, state, metric, back_z, terms)
     all_terms = lax.all_to_all(jnp.broadcast_to(terms, (128, 1, 256)), ("py", "pz"), 0, 0)
     summed_grad = jnp.sum(all_terms, axis=(0, 1))
     gradient_out = summed_grad / jnp.sqrt(jnp.mean(summed_grad * summed_grad) + 1e-06)

time: 340 us -> 329 us (0.968)
  waiting for transfers between devices: 149 us -> 122 us
  Pallas kernels: 83.6 us -> 95.2 us
    all_to_all x1, waiting for transfers between devices: 35.6 us -> 9.18 us  [on_device(): back_z = lax.all_to_all(products_z, 'pz', 0, 0)]
    pallas_call x2 -> x4, Pallas kernels: 36 us -> 47.4 us  [the longest x1 20.3 us: update_xy(): pl.pallas_call(update_xy_kernel, grid=(CZ,), in_specs=[plane(5), plane(5)...]
    unnamed x32 -> x36, local copies, waits for them, and re-layouts: 11.6 us -> 14.8 us
  transfers between devices with their start and end apart: 4 -> 4, of which waited for: 3 -> 3; matrix products, arithmetic and copies ran while one was open for 0% -> 0% of each run, Pallas kernels for 18% -> 24%
where the time goes in v2:
time: 329 us; the launch traced here: 327 us
  waiting for transfers between devices  122 us (37%)
  Pallas kernels  95.2 us (29%)
  blocking collectives  65.7 us (20%)
  starting transfers between devices  25.4 us (8%)
  local copies, waits for them, and re-layouts  15.7 us (5%)
    all_to_all x1, blocking collectives, on_device(): lines_y = lax.all_to_all(to_y, 'py', 0, 0)  65.7 us
    all_to_all x1, waiting for transfers between devices, on_device(): back_y = lax.all_to_all(products_y, 'py', 0, 0)  61.5 us
    all_to_all x1, waiting for transfers between devices, on_device(): lines_z = lax.all_to_all(to_z, 'pz', 0, 0)  51.5 us
    pallas_call x1, Pallas kernels, update_xy(): pl.pallas_call(update_xy_kernel, grid=(CZ,), in_specs=[plane(5), plane(5)...  20.3 us
    pallas_call x1, Pallas kernels, update_z(): pl.pallas_call(update_z_kernel, grid=(CZ,), in_specs=[plane(5), plane(5),...  16.4 us
    pallas_call x3, Pallas kernels, pick_cells(): pl.pallas_call(pick_kernel, grid=(count,), in_specs=[pl.BlockSpec((CELLS,...  15.8 us
    unnamed x36, local copies, waits for them, and re-layouts  14.8 us
    all_to_all x1, starting transfers between devices, on_device(): lines_z = lax.all_to_all(to_z, 'pz', 0, 0)  9.66 us
  transfers between devices with their start and end apart: 4, of which 3 were waited for; matrix products, arithmetic and copies ran while one was open for 0% of the time, Pallas kernels for 24%

profile of v2, /device:TPU:1, one launch (start us, length us, event | category | flops | bytes accessed | tf_op | source)
XLA Modules:
  0.0 326.9 jit_solution(5688490879149564220)
XLA Ops:
  0.6 8.5 %pieces.1 = (bf16[8,5,2,64,512]{4,3,2,1,0:T(8,128)(2,1)S(1)}, bf16[16,5,16,16,128]{4,3,2,1,0:T(8,128)(2,1)}) custom-call(bf16[5,16,64,512]{3,2,1,0:T(8,128)(2,1)} %field_ref.3), custom_call_target="tpu_custom_call" | custom-call | flops 2621440 | bytes 15728640 | tf_op jit(solution)/shard_map/pieces/pallas_call | solution.py:54
  9.2 65.7 %all_to_all.25.in_ref = bf16[8,5,2,64,512]{4,3,2,1,0:T(8,128)(2,1)} all-to-all(bf16[8,5,2,64,512]{4,3,2,1,0:T(8,128)(2,1)S(1)} %get-tuple-element.18), channel_id=1, replica_groups=mesh['py'=8,'pz'=16] {'py'}, dimensions={0} | all-to-all | bytes 10485760 | tf_op jit(solution)/shard_map/all_to_all | solution.py:401
  74.8 9.7 %all-to-all-start.1 = ((bf16[16,5,16,16,128]{4,3,2,1,0:T(8,128)(2,1)}), bf16[16,5,16,16,128]{4,3,2,1,0:T(8,128)(2,1)}, u32[]{:S(2)}, u32[]{:S(2)}) async-start(bf16[16,5,16,16,128]{4,3,2,1,0:T(8,128)(2,1)} %get-tuple-element.20), calls=%async_computation.1 | async-start | bytes 10485760 | tf_op jit(solution)/shard_map/all_to_all | solution.py:403
  84.5 0.2 copy.17
  84.7 8.2 %line_y.1 = bf16[8,5,2,64,512]{4,3,2,1,0:T(8,128)(2,1)S(1)} custom-call(bf16[8,5,2,64,512]{4,3,2,1,0:T(8,128)(2,1)} %all_to_all.25.in_ref, bf16[512,512]{1,0:T(8,128)(2,1)S(1)} %bitcast.12), custom_call_target="tpu_custom_call" | custom-call | flops 2684354560 | bytes 10485760 | tf_op jit(solution)/shard_map/line_y/pallas_call | solution.py:33
  93.0 2.4 copy-done.2
  95.3 51.5 %all-to-all-done.1.in_ref = bf16[16,5,16,16,128]{4,3,2,1,0:T(8,128)(2,1)} async-done(((bf16[16,5,16,16,128]{4,3,2,1,0:T(8,128)(2,1)}), bf16[16,5,16,16,128]{4,3,2,1,0:T(8,128)(2,1)}, u32[]{:S(2)}, u32[]{:S(2)}) %all-to-all-start.1) | async-done | bytes 5242912 | tf_op jit(solution)/shard_map/all_to_all | solution.py:403
  146.8 4.7 %all-to-all-start.2 = ((bf16[8,5,2,64,512]{4,3,2,1,0:T(8,128)(2,1)}), bf16[8,5,2,64,512]{4,3,2,1,0:T(8,128)(2,1)}, u32[]{:S(2)}, u32[]{:S(2)}) async-start(bf16[8,5,2,64,512]{4,3,2,1,0:T(8,128)(2,1)} %copy-done.2), calls=%async_computation.2 | async-start | bytes 10485760 | tf_op jit(solution)/shard_map/all_to_all | solution.py:405
  151.6 8.9 %line_z.1 = bf16[16,5,16,16,128]{4,3,2,1,0:T(8,128)(2,1)S(1)} custom-call(bf16[16,5,16,16,128]{4,3,2,1,0:T(8,128)(2,1)} %all-to-all-done.1.in_ref, bf16[256,256]{1,0:T(8,128)(2,1)S(1)} %bitcast.14), custom_call_target="tpu_custom_call" | custom-call | flops 1342177280 | bytes 10485760 | tf_op jit(solution)/shard_map/line_z/pallas_call | solution.py:89
  160.5 2.3 copy-done.1
  162.9 61.5 %all-to-all-done.2.y_ref.field_ref = bf16[8,5,2,64,512]{4,3,2,1,0:T(8,128)(2,1)} async-done(((bf16[8,5,2,64,512]{4,3,2,1,0:T(8,128)(2,1)}), bf16[8,5,2,64,512]{4,3,2,1,0:T(8,128)(2,1)}, u32[]{:S(2)}, u32[]{:S(2)}) %all-to-all-start.2) | async-done | bytes 5242912 | tf_op jit(solution)/shard_map/all_to_all | solution.py:405
  224.4 6.1 %all-to-all-start.3 = ((bf16[16,5,16,16,128]{4,3,2,1,0:T(8,128)(2,1)}), bf16[16,5,16,16,128]{4,3,2,1,0:T(8,128)(2,1)}, u32[]{:S(2)}, u32[]{:S(2)}) async-start(bf16[16,5,16,16,128]{4,3,2,1,0:T(8,128)(2,1)} %copy-done.1), calls=%async_computation.3 | async-start | bytes 10485760 | tf_op jit(solution)/shard_map/all_to_all | solution.py:417
  230.5 0.2 copy.19
  230.9 4.0 %rows_z.1.onehot_ref = bf16[512,4096]{1,0:T(8,128)(2,1)S(1)} custom-call(s32[512,128]{1,0:T(8,128)S(1)} %broadcast_in_dim.11.cell_ref), custom_call_target="tpu_custom_call" | custom-call | flops 20971520 | bytes 4194304 | tf_op jit(solution)/shard_map/rows_z/pallas_call | solution.py:325
  235.0 2.0 copy-done.3
  236.9 1.9 copy-done.5
  238.8 3.3 %pick_cells.5.metric_ref = f32[8,512]{1,0:T(8,128)S(1)} custom-call(s32[512,128]{1,0:T(8,128)S(1)} %broadcast_in_dim.11.cell_ref, bf16[3,16,64,512]{3,2,1,0:T(8,128)(2,1)S(1)} %copy-done.5), custom_call_target="tpu_custom_call" | custom-call | flops 1610612736 | bytes 3145728 | tf_op jit(solution)/shard_map/pick_cells/pallas_call | solution.py:256
  242.2 2.5 copy-done
  244.6 6.3 %pick_x.1 = (f32[8,512]{1,0:T(8,128)S(1)}, f32[8,512]{1,0:T(8,128)S(1)}) custom-call(s32[512,128]{1,0:T(8,128)S(1)} %broadcast_in_dim.11.cell_ref, bf16[5,16,64,512]{3,2,1,0:T(8,128)(2,1)S(1)} %copy-done, bf16[512,512]{1,0:T(8,128)(2,1)S(1)} %bitcast.13), custom_call_target="tpu_custom_call" | custom-call | flops 2684354560 | bytes 5242880 | tf_op jit(solution)/shard_map/pick_x/pallas_call | solution.py:294
  250.9 5.3 %pick_cells.4.state_ref = f32[8,512]{1,0:T(8,128)S(1)} custom-call(s32[512,128]{1,0:T(8,128)S(1)} %broadcast_in_dim.11.cell_ref, bf16[5,16,64,512]{3,2,1,0:T(8,128)(2,1)S(1)} %bitcast.11), custom_call_target="tpu_custom_call" | custom-call | flops 2684354560 | bytes 5242880 | tf_op jit(solution)/shard_map/pick_cells/pallas_call | solution.py:256
  256.3 7.2 %pick_cells.3.y_ref = f32[8,512]{1,0:T(8,128)S(1)} custom-call(s32[512,128]{1,0:T(8,128)S(1)} %broadcast_in_dim.11.cell_ref, bf16[8,5,2,64,512]{4,3,2,1,0:T(8,128)(2,1)} %all-to-all-done.2.y_ref.field_ref), custom_call_target="tpu_custom_call" | custom-call | flops 2684354560 | bytes 5242880 | tf_op jit(solution)/shard_map/pick_cells/pallas_call | solution.py:256
  263.5 20.3 %update_xy.1.before_ref = f32[5,16,64,512]{3,2,1,0:T(8,128)} custom-call(bf16[5,16,64,512]{3,2,1,0:T(8,128)(2,1)} %field_ref.3, bf16[5,16,64,512]{3,2,1,0:T(8,128)(2,1)} %state_ref.3, bf16[3,16,64,512]{3,2,1,0:T(8,128)(2,1)S(1)} %copy-done.6, bf16[512,512]{1,0:T(8,128)(2,1)S(1)} %copy-done.8, bf16[8,5,2,64,512]{4,3,2,1,0:T(8,128)(2,1)} %all-to-all-done.2.y_ref.field_ref), custom_call_target="tpu_custom_call" | custom-call | flops 7927234560 | bytes 28311552 | tf_op jit(solution)/shard_map/update_xy/pallas_call | solution.py:165
  283.7 9.2 %all-to-all-done.3.z_ref = bf16[16,5,16,16,128]{4,3,2,1,0:T(8,128)(2,1)} async-done(((bf16[16,5,16,16,128]{4,3,2,1,0:T(8,128)(2,1)}), bf16[16,5,16,16,128]{4,3,2,1,0:T(8,128)(2,1)}, u32[]{:S(2)}, u32[]{:S(2)}) %all-to-all-start.3) | async-done | bytes 5242912 | tf_op jit(solution)/shard_map/all_to_all | solution.py:417
  292.9 2.2 copy-done.4
  295.1 0.9 copy-done.9
  296.0 6.7 %surface_terms.1 = f32[8,256]{1,0:T(8,128)S(1)} custom-call(s32[512,128]{1,0:T(8,128)S(1)} %broadcast_in_dim.11.cell_ref, bf16[512,4096]{1,0:T(8,128)(2,1)S(1)} %copy-done.4, bf16[16,5,16,16,128]{4,3,2,1,0:T(8,128)(2,1)} %all-to-all-done.3.z_ref, f32[8,512]{1,0:T(8,128)S(1)} %get-tuple-element.29.adj_ref, f32[8,512]{1,0:T(8,128)S(1)} %get-tuple-element.30.x_ref, ...), custom_call_target="tpu_custom_call" | custom-call | flops 2684354560 | bytes 5242880 | tf_op jit(solution)/shard_map/surface_terms/pallas_call | solution.py:378
  302.7 0.7 broadcast_in_dim.12
  303.5 5.0 %all-to-all-start.4 = ((f32[128,1,256]{2,1,0:T(1,128)}), f32[128,1,256]{2,1,0:T(1,128)S(1)}, u32[]{:S(2)}, u32[]{:S(2)}) async-start(f32[128,1,256]{2,1,0:T(1,128)} %broadcast_in_dim.12), calls=%async_computation.4 | async-start | bytes 262144 | tf_op jit(solution)/shard_map/all_to_all | solution.py:430
  308.5 16.4 %update_z.1 = bf16[5,16,64,512]{3,2,1,0:T(8,128)(2,1)} custom-call(f32[5,16,64,512]{3,2,1,0:T(8,128)} %update_xy.1.before_ref, bf16[5,16,64,512]{3,2,1,0:T(8,128)(2,1)} %state_ref.3, bf16[3,16,64,512]{3,2,1,0:T(8,128)(2,1)S(1)} %copy-done.6, bf16[16,5,16,16,128]{4,3,2,1,0:T(8,128)(2,1)} %all-to-all-done.3.z_ref, f32[1,256]{1,0:T(1,128)S(1)} %slice.7.after_ref), custom_call_target="tpu_custom_call" | custom-call | flops 5242880000 | bytes 27262976 | tf_op jit(solution)/shard_map/update_z/pallas_call | solution.py:200
  324.9 0.2 reduce_sum.18
  325.0 0.6 multiply_reduce_fusion
  326.3 0.6 broadcast_divide_fusion
  (32 shorter events, 0.3 us)
Async XLA Ops:
  74.8 9.7 %copy-start.10 = (bf16[512,512]{1,0:T(8,128)(2,1)S(1)}, bf16[512,512]{1,0:T(8,128)(2,1)}, u32[]{:S(2)}) copy-start(bf16[512,512]{1,0:T(8,128)(2,1)} %param.13) | copy-start | bytes 1572868
  74.8 72.0 %all-to-all-start.1 = ((bf16[16,5,16,16,128]{4,3,2,1,0:T(8,128)(2,1)}), bf16[16,5,16,16,128]{4,3,2,1,0:T(8,128)(2,1)}, u32[]{:S(2)}, u32[]{:S(2)}) async-start(bf16[16,5,16,16,128]{4,3,2,1,0:T(8,128)(2,1)} %get-tuple-element.20), calls=%async_computation.1 | async-start | bytes 10485760 | tf_op jit(solution)/shard_map/all_to_all | solution.py:403
  93.0 2.4 copy-start.2
  95.3 56.2 %copy-start.11 = (bf16[256,256]{1,0:T(8,128)(2,1)S(1)}, bf16[256,256]{1,0:T(8,128)(2,1)}, u32[]{:S(2)}) copy-start(bf16[256,256]{1,0:T(8,128)(2,1)} %param.14) | copy-start | bytes 393220
  146.8 77.6 %all-to-all-start.2 = ((bf16[8,5,2,64,512]{4,3,2,1,0:T(8,128)(2,1)}), bf16[8,5,2,64,512]{4,3,2,1,0:T(8,128)(2,1)}, u32[]{:S(2)}, u32[]{:S(2)}) async-start(bf16[8,5,2,64,512]{4,3,2,1,0:T(8,128)(2,1)} %copy-done.2), calls=%async_computation.2 | async-start | bytes 10485760 | tf_op jit(solution)/shard_map/all_to_all | solution.py:405
  160.5 2.4 copy-start.1
  162.9 67.6 %copy-start.7 = (bf16[512,512]{1,0:T(8,128)(2,1)S(1)}, bf16[512,512]{1,0:T(8,128)(2,1)}, u32[]{:S(2)}) copy-start(bf16[512,512]{1,0:T(8,128)(2,1)} %op_ref.1) | copy-start | bytes 1572868
  162.9 67.8 %copy-start.12 = (bf16[4,3,128]{2,0,1:T(4,128)(2,1)S(1)}, bf16[4,3,128]{2,0,1:T(4,128)(2,1)}, u32[]{:S(2)}) copy-start(bf16[4,3,128]{2,0,1:T(4,128)(2,1)} %param.16) | copy-start | bytes 9220
  162.9 67.8 %copy-start.13 = (s32[4,128]{1,0:T(4,128)S(1)}, s32[4,128]{1,0:T(4,128)}, u32[]{:S(2)}) copy-start(s32[4,128]{1,0:T(4,128)} %param.15) | copy-start | bytes 6148
  224.4 26.5 %slice-start = ((s8[5242880]{0:T(1024)(128)(4,1)}), s8[1048576]{0:T(1024)(128)(4,1)S(1)}, s32[]{:S(2)}) async-start(s8[5242880]{0:T(1024)(128)(4,1)} %bitcast.10), calls=%async_computation.5 | async-start | bytes 2097152
  224.4 68.5 %all-to-all-start.3 = ((bf16[16,5,16,16,128]{4,3,2,1,0:T(8,128)(2,1)}), bf16[16,5,16,16,128]{4,3,2,1,0:T(8,128)(2,1)}, u32[]{:S(2)}, u32[]{:S(2)}) async-start(bf16[16,5,16,16,128]{4,3,2,1,0:T(8,128)(2,1)} %copy-done.1), calls=%async_computation.3 | async-start | bytes 10485760 | tf_op jit(solution)/shard_map/all_to_all | solution.py:417
  230.9 20.0 %slice-start.1 = ((s8[5242880]{0:T(1024)(128)(4,1)}), s8[4194304]{0:T(1024)(128)(4,1)S(1)}, s32[]{:S(2)}) async-start(s8[5242880]{0:T(1024)(128)(4,1)} %bitcast.10), calls=%async_computation.6 | async-start | bytes 8388608
  234.9 2.0 copy-start.3
  236.9 1.9 copy-start.5
  242.1 2.5 copy-start
  256.3 7.2 %copy-start.6 = (bf16[3,16,64,512]{3,2,1,0:T(8,128)(2,1)S(1)}, bf16[3,16,64,512]{3,2,1,0:T(8,128)(2,1)}, u32[]{:S(2)}) copy-start(bf16[3,16,64,512]{3,2,1,0:T(8,128)(2,1)} %metric_ref.3) | copy-start | bytes 9437188
  256.3 7.2 %copy-start.8 = (bf16[512,512]{1,0:T(8,128)(2,1)S(1)}, bf16[512,512]{1,0:T(8,128)(2,1)}, u32[]{:S(2)}) copy-start(bf16[512,512]{1,0:T(8,128)(2,1)} %op_ref.1) | copy-start | bytes 1572868
  292.9 2.2 copy-start.4
  295.1 0.9 copy-start.9
  303.5 21.4 %all-to-all-start.4 = ((f32[128,1,256]{2,1,0:T(1,128)}), f32[128,1,256]{2,1,0:T(1,128)S(1)}, u32[]{:S(2)}, u32[]{:S(2)}) async-start(f32[128,1,256]{2,1,0:T(1,128)} %broadcast_in_dim.12), calls=%async_computation.4 | async-start | bytes 262144 | tf_op jit(solution)/shard_map/all_to_all | solution.py:430

commit v3 on v2

--- a/solution.py
+++ b/solution.py
@@ -9,12 +9,13 @@
 section_step = 0.5
 FIELDS, CZ, CY, NX, NZ = 5, 16, 64, 512, 256
 CELLS = 512
+PLANES = 4
 BF, F32 = jnp.bfloat16, jnp.float32
-VMEM_LIMIT = 48 * 1024 * 1024
-
-
-def params():
-    return pltpu.CompilerParams(vmem_limit_bytes=VMEM_LIMIT)
+MIB = 1024 * 1024
+
+
+def params(mib=60):
+    return pltpu.CompilerParams(vmem_limit_bytes=mib * MIB)
 
 
 def cost(flops, nbytes):
@@ -63,39 +64,41 @@
             jax.ShapeDtypeStruct((8, FIELDS, 2, CY, NX), BF),
             jax.ShapeDtypeStruct((16, FIELDS, CZ, 16, 128), BF),
         ],
-        compiler_params=params(),
+        compiler_params=params(8),
         cost_estimate=cost(adjoint.size, 6 * adjoint.size),
         name="pieces",
     )(adjoint)
 
 
-def line_z_kernel(in_ref, op_ref, *rest):
-    outs, (wide, prod) = rest[:-2], rest[-2:]
-    wide[...] = in_ref[...].reshape(NZ * 16, 128).astype(F32)
-    for row in range(0, 16, 2):
-        pair = [wide[pl.ds(row + i, NZ, stride=16), :].astype(BF) for i in range(2)]
-        out = jnp.dot(op_ref[...], jnp.concatenate(pair, axis=1), preferred_element_type=F32)
-        for i in range(2):
-            prod[pl.ds(row + i, NZ, stride=16), :] = out[:, 128 * i : 128 * (i + 1)]
-    whole = prod[...].astype(BF).reshape(16, CZ, 16, 128)
-    depth = CZ // len(outs)
-    for i, out_ref in enumerate(outs):
-        out_ref[...] = whole[:, i * depth : (i + 1) * depth].reshape(out_ref.shape)
-
-
-def line_z(lines, deriv_t, parts):
-    f = lines.shape[1]
-    depth = CZ // parts
+def line_z_kernel(in_ref, op_ref, out_ref, held, made, in_sem, out_sem):
+    fetch, send = [], []
+    for f in range(FIELDS):
+        fetch.append(pltpu.make_async_copy(in_ref.at[:, f], held.at[f], in_sem.at[f]))
+        send.append(pltpu.make_async_copy(made.at[f], out_ref.at[:, f], out_sem.at[f]))
+        fetch[f].start()
+    for f in range(FIELDS):
+        fetch[f].wait()
+        line = held[f].reshape(NZ, 16 * 128)
+        out = jnp.dot(op_ref[...], line, preferred_element_type=F32).astype(BF)
+        made[f] = out.reshape(16, CZ, 16, 128)
+        send[f].start()
+    for copy in send:
+        copy.wait()
+
+
+def line_z(lines, deriv_t):
+    tile = pltpu.VMEM((FIELDS, 16, CZ, 16, 128), BF)
     return pl.pallas_call(
         line_z_kernel,
-        grid=(f,),
-        in_specs=[
-            pl.BlockSpec((16, 1, CZ, 16, 128), lambda i: (0, i, 0, 0, 0)),
-            pl.BlockSpec((NZ, NZ), lambda i: (0, 0)),
-        ],
-        out_specs=[pl.BlockSpec((16, 1, depth, 16, 128), lambda i: (0, i, 0, 0, 0))] * parts,
-        out_shape=[jax.ShapeDtypeStruct((16, f, depth, 16, 128), BF)] * parts,
-        scratch_shapes=[pltpu.VMEM((NZ * 16, 128), F32), pltpu.VMEM((NZ * 16, 128), F32)],
+        in_specs=[pl.BlockSpec(memory_space=pl.ANY), pl.BlockSpec(memory_space=pltpu.VMEM)],
+        out_specs=pl.BlockSpec(memory_space=pl.ANY),
+        out_shape=jax.ShapeDtypeStruct(lines.shape, BF),
+        scratch_shapes=[
+            tile,
+            tile,
+            pltpu.SemaphoreType.DMA((FIELDS,)),
+            pltpu.SemaphoreType.DMA((FIELDS,)),
+        ],
         compiler_params=params(),
         cost_estimate=cost(2 * lines.size * NZ, 4 * lines.size),
         name="line_z",
@@ -132,49 +135,51 @@
 
 
 def chunks(body):
-    def step(a, carry):
+    def step(n, carry):
+        z, a = n // 4, n % 4
         rows = pl.ds(pl.multiple_of(a * 16, 16), 16)
         for b in range(4):
-            body(a * 4 + b, rows, slice(128 * b, 128 * b + 128))
+            body(z, a * 4 + b, rows, slice(128 * b, 128 * b + 128))
         return carry
 
-    lax.fori_loop(0, 4, step, 0)
+    lax.fori_loop(0, PLANES * 4, step, 0)
 
 
 def update_xy_kernel(adj_ref, state_ref, metric_ref, op_ref, y_ref, out_ref, along_x):
-    along_x[...] = jnp.dot(
-        adj_ref[...].reshape(FIELDS * CY, NX), op_ref[...], preferred_element_type=F32
-    ).reshape(FIELDS, CY, NX)
-
-    def body(piece, rows, cols):
-        load = lambda ref, n: [ref[f, 0, rows, cols].astype(F32) for f in range(n)]
+    for f in range(FIELDS):
+        along_x[f] = jnp.dot(
+            adj_ref[f].reshape(PLANES * CY, NX), op_ref[...], preferred_element_type=F32
+        ).reshape(PLANES, CY, NX)
+
+    def body(z, piece, rows, cols):
+        load = lambda ref, n: [ref[f, z, rows, cols].astype(F32) for f in range(n)]
         alongs = [
-            [along_x[f, rows, cols] for f in range(5)],
-            [y_ref[0, f, 0, rows, cols].astype(F32) for f in range(5)],
+            [along_x[f, z, rows, cols] for f in range(5)],
+            [y_ref[z // 2, f, z % 2, rows, cols].astype(F32) for f in range(5)],
         ]
         new = update(load(adj_ref, 5), load(state_ref, 5), load(metric_ref, 2), alongs, (0, 1))
         for f in range(5):
-            out_ref[f, 0, rows, cols] = new[f]
+            out_ref[f, z, rows, cols] = new[f]
 
     chunks(body)
 
 
 def update_xy(adjoint, state, metric, deriv_x, along_y):
-    plane = lambda n: pl.BlockSpec((n, 1, CY, NX), lambda i: (0, i, 0, 0))
+    plane = lambda n: pl.BlockSpec((n, PLANES, CY, NX), lambda i: (0, i, 0, 0))
     cells = CZ * CY * NX
     return pl.pallas_call(
         update_xy_kernel,
-        grid=(CZ,),
+        grid=(CZ // PLANES,),
         in_specs=[
             plane(5),
             plane(5),
             plane(2),
             pl.BlockSpec((NX, NX), lambda i: (0, 0)),
-            pl.BlockSpec((1, 5, 1, CY, NX), lambda i: (i // 2, 0, i % 2, 0, 0)),
+            pl.BlockSpec((PLANES // 2, 5, 2, CY, NX), lambda i: (i, 0, 0, 0, 0)),
         ],
         out_specs=plane(5),
         out_shape=jax.ShapeDtypeStruct(adjoint.shape, F32),
-        scratch_shapes=[pltpu.VMEM((FIELDS, CY, NX), F32)],
+        scratch_shapes=[pltpu.VMEM((FIELDS, PLANES, CY, NX), F32)],
         compiler_params=params(),
         cost_estimate=cost(cells * 2 * 5 * NX + cells * 10000, cells * 54),
         name="update_xy",
@@ -182,29 +187,29 @@
 
 
 def update_z_kernel(before_ref, state_ref, metric_ref, z_ref, after_ref, out_ref):
-    def body(piece, rows, cols):
-        before = [before_ref[f, 0, rows, cols] for f in range(5)]
-        state = [state_ref[f, 0, rows, cols].astype(F32) for f in range(5)]
-        metric = {2: metric_ref[0, 0, rows, cols].astype(F32)}
-        along = {2: [z_ref[piece, f, 0].astype(F32) for f in range(5)]}
+    def body(z, piece, rows, cols):
+        before = [before_ref[f, z, rows, cols] for f in range(5)]
+        state = [state_ref[f, z, rows, cols].astype(F32) for f in range(5)]
+        metric = {2: metric_ref[0, z, rows, cols].astype(F32)}
+        along = {2: [z_ref[piece, f, z].astype(F32) for f in range(5)]}
         new = update(before, state, metric, along, (2,))
         for f in range(5):
-            out_ref[f, 0, rows, cols] = new[f].astype(BF)
+            out_ref[f, z, rows, cols] = new[f].astype(BF)
 
     chunks(body)
 
 
 def update_z(before, state, metric, along_z, after):
-    plane = lambda n: pl.BlockSpec((n, 1, CY, NX), lambda i: (0, i, 0, 0))
+    plane = lambda n: pl.BlockSpec((n, PLANES, CY, NX), lambda i: (0, i, 0, 0))
     cells = CZ * CY * NX
     return pl.pallas_call(
         update_z_kernel,
-        grid=(CZ,),
+        grid=(CZ // PLANES,),
         in_specs=[
             plane(5),
             plane(5),
-            pl.BlockSpec((1, 1, CY, NX), lambda i: (2, i, 0, 0)),
-            pl.BlockSpec((16, 5, 1, 16, 128), lambda i: (0, 0, i, 0, 0)),
+            pl.BlockSpec((1, PLANES, CY, NX), lambda i: (2, i, 0, 0)),
+            pl.BlockSpec((16, 5, PLANES, 16, 128), lambda i: (0, 0, i, 0, 0)),
             pl.BlockSpec(memory_space=pl.ANY),
         ],
         out_specs=plane(5),
@@ -313,85 +318,64 @@
     )(cells, adjoint, deriv_t)
 
 
-def rows_z_kernel(cell_ref, out_ref):
+def surface_kernel(
+    cell_ref, z_ref, adj_ref, x_ref, y_ref, state_ref, metric_ref, normal_ref, basis_ref,
+    out_ref, pieces_z, sem,
+):
+    fetch = []
+    for n in range(4):
+        part = pl.ds(4 * n, 4)
+        fetch.append(pltpu.make_async_copy(z_ref.at[part], pieces_z.at[part], sem.at[n]))
+        fetch[n].start()
     cell = cell_ref[:, 0:1]
     x, y, z = cell % NX, cell // NX % CY, cell // (NX * CY)
-    row = ((y // 16 * 4 + x // 128) * CZ + z) * 16 + y % 16 - pl.program_id(0) * 1024
-    at = lax.broadcasted_iota(jnp.int32, (CELLS, 1024), 1)
-    out_ref[...] = jnp.where(at == row, 1.0, 0.0).astype(BF)
-
-
-def rows_z(cells):
-    return pl.pallas_call(
-        rows_z_kernel,
-        grid=(4,),
-        in_specs=[pl.BlockSpec((CELLS, 128), lambda i: (0, 0))],
-        out_specs=pl.BlockSpec((CELLS, 1024), lambda i: (0, i)),
-        out_shape=jax.ShapeDtypeStruct((CELLS, 4096), BF),
-        compiler_params=params(),
-        cost_estimate=cost(CELLS * 4096 * 10, CELLS * 4096 * 2),
-        name="rows_z",
-    )(cells)
-
-
-def surface_kernel(
-    cell_ref, onehot_ref, z_ref, adj_ref, x_ref, y_ref, state_ref, metric_ref, normal_ref,
-    basis_ref, out_ref, total,
-):
-    step = pl.program_id(0)
-
-    @pl.when(step == 0)
-    def _():
-        total[...] = jnp.zeros_like(total)
-
-    fields = [z_ref[:, f].reshape(1024, 128) for f in range(FIELDS)]
-    total[...] += jnp.dot(
-        onehot_ref[...], jnp.concatenate(fields, axis=1), preferred_element_type=F32
+    row = ((y // 16 * 4 + x // 128) * CZ + z) * 16 + y % 16
+    total = jnp.zeros((CELLS, FIELDS * 128), F32)
+    for n in range(4):
+        at = lax.broadcasted_iota(jnp.int32, (CELLS, 1024), 1) + 1024 * n
+        onehot = jnp.where(at == row, 1.0, 0.0).astype(BF)
+        fetch[n].wait()
+        fields = [pieces_z[4 * n : 4 * n + 4, f].reshape(1024, 128) for f in range(FIELDS)]
+        total += jnp.dot(
+            onehot, jnp.concatenate(fields, axis=1), preferred_element_type=F32
+        )
+    lane = lax.broadcasted_iota(jnp.int32, (CELLS, 128), 1)
+    here = lane == x % 128
+    held = jnp.zeros((CELLS, 128), F32)
+    for f in range(FIELDS):
+        value = jnp.where(here, total[:, 128 * f : 128 * (f + 1)], 0.0)
+        held = jnp.where(lane == f, jnp.sum(value, axis=1, keepdims=True), held)
+    lines = lambda ref, n: [ref[i : i + 1, :] for i in range(n)]
+    picked = held.T
+    along_z = [picked[i : i + 1, :] for i in range(5)]
+    state = lines(state_ref, 5)
+    new = update(
+        lines(adj_ref, 5), state, lines(metric_ref, 3),
+        [lines(x_ref, 5), lines(y_ref, 5), along_z],
     )
-
-    @pl.when(step == pl.num_programs(0) - 1)
-    def _():
-        lane = lax.broadcasted_iota(jnp.int32, (CELLS, 128), 1)
-        here = lane == cell_ref[:, 0:1] % 128
-        held = jnp.zeros((CELLS, 128), F32)
-        for f in range(FIELDS):
-            value = jnp.where(here, total[:, 128 * f : 128 * (f + 1)], 0.0)
-            held = jnp.where(lane == f, jnp.sum(value, axis=1, keepdims=True), held)
-        lines = lambda ref, n: [ref[i : i + 1, :] for i in range(n)]
-        picked = held.T
-        along_z = [picked[i : i + 1, :] for i in range(5)]
-        state = lines(state_ref, 5)
-        new = update(
-            lines(adj_ref, 5), state, lines(metric_ref, 3),
-            [lines(x_ref, 5), lines(y_ref, 5), along_z],
-        )
-        work = sum(state[1 + i] * (state[1 + i] / state[0]) for i in range(3))
-        press = gamma_less * (state[4] - 0.5 * work)
-        normal = lines(normal_ref, 3)
-        force = sum(normal[i] * new[1 + i].astype(BF).astype(F32) for i in range(3))
-        sens = jnp.broadcast_to((press * force).astype(BF), (16, CELLS))
-        out_ref[...] = jnp.dot(sens, basis_ref[...], preferred_element_type=F32)[0:8]
-
-
-def surface_terms(cells, onehot, along_z, adj, along_x, along_y, state, metric, normals, basis):
-    small = pl.BlockSpec((8, CELLS), lambda i: (0, 0))
+    work = sum(state[1 + i] * (state[1 + i] / state[0]) for i in range(3))
+    press = gamma_less * (state[4] - 0.5 * work)
+    normal = lines(normal_ref, 3)
+    force = sum(normal[i] * new[1 + i].astype(BF).astype(F32) for i in range(3))
+    sens = jnp.broadcast_to((press * force).astype(BF), (16, CELLS))
+    out_ref[...] = jnp.dot(sens, basis_ref[...], preferred_element_type=F32)[0:8]
+
+
+def surface_terms(cells, along_z, adj, along_x, along_y, state, metric, normals, basis):
+    vmem = pl.BlockSpec(memory_space=pltpu.VMEM)
     return pl.pallas_call(
         surface_kernel,
-        grid=(4,),
-        in_specs=[
-            pl.BlockSpec((CELLS, 128), lambda i: (0, 0)),
-            pl.BlockSpec((CELLS, 1024), lambda i: (0, i)),
-            pl.BlockSpec((4, FIELDS, CZ, 16, 128), lambda i: (i, 0, 0, 0, 0)),
-            small, small, small, small, small, small,
-            pl.BlockSpec((CELLS, 256), lambda i: (0, 0)),
-        ],
-        out_specs=pl.BlockSpec((8, 256), lambda i: (0, 0)),
+        in_specs=[vmem, pl.BlockSpec(memory_space=pl.ANY)] + [vmem] * 7,
+        out_specs=vmem,
         out_shape=jax.ShapeDtypeStruct((8, 256), F32),
-        scratch_shapes=[pltpu.VMEM((CELLS, FIELDS * 128), F32)],
+        scratch_shapes=[
+            pltpu.VMEM((16, FIELDS, CZ, 16, 128), BF),
+            pltpu.SemaphoreType.DMA((4,)),
+        ],
         compiler_params=params(),
         cost_estimate=cost(2 * 5 * CELLS * CZ * CY * NX, 5 * CZ * CY * NX * 2),
         name="surface_terms",
-    )(cells, onehot, along_z, adj, along_x, along_y, state, metric, normals, basis)
+    )(cells, along_z, adj, along_x, along_y, state, metric, normals, basis)
 
 
 def on_device(
@@ -399,12 +383,13 @@
 ):
     to_y, to_z = pieces(adjoint)
     lines_y = lax.all_to_all(to_y, "py", 0, 0)
-    surf_cells, to_z, lines_y = lax.optimization_barrier((surf_cells, to_z, lines_y))
+
+    operators = (deriv_x, deriv_y, deriv_z)
+    (deriv_x, deriv_y, deriv_z), surf_cells, surf_normal, to_z, lines_y = lax.optimization_barrier(
+        (operators, surf_cells, surf_normal, to_z, lines_y)
+    )
     lines_z = lax.all_to_all(to_z, "pz", 0, 0)
-    products_y, lines_z = lax.optimization_barrier((line_y(lines_y, deriv_y.T), lines_z))
-    back_y = lax.all_to_all(products_y, "py", 0, 0)
-    (products_z,) = line_z(lines_z, deriv_z.T, 1)
-
+    products_y = line_y(lines_y, deriv_y.T)
     cells = jnp.broadcast_to(surf_cells.reshape(CELLS, 1), (CELLS, 128))
     normals = jnp.transpose(surf_normal, (1, 0, 2)).reshape(3, CELLS).astype(F32)
     normals = jnp.pad(normals, ((0, 5), (0, 0)))
@@ -412,19 +397,23 @@
     picked_state = pick_cells(cells, state, plain, 5)
     picked_metric = pick_cells(cells, metric, plain, 3)
     picked_adj, picked_x = pick_x(cells, adjoint, deriv_x.T)
-
-    products_z, back_y = lax.optimization_barrier((products_z, back_y))
-    back_z = lax.all_to_all(products_z, "pz", 0, 0)
+    picked = (picked_adj, picked_x, picked_state, picked_metric)
+    products_y, lines_z, cells, normals, picked, deriv_zt = lax.optimization_barrier(
+        (products_y, lines_z, cells, normals, picked, deriv_z.T)
+    )
+    picked_adj, picked_x, picked_state, picked_metric = picked
+
+    back_y = lax.all_to_all(products_y, "py", 0, 0)
+    lines_z, back_y, cells, deriv_x = lax.optimization_barrier((lines_z, back_y, cells, deriv_x))
+    back_z = lax.all_to_all(line_z(lines_z, deriv_zt), "pz", 0, 0)
+
     lines = pl.BlockSpec((8, 1, 2, CY, NX), lambda f: (0, f, 0, 0, 0))
     picked_y = pick_cells(cells, back_y, lines, 5)
     before = update_xy(adjoint, state, metric, deriv_x, back_y)
-
-    back_z, before, onehot, picked_y = lax.optimization_barrier(
-        (back_z, before, rows_z(cells), picked_y)
-    )
+    back_z, before, picked_y = lax.optimization_barrier((back_z, before, picked_y))
     terms = surface_terms(
-        cells, onehot, back_z, picked_adj, picked_x, picked_y, picked_state,
-        picked_metric, normals, shape_basis,
+        cells, back_z, picked_adj, picked_x, picked_y, picked_state, picked_metric, normals,
+        shape_basis,
     )[0:1]
     result = update_z(before, state, metric, back_z, terms)
     all_terms = lax.all_to_all(jnp.broadcast_to(terms, (128, 1, 256)), ("py", "pz"), 0, 0)

time: 329 us -> 312 us (0.948)
  blocking collectives: 65.7 us -> 130 us
  waiting for transfers between devices: 122 us -> 65 us
  Pallas kernels: 95.2 us -> 84.7 us
  local copies, waits for them, and re-layouts: 15.7 us -> 7.56 us
  starting transfers between devices: 25.4 us -> 20.7 us
    all_to_all x0 -> x1, blocking collectives: none -> 64.5 us  [on_device(): back_y = lax.all_to_all(products_y, 'py', 0, 0)]
    all_to_all x2 -> x1, waiting for transfers between devices: 70.7 us -> 38.5 us  [on_device(): back_z = lax.all_to_all(line_z(lines_z, deriv_zt), 'pz', 0, 0)]
    all_to_all x1, waiting for transfers between devices: 51.5 us -> 26.5 us  [on_device(): lines_z = lax.all_to_all(to_z, 'pz', 0, 0)]
    pallas_call x5 -> x4, Pallas kernels: 56.3 us -> 43.3 us  [the longest x1 16.2 us: update_xy(): pl.pallas_call(update_xy_kernel, grid=(CZ // PLANES,), in_specs=[plane(5)...]
    unnamed x36 -> x17, local copies, waits for them, and re-layouts: 14.8 us -> 2.52 us
    pallas_call x1, Pallas kernels: 8.53 us -> 2.13 us  [pieces(): pl.pallas_call(pieces_kernel, grid=(FIELDS, CZ // depth), in_specs=[pl.Bl...]
    pallas_call x3, Pallas kernels: 15.8 us -> 20.7 us  [pick_cells(): pl.pallas_call(pick_kernel, grid=(count,), in_specs=[pl.BlockSpec((CELLS,...]
    all_to_all x2 -> x1, starting transfers between devices: 10.7 us -> 6.17 us  [on_device(): back_z = lax.all_to_all(line_z(lines_z, deriv_zt), 'pz', 0, 0)]
  transfers between devices with their start and end apart: 4 -> 3, of which waited for: 3 -> 2; matrix products, arithmetic and copies ran while one was open for 0% -> 1% of each run, Pallas kernels for 24% -> 22%
where the time goes in v3:
time: 312 us; the launch traced here: 311 us
  blocking collectives  130 us (42%)
  Pallas kernels  84.7 us (27%)
  waiting for transfers between devices  65 us (21%)
  starting transfers between devices  20.7 us (7%)
  local copies, waits for them, and re-layouts  7.56 us (2%)
    all_to_all x1, blocking collectives, on_device(): lines_y = lax.all_to_all(to_y, 'py', 0, 0)  65.7 us
    all_to_all x1, blocking collectives, on_device(): back_y = lax.all_to_all(products_y, 'py', 0, 0)  64.5 us
    all_to_all x1, waiting for transfers between devices, on_device(): back_z = lax.all_to_all(line_z(lines_z, deriv_zt), 'pz', 0, 0)  38.5 us
    all_to_all x1, waiting for transfers between devices, on_device(): lines_z = lax.all_to_all(to_z, 'pz', 0, 0)  26.5 us
    pallas_call x3, Pallas kernels, pick_cells(): pl.pallas_call(pick_kernel, grid=(count,), in_specs=[pl.BlockSpec((CELLS,...  20.7 us
    pallas_call x1, Pallas kernels, update_xy(): pl.pallas_call(update_xy_kernel, grid=(CZ // PLANES,), in_specs=[plane(5)...  16.2 us
    pallas_call x1, Pallas kernels, update_z(): pl.pallas_call(update_z_kernel, grid=(CZ // PLANES,), in_specs=[plane(5),...  12.4 us
    pallas_call x1, Pallas kernels, line_y(): pl.pallas_call(line_y_kernel, grid=(f, z), in_specs=[spec, pl.BlockSpec((...  9.89 us
  transfers between devices with their start and end apart: 3, of which 2 were waited for; matrix products, arithmetic and copies ran while one was open for 1% of the time, Pallas kernels for 22%

profile of v3, /device:TPU:1, one launch (start us, length us, event | category | flops | bytes accessed | tf_op | source)
XLA Modules:
  0.0 311.4 jit_solution(15537602165757952433)
XLA Ops:
  0.6 0.0 copy-start
  0.6 2.5 copy-done
  3.1 2.1 pieces.1
  5.3 65.7 %all_to_all.25.in_ref = bf16[8,5,2,64,512]{4,3,2,1,0:T(8,128)(2,1)} all-to-all(bf16[8,5,2,64,512]{4,3,2,1,0:T(8,128)(2,1)S(1)} %get-tuple-element.30), channel_id=1, replica_groups=mesh['py'=8,'pz'=16] {'py'}, dimensions={0} | all-to-all | bytes 10485760 | tf_op jit(solution)/shard_map/all_to_all | solution.py:385
  71.0 0.0 copy-start.2
  71.0 0.0 copy-start.7
  71.0 9.7 %all-to-all-start.1 = ((bf16[16,5,16,16,128]{4,3,2,1,0:T(8,128)(2,1)}), bf16[16,5,16,16,128]{4,3,2,1,0:T(8,128)(2,1)}, u32[]{:S(2)}, u32[]{:S(2)}) async-start(bf16[16,5,16,16,128]{4,3,2,1,0:T(8,128)(2,1)} %copy-done.1), calls=%async_computation.1 | async-start | bytes 10485760 | tf_op jit(solution)/shard_map/all_to_all | solution.py:391
  80.7 0.8 copy.19
  81.4 1.0 copy.17
  82.5 1.0 copy.18
  83.5 0.6 pad_convert_fusion.normal_ref
  84.1 0.8 broadcast_in_dim.11.cell_ref
  84.9 5.4 %pick_cells.4.metric_ref = f32[8,512]{1,0:T(8,128)} custom-call(s32[512,128]{1,0:T(8,128)} %broadcast_in_dim.11.cell_ref, bf16[3,16,64,512]{3,2,1,0:T(8,128)(2,1)} %metric_ref.3), custom_call_target="tpu_custom_call" | custom-call | flops 1610612736 | bytes 3145728 | tf_op jit(solution)/shard_map/pick_cells/pallas_call | solution.py:261
  90.3 7.7 %pick_cells.3.state_ref = f32[8,512]{1,0:T(8,128)} custom-call(s32[512,128]{1,0:T(8,128)} %broadcast_in_dim.11.cell_ref, bf16[5,16,64,512]{3,2,1,0:T(8,128)(2,1)} %state_ref.3), custom_call_target="tpu_custom_call" | custom-call | flops 2684354560 | bytes 5242880 | tf_op jit(solution)/shard_map/pick_cells/pallas_call | solution.py:261
  98.0 8.6 %pick_x.1 = (f32[8,512]{1,0:T(8,128)}, f32[8,512]{1,0:T(8,128)}) custom-call(s32[512,128]{1,0:T(8,128)} %broadcast_in_dim.11.cell_ref, bf16[5,16,64,512]{3,2,1,0:T(8,128)(2,1)} %adj_ref.1, bf16[512,512]{1,0:T(8,128)(2,1)} %bitcast.11), custom_call_target="tpu_custom_call" | custom-call | flops 2684354560 | bytes 5242880 | tf_op jit(solution)/shard_map/pick_x/pallas_call | solution.py:299
  106.6 9.9 %line_y.1 = bf16[8,5,2,64,512]{4,3,2,1,0:T(8,128)(2,1)} custom-call(bf16[8,5,2,64,512]{4,3,2,1,0:T(8,128)(2,1)} %all_to_all.25.in_ref, bf16[512,512]{1,0:T(8,128)(2,1)} %bitcast.10), custom_call_target="tpu_custom_call" | custom-call | flops 2684354560 | bytes 10485760 | tf_op jit(solution)/shard_map/line_y/pallas_call | solution.py:34
  116.5 26.5 %all-to-all-done.1.in_ref = bf16[16,5,16,16,128]{4,3,2,1,0:T(8,128)(2,1)} async-done(((bf16[16,5,16,16,128]{4,3,2,1,0:T(8,128)(2,1)}), bf16[16,5,16,16,128]{4,3,2,1,0:T(8,128)(2,1)}, u32[]{:S(2)}, u32[]{:S(2)}) %all-to-all-start.1) | async-done | bytes 5242912 | tf_op jit(solution)/shard_map/all_to_all | solution.py:391
  143.0 64.5 %all_to_all.26.y_ref.field_ref = bf16[8,5,2,64,512]{4,3,2,1,0:T(8,128)(2,1)} all-to-all(bf16[8,5,2,64,512]{4,3,2,1,0:T(8,128)(2,1)} %line_y.1), channel_id=1, replica_groups=mesh['py'=8,'pz'=16] {'py'}, dimensions={0} | all-to-all | bytes 10485760 | tf_op jit(solution)/shard_map/all_to_all | solution.py:406
  207.5 6.5 %line_z.1 = bf16[16,5,16,16,128]{4,3,2,1,0:T(8,128)(2,1)} custom-call(bf16[16,5,16,16,128]{4,3,2,1,0:T(8,128)(2,1)} %all-to-all-done.1.in_ref, bf16[256,256]{1,0:T(8,128)(2,1)} %bitcast.12), custom_call_target="tpu_custom_call" | custom-call | flops 1342177280 | bytes 10485760 | tf_op jit(solution)/shard_map/line_z/pallas_call | solution.py:91
  213.9 6.2 %all-to-all-start.3 = ((bf16[16,5,16,16,128]{4,3,2,1,0:T(8,128)(2,1)}), bf16[16,5,16,16,128]{4,3,2,1,0:T(8,128)(2,1)}, u32[]{:S(2)}, u32[]{:S(2)}) async-start(bf16[16,5,16,16,128]{4,3,2,1,0:T(8,128)(2,1)} %line_z.1), calls=%async_computation.3 | async-start | bytes 10485760 | tf_op jit(solution)/shard_map/all_to_all | solution.py:408
  220.1 7.7 %pick_cells.5.y_ref = f32[8,512]{1,0:T(8,128)} custom-call(s32[512,128]{1,0:T(8,128)} %broadcast_in_dim.11.cell_ref, bf16[8,5,2,64,512]{4,3,2,1,0:T(8,128)(2,1)} %all_to_all.26.y_ref.field_ref), custom_call_target="tpu_custom_call" | custom-call | flops 2684354560 | bytes 5242880 | tf_op jit(solution)/shard_map/pick_cells/pallas_call | solution.py:261
  227.8 16.2 %update_xy.1.before_ref = f32[5,16,64,512]{3,2,1,0:T(8,128)} custom-call(bf16[5,16,64,512]{3,2,1,0:T(8,128)(2,1)} %adj_ref.1, bf16[5,16,64,512]{3,2,1,0:T(8,128)(2,1)} %state_ref.3, bf16[3,16,64,512]{3,2,1,0:T(8,128)(2,1)} %metric_ref.3, bf16[512,512]{1,0:T(8,128)(2,1)} %op_ref, bf16[8,5,2,64,512]{4,3,2,1,0:T(8,128)(2,1)} %all_to_all.26.y_ref.field_ref), custom_call_target="tpu_custom_call" | custom-call | flops 7927234560 | bytes 28311552 | tf_op jit(solution)/shard_map/update_xy/pallas_call | solution.py:170
  244.0 38.5 %all-to-all-done.3.z_ref = bf16[16,5,16,16,128]{4,3,2,1,0:T(8,128)(2,1)} async-done(((bf16[16,5,16,16,128]{4,3,2,1,0:T(8,128)(2,1)}), bf16[16,5,16,16,128]{4,3,2,1,0:T(8,128)(2,1)}, u32[]{:S(2)}, u32[]{:S(2)}) %all-to-all-start.3) | async-done | bytes 5242912 | tf_op jit(solution)/shard_map/all_to_all | solution.py:408
  282.5 8.2 %surface_terms.1 = f32[8,256]{1,0:T(8,128)} custom-call(s32[512,128]{1,0:T(8,128)} %broadcast_in_dim.11.cell_ref, bf16[16,5,16,16,128]{4,3,2,1,0:T(8,128)(2,1)} %all-to-all-done.3.z_ref, f32[8,512]{1,0:T(8,128)} %get-tuple-element.50.adj_ref, f32[8,512]{1,0:T(8,128)} %get-tuple-element.51.x_ref, f32[8,512]{1,0:T(8,128)} %pick_cells.5.y_ref, ...), custom_call_target="tpu_custom_call" | custom-call | flops 2684354560 | bytes 5242880 | tf_op jit(solution)/shard_map/surface_terms/pallas_call | solution.py:366
  290.7 0.7 slice.7.after_ref
  291.4 0.7 broadcast_in_dim.12
  292.1 4.8 %all-to-all-start.4 = ((f32[128,1,256]{2,1,0:T(1,128)}), f32[128,1,256]{2,1,0:T(1,128)S(1)}, u32[]{:S(2)}, u32[]{:S(2)}) async-start(f32[128,1,256]{2,1,0:T(1,128)} %broadcast_in_dim.12), calls=%async_computation.4 | async-start | bytes 262144 | tf_op jit(solution)/shard_map/all_to_all | solution.py:419
  297.0 12.4 %update_z.1 = bf16[5,16,64,512]{3,2,1,0:T(8,128)(2,1)} custom-call(f32[5,16,64,512]{3,2,1,0:T(8,128)} %update_xy.1.before_ref, bf16[5,16,64,512]{3,2,1,0:T(8,128)(2,1)} %state_ref.3, bf16[3,16,64,512]{3,2,1,0:T(8,128)(2,1)} %metric_ref.3, bf16[16,5,16,16,128]{4,3,2,1,0:T(8,128)(2,1)} %all-to-all-done.3.z_ref, f32[1,256]{1,0:T(1,128)} %copy-done.5), custom_call_target="tpu_custom_call" | custom-call | flops 5242880000 | bytes 27262976 | tf_op jit(solution)/shard_map/update_z/pallas_call | solution.py:205
  309.4 0.0 all-to-all-done.4
  309.4 0.2 reduce_sum.18
  309.5 0.6 multiply_reduce_fusion
  310.8 0.6 broadcast_divide_fusion
  (13 shorter events, 0.0 us)
Async XLA Ops:
  0.6 2.5 copy-start
  5.3 65.7 %copy-start.1 = (bf16[16,5,16,16,128]{4,3,2,1,0:T(8,128)(2,1)}, bf16[16,5,16,16,128]{4,3,2,1,0:T(8,128)(2,1)S(1)}, u32[]{:S(2)}) copy-start(bf16[16,5,16,16,128]{4,3,2,1,0:T(8,128)(2,1)S(1)} %get-tuple-element.33) | copy-start | bytes 15728644
  70.9 9.7 %copy-start.6 = (bf16[4,3,128]{2,0,1:T(4,128)(2,1)S(1)}, bf16[4,3,128]{2,0,1:T(4,128)(2,1)}, u32[]{:S(2)}) copy-start(bf16[4,3,128]{2,0,1:T(4,128)(2,1)} %param.16) | copy-start | bytes 9220
  70.9 9.7 %copy-start.4 = (bf16[256,256]{1,0:T(8,128)(2,1)S(1)}, bf16[256,256]{1,0:T(8,128)(2,1)}, u32[]{:S(2)}) copy-start(bf16[256,256]{1,0:T(8,128)(2,1)} %param.14) | copy-start | bytes 393220
  71.0 10.5 %copy-start.3 = (bf16[512,512]{1,0:T(8,128)(2,1)S(1)}, bf16[512,512]{1,0:T(8,128)(2,1)}, u32[]{:S(2)}) copy-start(bf16[512,512]{1,0:T(8,128)(2,1)} %param.13) | copy-start | bytes 1572868
  71.0 11.5 %copy-start.2 = (bf16[512,512]{1,0:T(8,128)(2,1)S(1)}, bf16[512,512]{1,0:T(8,128)(2,1)}, u32[]{:S(2)}) copy-start(bf16[512,512]{1,0:T(8,128)(2,1)} %op_ref) | copy-start | bytes 1572868
  71.0 13.1 %copy-start.7 = (s32[4,128]{1,0:T(4,128)S(1)}, s32[4,128]{1,0:T(4,128)}, u32[]{:S(2)}) copy-start(s32[4,128]{1,0:T(4,128)} %param.15) | copy-start | bytes 6148
  71.0 72.0 %all-to-all-start.1 = ((bf16[16,5,16,16,128]{4,3,2,1,0:T(8,128)(2,1)}), bf16[16,5,16,16,128]{4,3,2,1,0:T(8,128)(2,1)}, u32[]{:S(2)}, u32[]{:S(2)}) async-start(bf16[16,5,16,16,128]{4,3,2,1,0:T(8,128)(2,1)} %copy-done.1), calls=%async_computation.1 | async-start | bytes 10485760 | tf_op jit(solution)/shard_map/all_to_all | solution.py:391
  213.9 68.6 %all-to-all-start.3 = ((bf16[16,5,16,16,128]{4,3,2,1,0:T(8,128)(2,1)}), bf16[16,5,16,16,128]{4,3,2,1,0:T(8,128)(2,1)}, u32[]{:S(2)}, u32[]{:S(2)}) async-start(bf16[16,5,16,16,128]{4,3,2,1,0:T(8,128)(2,1)} %line_z.1), calls=%async_computation.3 | async-start | bytes 10485760 | tf_op jit(solution)/shard_map/all_to_all | solution.py:408
  291.4 5.5 %copy-start.5 = (f32[1,256]{1,0:T(1,128)}, f32[1,256]{1,0:T(1,128)S(1)}, u32[]{:S(2)}) copy-start(f32[1,256]{1,0:T(1,128)S(1)} %slice.7.after_ref) | copy-start | bytes 3076
  292.1 17.2 %all-to-all-start.4 = ((f32[128,1,256]{2,1,0:T(1,128)}), f32[128,1,256]{2,1,0:T(1,128)S(1)}, u32[]{:S(2)}, u32[]{:S(2)}) async-start(f32[128,1,256]{2,1,0:T(1,128)} %broadcast_in_dim.12), calls=%async_computation.4 | async-start | bytes 262144 | tf_op jit(solution)/shard_map/all_to_all | solution.py:419

commit v4 on v3

--- a/solution.py
+++ b/solution.py
@@ -14,8 +14,20 @@
 MIB = 1024 * 1024
 
 
-def params(mib=60):
+def params(mib=24):
     return pltpu.CompilerParams(vmem_limit_bytes=mib * MIB)
+
+
+def in_hbm(*arrays):
+    return [pltpu.with_memory_space_constraint(array, pltpu.HBM) for array in arrays]
+
+
+def in_vmem(array):
+    return pltpu.with_memory_space_constraint(array, pltpu.VMEM)
+
+
+def hbm_out(shape, dtype):
+    return pltpu.HBM(shape, dtype)
 
 
 def cost(flops, nbytes):
@@ -36,11 +48,11 @@
         grid=(f, z),
         in_specs=[spec, pl.BlockSpec((512, 512), lambda i, j: (0, 0))],
         out_specs=spec,
-        out_shape=jax.ShapeDtypeStruct(lines.shape, BF),
+        out_shape=hbm_out(lines.shape, BF),
         compiler_params=params(),
         cost_estimate=cost(2 * lines.size * 512, 4 * lines.size),
         name="line_y",
-    )(lines, deriv_t)
+    )(*in_hbm(lines), deriv_t)
 
 
 def pieces_kernel(in_ref, y_ref, z_ref):
@@ -92,7 +104,7 @@
         line_z_kernel,
         in_specs=[pl.BlockSpec(memory_space=pl.ANY), pl.BlockSpec(memory_space=pltpu.VMEM)],
         out_specs=pl.BlockSpec(memory_space=pl.ANY),
-        out_shape=jax.ShapeDtypeStruct(lines.shape, BF),
+        out_shape=hbm_out(lines.shape, BF),
         scratch_shapes=[
             tile,
             tile,
@@ -102,7 +114,7 @@
         compiler_params=params(),
         cost_estimate=cost(2 * lines.size * NZ, 4 * lines.size),
         name="line_z",
-    )(lines, deriv_t)
+    )(in_vmem(lines), deriv_t)
 
 
 def update(before, state, metric, alongs, directions=(0, 1, 2)):
@@ -178,12 +190,12 @@
             pl.BlockSpec((PLANES // 2, 5, 2, CY, NX), lambda i: (i, 0, 0, 0, 0)),
         ],
         out_specs=plane(5),
-        out_shape=jax.ShapeDtypeStruct(adjoint.shape, F32),
+        out_shape=hbm_out(adjoint.shape, F32),
         scratch_shapes=[pltpu.VMEM((FIELDS, PLANES, CY, NX), F32)],
         compiler_params=params(),
         cost_estimate=cost(cells * 2 * 5 * NX + cells * 10000, cells * 54),
         name="update_xy",
-    )(adjoint, state, metric, deriv_x, along_y)
+    )(*in_hbm(adjoint, state, metric, deriv_x, along_y))
 
 
 def update_z_kernel(before_ref, state_ref, metric_ref, z_ref, after_ref, out_ref):
@@ -217,7 +229,7 @@
         compiler_params=params(),
         cost_estimate=cost(cells * 10000, cells * 52),
         name="update_z",
-    )(before, state, metric, along_z, after)
+    )(*in_hbm(before, state, metric), in_vmem(along_z), after)
 
 
 def pick_rows(onehot_ref, row, f):
@@ -268,7 +280,7 @@
         compiler_params=params(),
         cost_estimate=cost(2 * count * CELLS * CZ * CY * NX, count * CZ * CY * NX * 2),
         name="pick_cells",
-    )(cells, fields)
+    )(cells, *in_hbm(fields))
 
 
 def pick_x_kernel(cell_ref, field_ref, op_ref, adj_out, along_out, onehot_ref, column, held, along):
@@ -315,30 +327,23 @@
         compiler_params=params(),
         cost_estimate=cost(2 * 5 * CELLS * CZ * CY * NX, 5 * CZ * CY * NX * 2),
         name="pick_x",
-    )(cells, adjoint, deriv_t)
+    )(cells, *in_hbm(adjoint), deriv_t)
 
 
 def surface_kernel(
     cell_ref, z_ref, adj_ref, x_ref, y_ref, state_ref, metric_ref, normal_ref, basis_ref,
-    out_ref, pieces_z, sem,
+    out_ref, onehot, total,
 ):
-    fetch = []
-    for n in range(4):
-        part = pl.ds(4 * n, 4)
-        fetch.append(pltpu.make_async_copy(z_ref.at[part], pieces_z.at[part], sem.at[n]))
-        fetch[n].start()
     cell = cell_ref[:, 0:1]
     x, y, z = cell % NX, cell // NX % CY, cell // (NX * CY)
     row = ((y // 16 * 4 + x // 128) * CZ + z) * 16 + y % 16
-    total = jnp.zeros((CELLS, FIELDS * 128), F32)
     for n in range(4):
         at = lax.broadcasted_iota(jnp.int32, (CELLS, 1024), 1) + 1024 * n
-        onehot = jnp.where(at == row, 1.0, 0.0).astype(BF)
-        fetch[n].wait()
-        fields = [pieces_z[4 * n : 4 * n + 4, f].reshape(1024, 128) for f in range(FIELDS)]
-        total += jnp.dot(
-            onehot, jnp.concatenate(fields, axis=1), preferred_element_type=F32
-        )
+        onehot[:, 1024 * n : 1024 * (n + 1)] = jnp.where(at == row, 1.0, 0.0).astype(BF)
+    fields = [z_ref[:, f].reshape(4096, 128) for f in range(FIELDS)]
+    total[...] = jnp.dot(
+        onehot[...], jnp.concatenate(fields, axis=1), preferred_element_type=F32
+    )
     lane = lax.broadcasted_iota(jnp.int32, (CELLS, 128), 1)
     here = lane == x % 128
     held = jnp.zeros((CELLS, 128), F32)
@@ -358,24 +363,40 @@
     normal = lines(normal_ref, 3)
     force = sum(normal[i] * new[1 + i].astype(BF).astype(F32) for i in range(3))
     sens = jnp.broadcast_to((press * force).astype(BF), (16, CELLS))
-    out_ref[...] = jnp.dot(sens, basis_ref[...], preferred_element_type=F32)[0:8]
+    terms = jnp.dot(sens, basis_ref[...], preferred_element_type=F32)[0:1]
+    out_ref[...] = jnp.broadcast_to(terms.reshape(1, 1, 256), out_ref.shape)
 
 
 def surface_terms(cells, along_z, adj, along_x, along_y, state, metric, normals, basis):
     vmem = pl.BlockSpec(memory_space=pltpu.VMEM)
     return pl.pallas_call(
         surface_kernel,
-        in_specs=[vmem, pl.BlockSpec(memory_space=pl.ANY)] + [vmem] * 7,
+        in_specs=[vmem] * 9,
         out_specs=vmem,
-        out_shape=jax.ShapeDtypeStruct((8, 256), F32),
+        out_shape=jax.ShapeDtypeStruct((128, 1, 256), F32),
         scratch_shapes=[
-            pltpu.VMEM((16, FIELDS, CZ, 16, 128), BF),
-            pltpu.SemaphoreType.DMA((4,)),
+            pltpu.VMEM((CELLS, 4096), BF),
+            pltpu.VMEM((CELLS, FIELDS * 128), F32),
         ],
         compiler_params=params(),
         cost_estimate=cost(2 * 5 * CELLS * CZ * CY * NX, 5 * CZ * CY * NX * 2),
         name="surface_terms",
-    )(cells, along_z, adj, along_x, along_y, state, metric, normals, basis)
+    )(cells, in_vmem(along_z), adj, along_x, along_y, state, metric, normals, basis)
+
+
+def normalized_kernel(terms_ref, out_ref):
+    summed = jnp.sum(terms_ref[...], axis=0)
+    mean = jnp.sum(summed * summed, axis=1, keepdims=True) * (1.0 / 256)
+    out_ref[...] = summed / jnp.sqrt(mean + 1e-06)
+
+
+def normalized(terms):
+    return pl.pallas_call(
+        normalized_kernel,
+        out_shape=jax.ShapeDtypeStruct((1, 256), F32),
+        cost_estimate=cost(4 * terms.size, 4 * terms.size),
+        name="normalized",
+    )(terms)
 
 
 def on_device(
@@ -414,12 +435,10 @@
     terms = surface_terms(
         cells, back_z, picked_adj, picked_x, picked_y, picked_state, picked_metric, normals,
         shape_basis,
-    )[0:1]
+    )
     result = update_z(before, state, metric, back_z, terms)
-    all_terms = lax.all_to_all(jnp.broadcast_to(terms, (128, 1, 256)), ("py", "pz"), 0, 0)
-    summed_grad = jnp.sum(all_terms, axis=(0, 1))
-    gradient_out = summed_grad / jnp.sqrt(jnp.mean(summed_grad * summed_grad) + 1e-06)
-    return (result, gradient_out)
+    all_terms = lax.all_to_all(terms, ("py", "pz"), 0, 0)
+    return (result, normalized(all_terms)[0])
 
 
 def solution(mesh):

time: 312 us -> 310 us (level)
  waiting for transfers between devices: 65 us -> 71.3 us
  local copies, waits for them, and re-layouts: 7.56 us -> 3.82 us
    all_to_all x1, waiting for transfers between devices: 26.5 us -> 32.3 us  [on_device(): lines_z = lax.all_to_all(to_z, 'pz', 0, 0)]
    pallas_call x1 -> x2, Pallas kernels: 8.18 us -> 9.47 us  [the longest x1 7.77 us: surface_terms(): pl.pallas_call(surface_kernel, in_specs=[vmem] * 9, out_specs=vmem, out_s...]
  transfers between devices with their start and end apart: 3 -> 3, of which waited for: 2 -> 2; matrix products, arithmetic and copies ran while one was open for 1% -> 0% of each run, Pallas kernels for 22% -> 21%
where the time goes in v4:
time: 310 us; the launch traced here: 309 us
  blocking collectives  130 us (42%)
  Pallas kernels  82.3 us (27%)
  waiting for transfers between devices  71.3 us (23%)
  starting transfers between devices  20.7 us (7%)
  local copies, waits for them, and re-layouts  3.82 us (1%)
    all_to_all x1, blocking collectives, on_device(): lines_y = lax.all_to_all(to_y, 'py', 0, 0)  65.7 us
    all_to_all x1, blocking collectives, on_device(): back_y = lax.all_to_all(products_y, 'py', 0, 0)  64.5 us
    all_to_all x1, waiting for transfers between devices, on_device(): back_z = lax.all_to_all(line_z(lines_z, deriv_zt), 'pz', 0, 0)  39 us
    all_to_all x1, waiting for transfers between devices, on_device(): lines_z = lax.all_to_all(to_z, 'pz', 0, 0)  32.3 us
    pallas_call x3, Pallas kernels, pick_cells(): pl.pallas_call(pick_kernel, grid=(count,), in_specs=[pl.BlockSpec((CELLS,...  18.8 us
    pallas_call x1, Pallas kernels, update_xy(): pl.pallas_call(update_xy_kernel, grid=(CZ // PLANES,), in_specs=[plane(5)...  16.4 us
    pallas_call x1, Pallas kernels, update_z(): pl.pallas_call(update_z_kernel, grid=(CZ // PLANES,), in_specs=[plane(5),...  12.4 us
    pallas_call x1, Pallas kernels, line_y(): pl.pallas_call(line_y_kernel, grid=(f, z), in_specs=[spec, pl.BlockSpec((...  9.74 us
  transfers between devices with their start and end apart: 3, of which 2 were waited for; matrix products, arithmetic and copies ran while one was open for 0% of the time, Pallas kernels for 21%

profile of v4, /device:TPU:1, one launch (start us, length us, event | category | flops | bytes accessed | tf_op | source)
XLA Modules:
  0.0 309.0 jit_solution(12986224126111285646)
XLA Ops:
  0.6 0.0 copy-start
  0.6 2.5 copy-done
  3.1 2.1 pieces.1
  5.3 0.0 copy-start.1
  5.3 65.7 %all_to_all.25.in_ref = bf16[8,5,2,64,512]{4,3,2,1,0:T(8,128)(2,1)} all-to-all(bf16[8,5,2,64,512]{4,3,2,1,0:T(8,128)(2,1)S(1)} %get-tuple-element.30), channel_id=1, replica_groups=mesh['py'=8,'pz'=16] {'py'}, dimensions={0} | all-to-all | bytes 10485760 | tf_op jit(solution)/shard_map/all_to_all | solution.py:406
  70.9 0.0 copy-done.1
  71.0 0.0 copy-start.3
  71.0 0.0 copy-start.8
  71.0 9.7 %all-to-all-start.1 = ((bf16[16,5,16,16,128]{4,3,2,1,0:T(8,128)(2,1)}), bf16[16,5,16,16,128]{4,3,2,1,0:T(8,128)(2,1)}, u32[]{:S(2)}, u32[]{:S(2)}) async-start(bf16[16,5,16,16,128]{4,3,2,1,0:T(8,128)(2,1)} %copy-done.1), calls=%async_computation.1 | async-start | bytes 10485760 | tf_op jit(solution)/shard_map/all_to_all | solution.py:412
  80.7 0.0 copy-done.7
  80.7 0.1 copy.13
  80.8 0.2 copy.11
  81.0 0.2 copy.12
  81.3 0.1 broadcast_in_dim.8.cell_ref
  81.4 4.8 %pick_cells.4.metric_ref = f32[8,512]{1,0:T(8,128)S(1)} custom-call(s32[512,128]{1,0:T(8,128)S(1)} %broadcast_in_dim.8.cell_ref, bf16[3,16,64,512]{3,2,1,0:T(8,128)(2,1)} %metric_ref.3), custom_call_target="tpu_custom_call" | custom-call | flops 1610612736 | bytes 3145728 | tf_op jit(solution)/shard_map/pick_cells/pallas_call | solution.py:273
  86.2 7.0 %pick_cells.3.state_ref = f32[8,512]{1,0:T(8,128)S(1)} custom-call(s32[512,128]{1,0:T(8,128)S(1)} %broadcast_in_dim.8.cell_ref, bf16[5,16,64,512]{3,2,1,0:T(8,128)(2,1)} %state_ref.3), custom_call_target="tpu_custom_call" | custom-call | flops 2684354560 | bytes 5242880 | tf_op jit(solution)/shard_map/pick_cells/pallas_call | solution.py:273
  93.2 7.8 %pick_x.1 = (f32[8,512]{1,0:T(8,128)S(1)}, f32[8,512]{1,0:T(8,128)S(1)}) custom-call(s32[512,128]{1,0:T(8,128)S(1)} %broadcast_in_dim.8.cell_ref, bf16[5,16,64,512]{3,2,1,0:T(8,128)(2,1)} %adj_ref.1, bf16[512,512]{1,0:T(8,128)(2,1)S(1)} %bitcast.11), custom_call_target="tpu_custom_call" | custom-call | flops 2684354560 | bytes 5242880 | tf_op jit(solution)/shard_map/pick_x/pallas_call | solution.py:311
  100.9 9.7 %line_y.1 = bf16[8,5,2,64,512]{4,3,2,1,0:T(8,128)(2,1)} custom-call(bf16[8,5,2,64,512]{4,3,2,1,0:T(8,128)(2,1)} %all_to_all.25.in_ref, bf16[512,512]{1,0:T(8,128)(2,1)S(1)} %bitcast.10), custom_call_target="tpu_custom_call" | custom-call | flops 2684354560 | bytes 10485760 | tf_op jit(solution)/shard_map/line_y/pallas_call | solution.py:46
  110.7 32.3 %all-to-all-done.1.in_ref = bf16[16,5,16,16,128]{4,3,2,1,0:T(8,128)(2,1)} async-done(((bf16[16,5,16,16,128]{4,3,2,1,0:T(8,128)(2,1)}), bf16[16,5,16,16,128]{4,3,2,1,0:T(8,128)(2,1)}, u32[]{:S(2)}, u32[]{:S(2)}) %all-to-all-start.1) | async-done | bytes 5242912 | tf_op jit(solution)/shard_map/all_to_all | solution.py:412
  143.0 64.5 %all_to_all.26.y_ref.field_ref = bf16[8,5,2,64,512]{4,3,2,1,0:T(8,128)(2,1)} all-to-all(bf16[8,5,2,64,512]{4,3,2,1,0:T(8,128)(2,1)} %line_y.1), channel_id=1, replica_groups=mesh['py'=8,'pz'=16] {'py'}, dimensions={0} | all-to-all | bytes 10485760 | tf_op jit(solution)/shard_map/all_to_all | solution.py:427
  207.5 5.6 %line_z.1 = bf16[16,5,16,16,128]{4,3,2,1,0:T(8,128)(2,1)} custom-call(bf16[16,5,16,16,128]{4,3,2,1,0:T(8,128)(2,1)} %all-to-all-done.1.in_ref, bf16[256,256]{1,0:T(8,128)(2,1)S(1)} %bitcast.12), custom_call_target="tpu_custom_call" | custom-call | flops 1342177280 | bytes 10485760 | tf_op jit(solution)/shard_map/line_z/pallas_call | solution.py:103
  213.1 6.2 %all-to-all-start.3 = ((bf16[16,5,16,16,128]{4,3,2,1,0:T(8,128)(2,1)}), bf16[16,5,16,16,128]{4,3,2,1,0:T(8,128)(2,1)}, u32[]{:S(2)}, u32[]{:S(2)}) async-start(bf16[16,5,16,16,128]{4,3,2,1,0:T(8,128)(2,1)} %line_z.1), calls=%async_computation.3 | async-start | bytes 10485760 | tf_op jit(solution)/shard_map/all_to_all | solution.py:429
  219.2 7.0 %pick_cells.5.y_ref = f32[8,512]{1,0:T(8,128)S(1)} custom-call(s32[512,128]{1,0:T(8,128)S(1)} %broadcast_in_dim.8.cell_ref, bf16[8,5,2,64,512]{4,3,2,1,0:T(8,128)(2,1)} %all_to_all.26.y_ref.field_ref), custom_call_target="tpu_custom_call" | custom-call | flops 2684354560 | bytes 5242880 | tf_op jit(solution)/shard_map/pick_cells/pallas_call | solution.py:273
  226.3 0.0 copy-start.2
  226.3 16.4 %update_xy.1.before_ref = f32[5,16,64,512]{3,2,1,0:T(8,128)} custom-call(bf16[5,16,64,512]{3,2,1,0:T(8,128)(2,1)} %adj_ref.1, bf16[5,16,64,512]{3,2,1,0:T(8,128)(2,1)} %state_ref.3, bf16[3,16,64,512]{3,2,1,0:T(8,128)(2,1)} %metric_ref.3, bf16[512,512]{1,0:T(8,128)(2,1)} %op_ref, bf16[8,5,2,64,512]{4,3,2,1,0:T(8,128)(2,1)} %all_to_all.26.y_ref.field_ref), custom_call_target="tpu_custom_call" | custom-call | flops 7927234560 | bytes 28311552 | tf_op jit(solution)/shard_map/update_xy/pallas_call | solution.py:182
  242.6 39.0 %all-to-all-done.3.z_ref = bf16[16,5,16,16,128]{4,3,2,1,0:T(8,128)(2,1)} async-done(((bf16[16,5,16,16,128]{4,3,2,1,0:T(8,128)(2,1)}), bf16[16,5,16,16,128]{4,3,2,1,0:T(8,128)(2,1)}, u32[]{:S(2)}, u32[]{:S(2)}) %all-to-all-start.3) | async-done | bytes 5242912 | tf_op jit(solution)/shard_map/all_to_all | solution.py:429
  281.7 7.8 %surface_terms.1.after_ref = f32[128,1,256]{2,1,0:T(1,128)} custom-call(s32[512,128]{1,0:T(8,128)S(1)} %broadcast_in_dim.8.cell_ref, bf16[16,5,16,16,128]{4,3,2,1,0:T(8,128)(2,1)} %all-to-all-done.3.z_ref, f32[8,512]{1,0:T(8,128)S(1)} %get-tuple-element.50.adj_ref, f32[8,512]{1,0:T(8,128)S(1)} %get-tuple-element.51.x_ref, f32[8,512]{1,0:T(8,128)S(1)} %pick_cells.5.y_ref, ...), custom_call_target="tpu_custom_call" | custom-call | flops 2684354560 | bytes 5242880 | tf_op jit(solution)/shard_map/surface_terms/pallas_call | solution.py:372
  289.4 4.8 %all-to-all-start.4 = ((f32[128,1,256]{2,1,0:T(1,128)}), f32[128,1,256]{2,1,0:T(1,128)S(1)}, u32[]{:S(2)}, u32[]{:S(2)}) async-start(f32[128,1,256]{2,1,0:T(1,128)} %surface_terms.1.after_ref), calls=%async_computation.4 | async-start | bytes 262144 | tf_op jit(solution)/shard_map/all_to_all | solution.py:440
  294.2 12.4 %update_z.1 = bf16[5,16,64,512]{3,2,1,0:T(8,128)(2,1)} custom-call(f32[5,16,64,512]{3,2,1,0:T(8,128)} %update_xy.1.before_ref, bf16[5,16,64,512]{3,2,1,0:T(8,128)(2,1)} %state_ref.3, bf16[3,16,64,512]{3,2,1,0:T(8,128)(2,1)} %metric_ref.3, bf16[16,5,16,16,128]{4,3,2,1,0:T(8,128)(2,1)} %all-to-all-done.3.z_ref, f32[128,1,256]{2,1,0:T(1,128)} %surface_terms.1.after_ref), custom_call_target="tpu_custom_call" | custom-call | flops 5242880000 | bytes 27262976 | tf_op jit(solution)/shard_map/update_z/pallas_call | solution.py:217
  306.6 0.0 all-to-all-done.4.terms_ref
  306.6 0.7 copy-done.5
  307.3 1.7 normalized.1
  (11 shorter events, 0.0 us)
Async XLA Ops:
  0.6 2.5 copy-start
  5.3 65.7 %copy-start.1 = (bf16[16,5,16,16,128]{4,3,2,1,0:T(8,128)(2,1)}, bf16[16,5,16,16,128]{4,3,2,1,0:T(8,128)(2,1)S(1)}, u32[]{:S(2)}) copy-start(bf16[16,5,16,16,128]{4,3,2,1,0:T(8,128)(2,1)S(1)} %get-tuple-element.33) | copy-start | bytes 15728644
  70.9 9.7 %copy-start.7 = (bf16[4,3,128]{2,0,1:T(4,128)(2,1)S(1)}, bf16[4,3,128]{2,0,1:T(4,128)(2,1)}, u32[]{:S(2)}) copy-start(bf16[4,3,128]{2,0,1:T(4,128)(2,1)} %param.16) | copy-start | bytes 9220
  70.9 9.7 %copy-start.6 = (bf16[256,256]{1,0:T(8,128)(2,1)S(1)}, bf16[256,256]{1,0:T(8,128)(2,1)}, u32[]{:S(2)}) copy-start(bf16[256,256]{1,0:T(8,128)(2,1)} %param.14) | copy-start | bytes 393220
  71.0 9.8 %copy-start.4 = (bf16[512,512]{1,0:T(8,128)(2,1)S(1)}, bf16[512,512]{1,0:T(8,128)(2,1)}, u32[]{:S(2)}) copy-start(bf16[512,512]{1,0:T(8,128)(2,1)} %param.13) | copy-start | bytes 1572868
  71.0 10.1 %copy-start.3 = (bf16[512,512]{1,0:T(8,128)(2,1)S(1)}, bf16[512,512]{1,0:T(8,128)(2,1)}, u32[]{:S(2)}) copy-start(bf16[512,512]{1,0:T(8,128)(2,1)} %op_ref) | copy-start | bytes 1572868
  71.0 10.3 %copy-start.8 = (s32[4,128]{1,0:T(4,128)S(1)}, s32[4,128]{1,0:T(4,128)}, u32[]{:S(2)}) copy-start(s32[4,128]{1,0:T(4,128)} %param.15) | copy-start | bytes 6148
  71.0 72.0 %all-to-all-start.1 = ((bf16[16,5,16,16,128]{4,3,2,1,0:T(8,128)(2,1)}), bf16[16,5,16,16,128]{4,3,2,1,0:T(8,128)(2,1)}, u32[]{:S(2)}, u32[]{:S(2)}) async-start(bf16[16,5,16,16,128]{4,3,2,1,0:T(8,128)(2,1)} %copy-done.1), calls=%async_computation.1 | async-start | bytes 10485760 | tf_op jit(solution)/shard_map/all_to_all | solution.py:412
  213.1 68.6 %all-to-all-start.3 = ((bf16[16,5,16,16,128]{4,3,2,1,0:T(8,128)(2,1)}), bf16[16,5,16,16,128]{4,3,2,1,0:T(8,128)(2,1)}, u32[]{:S(2)}, u32[]{:S(2)}) async-start(bf16[16,5,16,16,128]{4,3,2,1,0:T(8,128)(2,1)} %line_z.1), calls=%async_computation.3 | async-start | bytes 10485760 | tf_op jit(solution)/shard_map/all_to_all | solution.py:429
  226.3 55.4 %copy-start.2 = (bf16[512,256]{1,0:T(8,128)(2,1)S(1)}, bf16[512,256]{1,0:T(8,128)(2,1)}, u32[]{:S(2)}) copy-start(bf16[512,256]{1,0:T(8,128)(2,1)} %basis_ref.1) | copy-start | bytes 786436
  289.4 17.2 %all-to-all-start.4 = ((f32[128,1,256]{2,1,0:T(1,128)}), f32[128,1,256]{2,1,0:T(1,128)S(1)}, u32[]{:S(2)}, u32[]{:S(2)}) async-start(f32[128,1,256]{2,1,0:T(1,128)} %surface_terms.1.after_ref), calls=%async_computation.4 | async-start | bytes 262144 | tf_op jit(solution)/shard_map/all_to_all | solution.py:440
  306.6 0.7 copy-start.5

commit v5 on v4

--- a/solution.py
+++ b/solution.py
@@ -55,31 +55,37 @@
     )(*in_hbm(lines), deriv_t)
 
 
-def pieces_kernel(in_ref, y_ref, z_ref):
-    y_ref[:, 0] = in_ref[0].reshape(y_ref.shape[0], 2, CY, NX)
-    for a in range(4):
-        for b in range(4):
-            z_ref[4 * a + b, 0] = in_ref[0, :, 16 * a : 16 * a + 16, 128 * b : 128 * b + 128]
+def pieces_kernel(in_ref, y_ref, z_ref, sem):
+    fetch = []
+    for f in range(FIELDS):
+        for i in range(8):
+            planes = in_ref.at[f, pl.ds(2 * i, 2)]
+            fetch.append(pltpu.make_async_copy(planes, y_ref.at[i, f], sem.at[8 * f + i]))
+            fetch[-1].start()
+    for f in range(FIELDS):
+        for i in range(8):
+            fetch[8 * f + i].wait()
+            for a in range(4):
+                for b in range(4):
+                    part = y_ref[i, f, :, 16 * a : 16 * a + 16, 128 * b : 128 * b + 128]
+                    z_ref[4 * a + b, f, 2 * i : 2 * i + 2] = part
 
 
 def pieces(adjoint):
-    depth = 8
+    vmem = pl.BlockSpec(memory_space=pltpu.VMEM)
     return pl.pallas_call(
         pieces_kernel,
-        grid=(FIELDS, CZ // depth),
-        in_specs=[pl.BlockSpec((1, depth, CY, NX), lambda f, i: (f, i, 0, 0))],
-        out_specs=[
-            pl.BlockSpec((depth // 2, 1, 2, CY, NX), lambda f, i: (i, f, 0, 0, 0)),
-            pl.BlockSpec((16, 1, depth, 16, 128), lambda f, i: (0, f, i, 0, 0)),
-        ],
+        in_specs=[pl.BlockSpec(memory_space=pl.ANY)],
+        out_specs=[vmem, vmem],
         out_shape=[
-            jax.ShapeDtypeStruct((8, FIELDS, 2, CY, NX), BF),
-            jax.ShapeDtypeStruct((16, FIELDS, CZ, 16, 128), BF),
-        ],
-        compiler_params=params(8),
+            pltpu.VMEM((8, FIELDS, 2, CY, NX), BF),
+            pltpu.VMEM((16, FIELDS, CZ, 16, 128), BF),
+        ],
+        scratch_shapes=[pltpu.SemaphoreType.DMA((FIELDS * 8,))],
+        compiler_params=params(),
         cost_estimate=cost(adjoint.size, 6 * adjoint.size),
         name="pieces",
-    )(adjoint)
+    )(*in_hbm(adjoint))
 
 
 def line_z_kernel(in_ref, op_ref, out_ref, held, made, in_sem, out_sem):
@@ -121,8 +127,7 @@
     recip = 1.0 / state[0]
     vel = [state[1 + i] * recip for i in range(3)]
     speed_sq = vel[0] * vel[0] + vel[1] * vel[1] + vel[2] * vel[2]
-    kinetic = 0.5 * (state[1] * vel[0] + state[2] * vel[1] + state[3] * vel[2])
-    enthalpy = (state[4] + gamma_less * (state[4] - kinetic)) * recip
+    enthalpy = (1.0 + gamma_less) * (state[4] * recip) - 0.5 * gamma_less * speed_sq
     press = energy = back = None
     mom = [None] * 3
     plus = lambda a, b: b if a is None else a + b
@@ -396,7 +401,7 @@
         out_shape=jax.ShapeDtypeStruct((1, 256), F32),
         cost_estimate=cost(4 * terms.size, 4 * terms.size),
         name="normalized",
-    )(terms)
+    )(in_vmem(terms))
 
 
 def on_device(

time: 310 us -> 306 us (0.987)
  local copies, waits for them, and re-layouts: 3.82 us -> 0.68 us
    unnamed x19 -> x15, local copies, waits for them, and re-layouts: 3.17 us -> 0.04 us
where the time goes in v5:
time: 306 us; the launch traced here: 305 us
  blocking collectives  130 us (42%)
  Pallas kernels  81.2 us (27%)
  waiting for transfers between devices  71.9 us (23%)
  starting transfers between devices  20.7 us (7%)
    all_to_all x1, blocking collectives, on_device(): lines_y = lax.all_to_all(to_y, 'py', 0, 0)  65.7 us
    all_to_all x1, blocking collectives, on_device(): back_y = lax.all_to_all(products_y, 'py', 0, 0)  64.5 us
    all_to_all x1, waiting for transfers between devices, on_device(): back_z = lax.all_to_all(line_z(lines_z, deriv_zt), 'pz', 0, 0)  39.6 us
    all_to_all x1, waiting for transfers between devices, on_device(): lines_z = lax.all_to_all(to_z, 'pz', 0, 0)  32.3 us
    pallas_call x3, Pallas kernels, pick_cells(): pl.pallas_call(pick_kernel, grid=(count,), in_specs=[pl.BlockSpec((CELLS,...  18.8 us
    pallas_call x1, Pallas kernels, update_xy(): pl.pallas_call(update_xy_kernel, grid=(CZ // PLANES,), in_specs=[plane(5)...  15.8 us
    pallas_call x1, Pallas kernels, update_z(): pl.pallas_call(update_z_kernel, grid=(CZ // PLANES,), in_specs=[plane(5),...  12 us
    pallas_call x1, Pallas kernels, line_y(): pl.pallas_call(line_y_kernel, grid=(f, z), in_specs=[spec, pl.BlockSpec((...  9.75 us
  transfers between devices with their start and end apart: 3, of which 2 were waited for; matrix products, arithmetic and copies ran while one was open for 0% of the time, Pallas kernels for 21%

profile of v5, /device:TPU:1, one launch (start us, length us, event | category | flops | bytes accessed | tf_op | source)
XLA Modules:
  0.0 305.4 jit_solution(18015463588089666662)
XLA Ops:
  0.6 2.9 pieces.1
  3.6 0.0 copy-start
  3.6 65.7 %all_to_all.25.in_ref = bf16[8,5,2,64,512]{4,3,2,1,0:T(8,128)(2,1)} all-to-all(bf16[8,5,2,64,512]{4,3,2,1,0:T(8,128)(2,1)S(1)} %get-tuple-element.30), channel_id=1, replica_groups=mesh['py'=8,'pz'=16] {'py'}, dimensions={0} | all-to-all | bytes 10485760 | tf_op jit(solution)/shard_map/all_to_all | solution.py:411
  69.2 0.0 copy-done
  69.3 0.0 copy-start.2
  69.3 0.0 copy-start.6
  69.3 9.7 %all-to-all-start.1 = ((bf16[16,5,16,16,128]{4,3,2,1,0:T(8,128)(2,1)}), bf16[16,5,16,16,128]{4,3,2,1,0:T(8,128)(2,1)}, u32[]{:S(2)}, u32[]{:S(2)}) async-start(bf16[16,5,16,16,128]{4,3,2,1,0:T(8,128)(2,1)} %copy-done), calls=%async_computation.1 | async-start | bytes 10485760 | tf_op jit(solution)/shard_map/all_to_all | solution.py:417
  79.0 0.0 copy-done.5
  79.0 0.0 copy-done.4
  79.0 0.1 copy.13
  79.1 0.0 copy-done.3
  79.1 0.2 copy.11
  79.3 0.0 copy-done.2
  79.3 0.2 copy.12
  79.6 0.1 broadcast_in_dim.8.cell_ref
  79.7 4.8 %pick_cells.4.metric_ref = f32[8,512]{1,0:T(8,128)S(1)} custom-call(s32[512,128]{1,0:T(8,128)S(1)} %broadcast_in_dim.8.cell_ref, bf16[3,16,64,512]{3,2,1,0:T(8,128)(2,1)} %metric_ref.3), custom_call_target="tpu_custom_call" | custom-call | flops 1610612736 | bytes 3145728 | tf_op jit(solution)/shard_map/pick_cells/pallas_call | solution.py:278
  84.5 7.0 %pick_cells.3.state_ref = f32[8,512]{1,0:T(8,128)S(1)} custom-call(s32[512,128]{1,0:T(8,128)S(1)} %broadcast_in_dim.8.cell_ref, bf16[5,16,64,512]{3,2,1,0:T(8,128)(2,1)} %state_ref.3), custom_call_target="tpu_custom_call" | custom-call | flops 2684354560 | bytes 5242880 | tf_op jit(solution)/shard_map/pick_cells/pallas_call | solution.py:278
  91.5 7.8 %pick_x.1 = (f32[8,512]{1,0:T(8,128)S(1)}, f32[8,512]{1,0:T(8,128)S(1)}) custom-call(s32[512,128]{1,0:T(8,128)S(1)} %broadcast_in_dim.8.cell_ref, bf16[5,16,64,512]{3,2,1,0:T(8,128)(2,1)} %adj_ref.1, bf16[512,512]{1,0:T(8,128)(2,1)S(1)} %bitcast.11), custom_call_target="tpu_custom_call" | custom-call | flops 2684354560 | bytes 5242880 | tf_op jit(solution)/shard_map/pick_x/pallas_call | solution.py:316
  99.3 9.7 %line_y.1 = bf16[8,5,2,64,512]{4,3,2,1,0:T(8,128)(2,1)} custom-call(bf16[8,5,2,64,512]{4,3,2,1,0:T(8,128)(2,1)} %all_to_all.25.in_ref, bf16[512,512]{1,0:T(8,128)(2,1)S(1)} %bitcast.10), custom_call_target="tpu_custom_call" | custom-call | flops 2684354560 | bytes 10485760 | tf_op jit(solution)/shard_map/line_y/pallas_call | solution.py:46
  109.0 32.3 %all-to-all-done.1.in_ref = bf16[16,5,16,16,128]{4,3,2,1,0:T(8,128)(2,1)} async-done(((bf16[16,5,16,16,128]{4,3,2,1,0:T(8,128)(2,1)}), bf16[16,5,16,16,128]{4,3,2,1,0:T(8,128)(2,1)}, u32[]{:S(2)}, u32[]{:S(2)}) %all-to-all-start.1) | async-done | bytes 5242912 | tf_op jit(solution)/shard_map/all_to_all | solution.py:417
  141.3 64.5 %all_to_all.26.y_ref.field_ref = bf16[8,5,2,64,512]{4,3,2,1,0:T(8,128)(2,1)} all-to-all(bf16[8,5,2,64,512]{4,3,2,1,0:T(8,128)(2,1)} %line_y.1), channel_id=1, replica_groups=mesh['py'=8,'pz'=16] {'py'}, dimensions={0} | all-to-all | bytes 10485760 | tf_op jit(solution)/shard_map/all_to_all | solution.py:432
  205.8 5.6 %line_z.1 = bf16[16,5,16,16,128]{4,3,2,1,0:T(8,128)(2,1)} custom-call(bf16[16,5,16,16,128]{4,3,2,1,0:T(8,128)(2,1)} %all-to-all-done.1.in_ref, bf16[256,256]{1,0:T(8,128)(2,1)S(1)} %bitcast.12), custom_call_target="tpu_custom_call" | custom-call | flops 1342177280 | bytes 10485760 | tf_op jit(solution)/shard_map/line_z/pallas_call | solution.py:109
  211.4 6.2 %all-to-all-start.3 = ((bf16[16,5,16,16,128]{4,3,2,1,0:T(8,128)(2,1)}), bf16[16,5,16,16,128]{4,3,2,1,0:T(8,128)(2,1)}, u32[]{:S(2)}, u32[]{:S(2)}) async-start(bf16[16,5,16,16,128]{4,3,2,1,0:T(8,128)(2,1)} %line_z.1), calls=%async_computation.3 | async-start | bytes 10485760 | tf_op jit(solution)/shard_map/all_to_all | solution.py:434
  217.5 7.0 %pick_cells.5.y_ref = f32[8,512]{1,0:T(8,128)S(1)} custom-call(s32[512,128]{1,0:T(8,128)S(1)} %broadcast_in_dim.8.cell_ref, bf16[8,5,2,64,512]{4,3,2,1,0:T(8,128)(2,1)} %all_to_all.26.y_ref.field_ref), custom_call_target="tpu_custom_call" | custom-call | flops 2684354560 | bytes 5242880 | tf_op jit(solution)/shard_map/pick_cells/pallas_call | solution.py:278
  224.6 0.0 copy-start.1
  224.6 15.8 %update_xy.1.before_ref = f32[5,16,64,512]{3,2,1,0:T(8,128)} custom-call(bf16[5,16,64,512]{3,2,1,0:T(8,128)(2,1)} %adj_ref.1, bf16[5,16,64,512]{3,2,1,0:T(8,128)(2,1)} %state_ref.3, bf16[3,16,64,512]{3,2,1,0:T(8,128)(2,1)} %metric_ref.3, bf16[512,512]{1,0:T(8,128)(2,1)} %op_ref, bf16[8,5,2,64,512]{4,3,2,1,0:T(8,128)(2,1)} %all_to_all.26.y_ref.field_ref), custom_call_target="tpu_custom_call" | custom-call | flops 7927234560 | bytes 28311552 | tf_op jit(solution)/shard_map/update_xy/pallas_call | solution.py:187
  240.4 39.6 %all-to-all-done.3.z_ref = bf16[16,5,16,16,128]{4,3,2,1,0:T(8,128)(2,1)} async-done(((bf16[16,5,16,16,128]{4,3,2,1,0:T(8,128)(2,1)}), bf16[16,5,16,16,128]{4,3,2,1,0:T(8,128)(2,1)}, u32[]{:S(2)}, u32[]{:S(2)}) %all-to-all-start.3) | async-done | bytes 5242912 | tf_op jit(solution)/shard_map/all_to_all | solution.py:434
  280.0 7.8 %surface_terms.1.after_ref = f32[128,1,256]{2,1,0:T(1,128)} custom-call(s32[512,128]{1,0:T(8,128)S(1)} %broadcast_in_dim.8.cell_ref, bf16[16,5,16,16,128]{4,3,2,1,0:T(8,128)(2,1)} %all-to-all-done.3.z_ref, f32[8,512]{1,0:T(8,128)S(1)} %get-tuple-element.50.adj_ref, f32[8,512]{1,0:T(8,128)S(1)} %get-tuple-element.51.x_ref, f32[8,512]{1,0:T(8,128)S(1)} %pick_cells.5.y_ref, ...), custom_call_target="tpu_custom_call" | custom-call | flops 2684354560 | bytes 5242880 | tf_op jit(solution)/shard_map/surface_terms/pallas_call | solution.py:377
  287.7 4.8 %all-to-all-start.4 = ((f32[128,1,256]{2,1,0:T(1,128)}), f32[128,1,256]{2,1,0:T(1,128)S(1)}, u32[]{:S(2)}, u32[]{:S(2)}) async-start(f32[128,1,256]{2,1,0:T(1,128)} %surface_terms.1.after_ref), calls=%async_computation.4 | async-start | bytes 262144 | tf_op jit(solution)/shard_map/all_to_all | solution.py:445
  292.5 12.0 %update_z.1 = bf16[5,16,64,512]{3,2,1,0:T(8,128)(2,1)} custom-call(f32[5,16,64,512]{3,2,1,0:T(8,128)} %update_xy.1.before_ref, bf16[5,16,64,512]{3,2,1,0:T(8,128)(2,1)} %state_ref.3, bf16[3,16,64,512]{3,2,1,0:T(8,128)(2,1)} %metric_ref.3, bf16[16,5,16,16,128]{4,3,2,1,0:T(8,128)(2,1)} %all-to-all-done.3.z_ref, f32[128,1,256]{2,1,0:T(1,128)} %surface_terms.1.after_ref), custom_call_target="tpu_custom_call" | custom-call | flops 5242880000 | bytes 27262976 | tf_op jit(solution)/shard_map/update_z/pallas_call | solution.py:222
  304.6 0.0 all-to-all-done.4.terms_ref
  304.6 0.8 normalized.1
  (7 shorter events, 0.0 us)
Async XLA Ops:
  3.6 65.7 %copy-start = (bf16[16,5,16,16,128]{4,3,2,1,0:T(8,128)(2,1)}, bf16[16,5,16,16,128]{4,3,2,1,0:T(8,128)(2,1)S(1)}, u32[]{:S(2)}) copy-start(bf16[16,5,16,16,128]{4,3,2,1,0:T(8,128)(2,1)S(1)} %get-tuple-element.33) | copy-start | bytes 15728644
  69.3 9.7 %copy-start.5 = (bf16[4,3,128]{2,0,1:T(4,128)(2,1)S(1)}, bf16[4,3,128]{2,0,1:T(4,128)(2,1)}, u32[]{:S(2)}) copy-start(bf16[4,3,128]{2,0,1:T(4,128)(2,1)} %param.16) | copy-start | bytes 9220
  69.3 9.7 %copy-start.4 = (bf16[256,256]{1,0:T(8,128)(2,1)S(1)}, bf16[256,256]{1,0:T(8,128)(2,1)}, u32[]{:S(2)}) copy-start(bf16[256,256]{1,0:T(8,128)(2,1)} %param.14) | copy-start | bytes 393220
  69.3 9.8 %copy-start.3 = (bf16[512,512]{1,0:T(8,128)(2,1)S(1)}, bf16[512,512]{1,0:T(8,128)(2,1)}, u32[]{:S(2)}) copy-start(bf16[512,512]{1,0:T(8,128)(2,1)} %param.13) | copy-start | bytes 1572868
  69.3 10.1 %copy-start.2 = (bf16[512,512]{1,0:T(8,128)(2,1)S(1)}, bf16[512,512]{1,0:T(8,128)(2,1)}, u32[]{:S(2)}) copy-start(bf16[512,512]{1,0:T(8,128)(2,1)} %op_ref) | copy-start | bytes 1572868
  69.3 10.3 %copy-start.6 = (s32[4,128]{1,0:T(4,128)S(1)}, s32[4,128]{1,0:T(4,128)}, u32[]{:S(2)}) copy-start(s32[4,128]{1,0:T(4,128)} %param.15) | copy-start | bytes 6148
  69.3 72.0 %all-to-all-start.1 = ((bf16[16,5,16,16,128]{4,3,2,1,0:T(8,128)(2,1)}), bf16[16,5,16,16,128]{4,3,2,1,0:T(8,128)(2,1)}, u32[]{:S(2)}, u32[]{:S(2)}) async-start(bf16[16,5,16,16,128]{4,3,2,1,0:T(8,128)(2,1)} %copy-done), calls=%async_computation.1 | async-start | bytes 10485760 | tf_op jit(solution)/shard_map/all_to_all | solution.py:417
  211.4 68.6 %all-to-all-start.3 = ((bf16[16,5,16,16,128]{4,3,2,1,0:T(8,128)(2,1)}), bf16[16,5,16,16,128]{4,3,2,1,0:T(8,128)(2,1)}, u32[]{:S(2)}, u32[]{:S(2)}) async-start(bf16[16,5,16,16,128]{4,3,2,1,0:T(8,128)(2,1)} %line_z.1), calls=%async_computation.3 | async-start | bytes 10485760 | tf_op jit(solution)/shard_map/all_to_all | solution.py:434
  224.6 55.4 %copy-start.1 = (bf16[512,256]{1,0:T(8,128)(2,1)S(1)}, bf16[512,256]{1,0:T(8,128)(2,1)}, u32[]{:S(2)}) copy-start(bf16[512,256]{1,0:T(8,128)(2,1)} %basis_ref.1) | copy-start | bytes 786436
  287.7 16.8 %all-to-all-start.4 = ((f32[128,1,256]{2,1,0:T(1,128)}), f32[128,1,256]{2,1,0:T(1,128)S(1)}, u32[]{:S(2)}, u32[]{:S(2)}) async-start(f32[128,1,256]{2,1,0:T(1,128)} %surface_terms.1.after_ref), calls=%async_computation.4 | async-start | bytes 262144 | tf_op jit(solution)/shard_map/all_to_all | solution.py:445

commit v6 on v5

--- a/solution.py
+++ b/solution.py
@@ -176,7 +176,7 @@
         ]
         new = update(load(adj_ref, 5), load(state_ref, 5), load(metric_ref, 2), alongs, (0, 1))
         for f in range(5):
-            out_ref[f, z, rows, cols] = new[f]
+            out_ref[f, z, rows, cols] = new[f].astype(BF)
 
     chunks(body)
 
@@ -195,7 +195,7 @@
             pl.BlockSpec((PLANES // 2, 5, 2, CY, NX), lambda i: (i, 0, 0, 0, 0)),
         ],
         out_specs=plane(5),
-        out_shape=hbm_out(adjoint.shape, F32),
+        out_shape=hbm_out(adjoint.shape, BF),
         scratch_shapes=[pltpu.VMEM((FIELDS, PLANES, CY, NX), F32)],
         compiler_params=params(),
         cost_estimate=cost(cells * 2 * 5 * NX + cells * 10000, cells * 54),
@@ -205,7 +205,7 @@
 
 def update_z_kernel(before_ref, state_ref, metric_ref, z_ref, after_ref, out_ref):
     def body(z, piece, rows, cols):
-        before = [before_ref[f, z, rows, cols] for f in range(5)]
+        before = [before_ref[f, z, rows, cols].astype(F32) for f in range(5)]
         state = [state_ref[f, z, rows, cols].astype(F32) for f in range(5)]
         metric = {2: metric_ref[0, z, rows, cols].astype(F32)}
         along = {2: [z_ref[piece, f, z].astype(F32) for f in range(5)]}
@@ -234,7 +234,7 @@
         compiler_params=params(),
         cost_estimate=cost(cells * 10000, cells * 52),
         name="update_z",
-    )(*in_hbm(before, state, metric), in_vmem(along_z), after)
+    )(*in_hbm(before, state, metric), *in_hbm(along_z), after)
 
 
 def pick_rows(onehot_ref, row, f):
@@ -337,15 +337,18 @@
 
 def surface_kernel(
     cell_ref, z_ref, adj_ref, x_ref, y_ref, state_ref, metric_ref, normal_ref, basis_ref,
-    out_ref, onehot, total,
+    out_ref, onehot, total, pieces_z, sem,
 ):
+    fetch = pltpu.make_async_copy(z_ref, pieces_z, sem)
+    fetch.start()
     cell = cell_ref[:, 0:1]
     x, y, z = cell % NX, cell // NX % CY, cell // (NX * CY)
     row = ((y // 16 * 4 + x // 128) * CZ + z) * 16 + y % 16
     for n in range(4):
         at = lax.broadcasted_iota(jnp.int32, (CELLS, 1024), 1) + 1024 * n
         onehot[:, 1024 * n : 1024 * (n + 1)] = jnp.where(at == row, 1.0, 0.0).astype(BF)
-    fields = [z_ref[:, f].reshape(4096, 128) for f in range(FIELDS)]
+    fetch.wait()
+    fields = [pieces_z[:, f].reshape(4096, 128) for f in range(FIELDS)]
     total[...] = jnp.dot(
         onehot[...], jnp.concatenate(fields, axis=1), preferred_element_type=F32
     )
@@ -376,17 +379,19 @@
     vmem = pl.BlockSpec(memory_space=pltpu.VMEM)
     return pl.pallas_call(
         surface_kernel,
-        in_specs=[vmem] * 9,
+        in_specs=[vmem, pl.BlockSpec(memory_space=pl.ANY)] + [vmem] * 7,
         out_specs=vmem,
         out_shape=jax.ShapeDtypeStruct((128, 1, 256), F32),
         scratch_shapes=[
             pltpu.VMEM((CELLS, 4096), BF),
             pltpu.VMEM((CELLS, FIELDS * 128), F32),
+            pltpu.VMEM((16, FIELDS, CZ, 16, 128), BF),
+            pltpu.SemaphoreType.DMA,
         ],
         compiler_params=params(),
         cost_estimate=cost(2 * 5 * CELLS * CZ * CY * NX, 5 * CZ * CY * NX * 2),
         name="surface_terms",
-    )(cells, in_vmem(along_z), adj, along_x, along_y, state, metric, normals, basis)
+    )(cells, *in_hbm(along_z), adj, along_x, along_y, state, metric, normals, basis)
 
 
 def normalized_kernel(terms_ref, out_ref):

time: 306 us -> 305 us (level)
  no operation moved by 1% of the time
where the time goes in v6:
time: 305 us; the launch traced here: 304 us
  blocking collectives  130 us (43%)
  Pallas kernels  79.8 us (26%)
  waiting for transfers between devices  72.3 us (24%)
  starting transfers between devices  20.7 us (7%)
    all_to_all x1, blocking collectives, on_device(): lines_y = lax.all_to_all(to_y, 'py', 0, 0)  65.7 us
    all_to_all x1, blocking collectives, on_device(): back_y = lax.all_to_all(products_y, 'py', 0, 0)  64.5 us
    all_to_all x1, waiting for transfers between devices, on_device(): back_z = lax.all_to_all(line_z(lines_z, deriv_zt), 'pz', 0, 0)  40 us
    all_to_all x1, waiting for transfers between devices, on_device(): lines_z = lax.all_to_all(to_z, 'pz', 0, 0)  32.3 us
    pallas_call x3, Pallas kernels, pick_cells(): pl.pallas_call(pick_kernel, grid=(count,), in_specs=[pl.BlockSpec((CELLS,...  18.8 us
    pallas_call x1, Pallas kernels, update_xy(): pl.pallas_call(update_xy_kernel, grid=(CZ // PLANES,), in_specs=[plane(5)...  15.4 us
    pallas_call x1, Pallas kernels, update_z(): pl.pallas_call(update_z_kernel, grid=(CZ // PLANES,), in_specs=[plane(5),...  11 us
    pallas_call x1, Pallas kernels, line_y(): pl.pallas_call(line_y_kernel, grid=(f, z), in_specs=[spec, pl.BlockSpec((...  9.75 us
  transfers between devices with their start and end apart: 3, of which 2 were waited for; matrix products, arithmetic and copies ran while one was open for 0% of the time, Pallas kernels for 21%

profile of v6, /device:TPU:1, one launch (start us, length us, event | category | flops | bytes accessed | tf_op | source)
XLA Modules:
  0.0 304.4 jit_solution(17218990669199902388)
XLA Ops:
  0.6 2.9 pieces.1
  3.6 0.0 copy-start
  3.6 65.7 %all_to_all.25.in_ref = bf16[8,5,2,64,512]{4,3,2,1,0:T(8,128)(2,1)} all-to-all(bf16[8,5,2,64,512]{4,3,2,1,0:T(8,128)(2,1)S(1)} %get-tuple-element.30), channel_id=1, replica_groups=mesh['py'=8,'pz'=16] {'py'}, dimensions={0} | all-to-all | bytes 10485760 | tf_op jit(solution)/shard_map/all_to_all | solution.py:416
  69.2 0.0 copy-done
  69.3 0.0 copy-start.4
  69.3 0.0 copy-start.6
  69.3 9.7 %all-to-all-start.1 = ((bf16[16,5,16,16,128]{4,3,2,1,0:T(8,128)(2,1)}), bf16[16,5,16,16,128]{4,3,2,1,0:T(8,128)(2,1)}, u32[]{:S(2)}, u32[]{:S(2)}) async-start(bf16[16,5,16,16,128]{4,3,2,1,0:T(8,128)(2,1)} %copy-done), calls=%async_computation.1 | async-start | bytes 10485760 | tf_op jit(solution)/shard_map/all_to_all | solution.py:422
  79.0 0.0 copy-done.2
  79.0 0.2 copy.11
  79.2 0.0 copy-done.5
  79.2 0.0 copy-done.3
  79.2 0.2 copy.12
  79.4 0.1 copy.13
  79.6 0.1 broadcast_in_dim.8.cell_ref
  79.7 4.8 %pick_cells.4.metric_ref = f32[8,512]{1,0:T(8,128)S(1)} custom-call(s32[512,128]{1,0:T(8,128)S(1)} %broadcast_in_dim.8.cell_ref, bf16[3,16,64,512]{3,2,1,0:T(8,128)(2,1)} %metric_ref.3), custom_call_target="tpu_custom_call" | custom-call | flops 1610612736 | bytes 3145728 | tf_op jit(solution)/shard_map/pick_cells/pallas_call | solution.py:278
  84.5 7.8 %pick_x.1 = (f32[8,512]{1,0:T(8,128)S(1)}, f32[8,512]{1,0:T(8,128)S(1)}) custom-call(s32[512,128]{1,0:T(8,128)S(1)} %broadcast_in_dim.8.cell_ref, bf16[5,16,64,512]{3,2,1,0:T(8,128)(2,1)} %adj_ref.1, bf16[512,512]{1,0:T(8,128)(2,1)S(1)} %bitcast.11), custom_call_target="tpu_custom_call" | custom-call | flops 2684354560 | bytes 5242880 | tf_op jit(solution)/shard_map/pick_x/pallas_call | solution.py:316
  92.2 7.0 %pick_cells.3.state_ref = f32[8,512]{1,0:T(8,128)S(1)} custom-call(s32[512,128]{1,0:T(8,128)S(1)} %broadcast_in_dim.8.cell_ref, bf16[5,16,64,512]{3,2,1,0:T(8,128)(2,1)} %state_ref.3), custom_call_target="tpu_custom_call" | custom-call | flops 2684354560 | bytes 5242880 | tf_op jit(solution)/shard_map/pick_cells/pallas_call | solution.py:278
  99.3 9.7 %line_y.1 = bf16[8,5,2,64,512]{4,3,2,1,0:T(8,128)(2,1)} custom-call(bf16[8,5,2,64,512]{4,3,2,1,0:T(8,128)(2,1)} %all_to_all.25.in_ref, bf16[512,512]{1,0:T(8,128)(2,1)S(1)} %bitcast.10), custom_call_target="tpu_custom_call" | custom-call | flops 2684354560 | bytes 10485760 | tf_op jit(solution)/shard_map/line_y/pallas_call | solution.py:46
  109.0 32.3 %all-to-all-done.1.in_ref = bf16[16,5,16,16,128]{4,3,2,1,0:T(8,128)(2,1)} async-done(((bf16[16,5,16,16,128]{4,3,2,1,0:T(8,128)(2,1)}), bf16[16,5,16,16,128]{4,3,2,1,0:T(8,128)(2,1)}, u32[]{:S(2)}, u32[]{:S(2)}) %all-to-all-start.1) | async-done | bytes 5242912 | tf_op jit(solution)/shard_map/all_to_all | solution.py:422
  141.3 64.5 %all_to_all.26.y_ref.field_ref = bf16[8,5,2,64,512]{4,3,2,1,0:T(8,128)(2,1)} all-to-all(bf16[8,5,2,64,512]{4,3,2,1,0:T(8,128)(2,1)} %line_y.1), channel_id=1, replica_groups=mesh['py'=8,'pz'=16] {'py'}, dimensions={0} | all-to-all | bytes 10485760 | tf_op jit(solution)/shard_map/all_to_all | solution.py:437
  205.8 5.6 %line_z.1 = bf16[16,5,16,16,128]{4,3,2,1,0:T(8,128)(2,1)} custom-call(bf16[16,5,16,16,128]{4,3,2,1,0:T(8,128)(2,1)} %all-to-all-done.1.in_ref, bf16[256,256]{1,0:T(8,128)(2,1)S(1)} %bitcast.12), custom_call_target="tpu_custom_call" | custom-call | flops 1342177280 | bytes 10485760 | tf_op jit(solution)/shard_map/line_z/pallas_call | solution.py:109
  211.4 6.2 %all-to-all-start.3 = ((bf16[16,5,16,16,128]{4,3,2,1,0:T(8,128)(2,1)}), bf16[16,5,16,16,128]{4,3,2,1,0:T(8,128)(2,1)}, u32[]{:S(2)}, u32[]{:S(2)}) async-start(bf16[16,5,16,16,128]{4,3,2,1,0:T(8,128)(2,1)} %line_z.1), calls=%async_computation.3 | async-start | bytes 10485760 | tf_op jit(solution)/shard_map/all_to_all | solution.py:439
  217.5 7.0 %pick_cells.5.y_ref = f32[8,512]{1,0:T(8,128)S(1)} custom-call(s32[512,128]{1,0:T(8,128)S(1)} %broadcast_in_dim.8.cell_ref, bf16[8,5,2,64,512]{4,3,2,1,0:T(8,128)(2,1)} %all_to_all.26.y_ref.field_ref), custom_call_target="tpu_custom_call" | custom-call | flops 2684354560 | bytes 5242880 | tf_op jit(solution)/shard_map/pick_cells/pallas_call | solution.py:278
  224.6 0.0 copy-start.1
  224.6 15.4 %update_xy.1.before_ref = bf16[5,16,64,512]{3,2,1,0:T(8,128)(2,1)} custom-call(bf16[5,16,64,512]{3,2,1,0:T(8,128)(2,1)} %adj_ref.1, bf16[5,16,64,512]{3,2,1,0:T(8,128)(2,1)} %state_ref.3, bf16[3,16,64,512]{3,2,1,0:T(8,128)(2,1)} %metric_ref.3, bf16[512,512]{1,0:T(8,128)(2,1)} %op_ref, bf16[8,5,2,64,512]{4,3,2,1,0:T(8,128)(2,1)} %all_to_all.26.y_ref.field_ref), custom_call_target="tpu_custom_call" | custom-call | flops 7927234560 | bytes 28311552 | tf_op jit(solution)/shard_map/update_xy/pallas_call | solution.py:187
  240.0 40.0 %all-to-all-done.3.z_ref = bf16[16,5,16,16,128]{4,3,2,1,0:T(8,128)(2,1)} async-done(((bf16[16,5,16,16,128]{4,3,2,1,0:T(8,128)(2,1)}), bf16[16,5,16,16,128]{4,3,2,1,0:T(8,128)(2,1)}, u32[]{:S(2)}, u32[]{:S(2)}) %all-to-all-start.3) | async-done | bytes 5242912 | tf_op jit(solution)/shard_map/all_to_all | solution.py:439
  280.0 0.0 copy-done.1
  280.0 7.8 %surface_terms.1.after_ref = f32[128,1,256]{2,1,0:T(1,128)} custom-call(s32[512,128]{1,0:T(8,128)S(1)} %broadcast_in_dim.8.cell_ref, bf16[16,5,16,16,128]{4,3,2,1,0:T(8,128)(2,1)} %all-to-all-done.3.z_ref, f32[8,512]{1,0:T(8,128)S(1)} %get-tuple-element.50.adj_ref, f32[8,512]{1,0:T(8,128)S(1)} %get-tuple-element.51.x_ref, f32[8,512]{1,0:T(8,128)S(1)} %pick_cells.5.y_ref, ...), custom_call_target="tpu_custom_call" | custom-call | flops 2684354560 | bytes 5242880 | tf_op jit(solution)/shard_map/surface_terms/pallas_call | solution.py:380
  287.7 4.8 %all-to-all-start.4 = ((f32[128,1,256]{2,1,0:T(1,128)}), f32[128,1,256]{2,1,0:T(1,128)S(1)}, u32[]{:S(2)}, u32[]{:S(2)}) async-start(f32[128,1,256]{2,1,0:T(1,128)} %surface_terms.1.after_ref), calls=%async_computation.4 | async-start | bytes 262144 | tf_op jit(solution)/shard_map/all_to_all | solution.py:450
  292.6 11.0 %update_z.1 = bf16[5,16,64,512]{3,2,1,0:T(8,128)(2,1)} custom-call(bf16[5,16,64,512]{3,2,1,0:T(8,128)(2,1)} %update_xy.1.before_ref, bf16[5,16,64,512]{3,2,1,0:T(8,128)(2,1)} %state_ref.3, bf16[3,16,64,512]{3,2,1,0:T(8,128)(2,1)} %metric_ref.3, bf16[16,5,16,16,128]{4,3,2,1,0:T(8,128)(2,1)} %all-to-all-done.3.z_ref, f32[128,1,256]{2,1,0:T(1,128)} %surface_terms.1.after_ref), custom_call_target="tpu_custom_call" | custom-call | flops 5242880000 | bytes 27262976 | tf_op jit(solution)/shard_map/update_z/pallas_call | solution.py:222
  303.6 0.0 all-to-all-done.4.terms_ref
  303.6 0.8 normalized.1
  (7 shorter events, 0.0 us)
Async XLA Ops:
  3.6 65.7 %copy-start = (bf16[16,5,16,16,128]{4,3,2,1,0:T(8,128)(2,1)}, bf16[16,5,16,16,128]{4,3,2,1,0:T(8,128)(2,1)S(1)}, u32[]{:S(2)}) copy-start(bf16[16,5,16,16,128]{4,3,2,1,0:T(8,128)(2,1)S(1)} %get-tuple-element.33) | copy-start | bytes 15728644
  69.3 9.7 %copy-start.2 = (bf16[512,512]{1,0:T(8,128)(2,1)S(1)}, bf16[512,512]{1,0:T(8,128)(2,1)}, u32[]{:S(2)}) copy-start(bf16[512,512]{1,0:T(8,128)(2,1)} %param.13) | copy-start | bytes 1572868
  69.3 9.9 %copy-start.5 = (bf16[4,3,128]{2,0,1:T(4,128)(2,1)S(1)}, bf16[4,3,128]{2,0,1:T(4,128)(2,1)}, u32[]{:S(2)}) copy-start(bf16[4,3,128]{2,0,1:T(4,128)(2,1)} %param.16) | copy-start | bytes 9220
  69.3 9.9 %copy-start.3 = (bf16[512,512]{1,0:T(8,128)(2,1)S(1)}, bf16[512,512]{1,0:T(8,128)(2,1)}, u32[]{:S(2)}) copy-start(bf16[512,512]{1,0:T(8,128)(2,1)} %op_ref) | copy-start | bytes 1572868
  69.3 10.2 %copy-start.4 = (bf16[256,256]{1,0:T(8,128)(2,1)S(1)}, bf16[256,256]{1,0:T(8,128)(2,1)}, u32[]{:S(2)}) copy-start(bf16[256,256]{1,0:T(8,128)(2,1)} %param.14) | copy-start | bytes 393220
  69.3 10.3 %copy-start.6 = (s32[4,128]{1,0:T(4,128)S(1)}, s32[4,128]{1,0:T(4,128)}, u32[]{:S(2)}) copy-start(s32[4,128]{1,0:T(4,128)} %param.15) | copy-start | bytes 6148
  69.3 72.0 %all-to-all-start.1 = ((bf16[16,5,16,16,128]{4,3,2,1,0:T(8,128)(2,1)}), bf16[16,5,16,16,128]{4,3,2,1,0:T(8,128)(2,1)}, u32[]{:S(2)}, u32[]{:S(2)}) async-start(bf16[16,5,16,16,128]{4,3,2,1,0:T(8,128)(2,1)} %copy-done), calls=%async_computation.1 | async-start | bytes 10485760 | tf_op jit(solution)/shard_map/all_to_all | solution.py:422
  211.4 68.6 %all-to-all-start.3 = ((bf16[16,5,16,16,128]{4,3,2,1,0:T(8,128)(2,1)}), bf16[16,5,16,16,128]{4,3,2,1,0:T(8,128)(2,1)}, u32[]{:S(2)}, u32[]{:S(2)}) async-start(bf16[16,5,16,16,128]{4,3,2,1,0:T(8,128)(2,1)} %line_z.1), calls=%async_computation.3 | async-start | bytes 10485760 | tf_op jit(solution)/shard_map/all_to_all | solution.py:439
  224.6 55.4 %copy-start.1 = (bf16[512,256]{1,0:T(8,128)(2,1)S(1)}, bf16[512,256]{1,0:T(8,128)(2,1)}, u32[]{:S(2)}) copy-start(bf16[512,256]{1,0:T(8,128)(2,1)} %basis_ref.1) | copy-start | bytes 786436
  287.7 15.8 %all-to-all-start.4 = ((f32[128,1,256]{2,1,0:T(1,128)}), f32[128,1,256]{2,1,0:T(1,128)S(1)}, u32[]{:S(2)}, u32[]{:S(2)}) async-start(f32[128,1,256]{2,1,0:T(1,128)} %surface_terms.1.after_ref), calls=%async_computation.4 | async-start | bytes 262144 | tf_op jit(solution)/shard_map/all_to_all | solution.py:450

commit v7 on v6

--- a/solution.py
+++ b/solution.py
@@ -93,9 +93,12 @@
     for f in range(FIELDS):
         fetch.append(pltpu.make_async_copy(in_ref.at[:, f], held.at[f], in_sem.at[f]))
         send.append(pltpu.make_async_copy(made.at[f], out_ref.at[:, f], out_sem.at[f]))
+    for f in range(3):
         fetch[f].start()
     for f in range(FIELDS):
         fetch[f].wait()
+        if f + 3 < FIELDS:
+            fetch[f + 3].start()
         line = held[f].reshape(NZ, 16 * 128)
         out = jnp.dot(op_ref[...], line, preferred_element_type=F32).astype(BF)
         made[f] = out.reshape(16, CZ, 16, 128)
@@ -176,7 +179,7 @@
         ]
         new = update(load(adj_ref, 5), load(state_ref, 5), load(metric_ref, 2), alongs, (0, 1))
         for f in range(5):
-            out_ref[f, z, rows, cols] = new[f].astype(BF)
+            out_ref[f, z, rows, cols] = new[f]
 
     chunks(body)
 
@@ -195,7 +198,7 @@
             pl.BlockSpec((PLANES // 2, 5, 2, CY, NX), lambda i: (i, 0, 0, 0, 0)),
         ],
         out_specs=plane(5),
-        out_shape=hbm_out(adjoint.shape, BF),
+        out_shape=hbm_out(adjoint.shape, F32),
         scratch_shapes=[pltpu.VMEM((FIELDS, PLANES, CY, NX), F32)],
         compiler_params=params(),
         cost_estimate=cost(cells * 2 * 5 * NX + cells * 10000, cells * 54),
@@ -205,7 +208,7 @@
 
 def update_z_kernel(before_ref, state_ref, metric_ref, z_ref, after_ref, out_ref):
     def body(z, piece, rows, cols):
-        before = [before_ref[f, z, rows, cols].astype(F32) for f in range(5)]
+        before = [before_ref[f, z, rows, cols] for f in range(5)]
         state = [state_ref[f, z, rows, cols].astype(F32) for f in range(5)]
         metric = {2: metric_ref[0, z, rows, cols].astype(F32)}
         along = {2: [z_ref[piece, f, z].astype(F32) for f in range(5)]}

time: 305 us -> 306 us (level)
  no operation moved by 1% of the time
where the time goes in v7:
time: 306 us; the launch traced here: 305 us
  blocking collectives  130 us (42%)
  Pallas kernels  81.2 us (27%)
  waiting for transfers between devices  71.9 us (23%)
  starting transfers between devices  20.7 us (7%)
    all_to_all x1, blocking collectives, on_device(): lines_y = lax.all_to_all(to_y, 'py', 0, 0)  65.7 us
    all_to_all x1, blocking collectives, on_device(): back_y = lax.all_to_all(products_y, 'py', 0, 0)  64.5 us
    all_to_all x1, waiting for transfers between devices, on_device(): back_z = lax.all_to_all(line_z(lines_z, deriv_zt), 'pz', 0, 0)  39.6 us
    all_to_all x1, waiting for transfers between devices, on_device(): lines_z = lax.all_to_all(to_z, 'pz', 0, 0)  32.3 us
    pallas_call x3, Pallas kernels, pick_cells(): pl.pallas_call(pick_kernel, grid=(count,), in_specs=[pl.BlockSpec((CELLS,...  18.8 us
    pallas_call x1, Pallas kernels, update_xy(): pl.pallas_call(update_xy_kernel, grid=(CZ // PLANES,), in_specs=[plane(5)...  15.8 us
    pallas_call x1, Pallas kernels, update_z(): pl.pallas_call(update_z_kernel, grid=(CZ // PLANES,), in_specs=[plane(5),...  12 us
    pallas_call x1, Pallas kernels, line_y(): pl.pallas_call(line_y_kernel, grid=(f, z), in_specs=[spec, pl.BlockSpec((...  9.75 us
  transfers between devices with their start and end apart: 3, of which 2 were waited for; matrix products, arithmetic and copies ran while one was open for 0% of the time, Pallas kernels for 21%

profile of v7, /device:TPU:1, one launch (start us, length us, event | category | flops | bytes accessed | tf_op | source)
XLA Modules:
  0.0 305.4 jit_solution(12377527595602374289)
XLA Ops:
  0.6 2.9 pieces.1
  3.6 0.0 copy-start
  3.6 65.7 %all_to_all.25.in_ref = bf16[8,5,2,64,512]{4,3,2,1,0:T(8,128)(2,1)} all-to-all(bf16[8,5,2,64,512]{4,3,2,1,0:T(8,128)(2,1)S(1)} %get-tuple-element.30), channel_id=1, replica_groups=mesh['py'=8,'pz'=16] {'py'}, dimensions={0} | all-to-all | bytes 10485760 | tf_op jit(solution)/shard_map/all_to_all | solution.py:419
  69.2 0.0 copy-done
  69.3 0.0 copy-start.2
  69.3 0.0 copy-start.6
  69.3 9.7 %all-to-all-start.1 = ((bf16[16,5,16,16,128]{4,3,2,1,0:T(8,128)(2,1)}), bf16[16,5,16,16,128]{4,3,2,1,0:T(8,128)(2,1)}, u32[]{:S(2)}, u32[]{:S(2)}) async-start(bf16[16,5,16,16,128]{4,3,2,1,0:T(8,128)(2,1)} %copy-done), calls=%async_computation.1 | async-start | bytes 10485760 | tf_op jit(solution)/shard_map/all_to_all | solution.py:425
  79.0 0.0 copy-done.5
  79.0 0.0 copy-done.4
  79.0 0.1 copy.13
  79.1 0.0 copy-done.3
  79.1 0.2 copy.11
  79.3 0.0 copy-done.2
  79.3 0.2 copy.12
  79.6 0.1 broadcast_in_dim.8.cell_ref
  79.7 4.8 %pick_cells.4.metric_ref = f32[8,512]{1,0:T(8,128)S(1)} custom-call(s32[512,128]{1,0:T(8,128)S(1)} %broadcast_in_dim.8.cell_ref, bf16[3,16,64,512]{3,2,1,0:T(8,128)(2,1)} %metric_ref.3), custom_call_target="tpu_custom_call" | custom-call | flops 1610612736 | bytes 3145728 | tf_op jit(solution)/shard_map/pick_cells/pallas_call | solution.py:281
  84.5 7.0 %pick_cells.3.state_ref = f32[8,512]{1,0:T(8,128)S(1)} custom-call(s32[512,128]{1,0:T(8,128)S(1)} %broadcast_in_dim.8.cell_ref, bf16[5,16,64,512]{3,2,1,0:T(8,128)(2,1)} %state_ref.3), custom_call_target="tpu_custom_call" | custom-call | flops 2684354560 | bytes 5242880 | tf_op jit(solution)/shard_map/pick_cells/pallas_call | solution.py:281
  91.5 7.8 %pick_x.1 = (f32[8,512]{1,0:T(8,128)S(1)}, f32[8,512]{1,0:T(8,128)S(1)}) custom-call(s32[512,128]{1,0:T(8,128)S(1)} %broadcast_in_dim.8.cell_ref, bf16[5,16,64,512]{3,2,1,0:T(8,128)(2,1)} %adj_ref.1, bf16[512,512]{1,0:T(8,128)(2,1)S(1)} %bitcast.11), custom_call_target="tpu_custom_call" | custom-call | flops 2684354560 | bytes 5242880 | tf_op jit(solution)/shard_map/pick_x/pallas_call | solution.py:319
  99.3 9.7 %line_y.1 = bf16[8,5,2,64,512]{4,3,2,1,0:T(8,128)(2,1)} custom-call(bf16[8,5,2,64,512]{4,3,2,1,0:T(8,128)(2,1)} %all_to_all.25.in_ref, bf16[512,512]{1,0:T(8,128)(2,1)S(1)} %bitcast.10), custom_call_target="tpu_custom_call" | custom-call | flops 2684354560 | bytes 10485760 | tf_op jit(solution)/shard_map/line_y/pallas_call | solution.py:46
  109.0 32.3 %all-to-all-done.1.in_ref = bf16[16,5,16,16,128]{4,3,2,1,0:T(8,128)(2,1)} async-done(((bf16[16,5,16,16,128]{4,3,2,1,0:T(8,128)(2,1)}), bf16[16,5,16,16,128]{4,3,2,1,0:T(8,128)(2,1)}, u32[]{:S(2)}, u32[]{:S(2)}) %all-to-all-start.1) | async-done | bytes 5242912 | tf_op jit(solution)/shard_map/all_to_all | solution.py:425
  141.3 64.5 %all_to_all.26.y_ref.field_ref = bf16[8,5,2,64,512]{4,3,2,1,0:T(8,128)(2,1)} all-to-all(bf16[8,5,2,64,512]{4,3,2,1,0:T(8,128)(2,1)} %line_y.1), channel_id=1, replica_groups=mesh['py'=8,'pz'=16] {'py'}, dimensions={0} | all-to-all | bytes 10485760 | tf_op jit(solution)/shard_map/all_to_all | solution.py:440
  205.8 5.6 %line_z.1 = bf16[16,5,16,16,128]{4,3,2,1,0:T(8,128)(2,1)} custom-call(bf16[16,5,16,16,128]{4,3,2,1,0:T(8,128)(2,1)} %all-to-all-done.1.in_ref, bf16[256,256]{1,0:T(8,128)(2,1)S(1)} %bitcast.12), custom_call_target="tpu_custom_call" | custom-call | flops 1342177280 | bytes 10485760 | tf_op jit(solution)/shard_map/line_z/pallas_call | solution.py:112
  211.4 6.2 %all-to-all-start.3 = ((bf16[16,5,16,16,128]{4,3,2,1,0:T(8,128)(2,1)}), bf16[16,5,16,16,128]{4,3,2,1,0:T(8,128)(2,1)}, u32[]{:S(2)}, u32[]{:S(2)}) async-start(bf16[16,5,16,16,128]{4,3,2,1,0:T(8,128)(2,1)} %line_z.1), calls=%async_computation.3 | async-start | bytes 10485760 | tf_op jit(solution)/shard_map/all_to_all | solution.py:442
  217.5 7.0 %pick_cells.5.y_ref = f32[8,512]{1,0:T(8,128)S(1)} custom-call(s32[512,128]{1,0:T(8,128)S(1)} %broadcast_in_dim.8.cell_ref, bf16[8,5,2,64,512]{4,3,2,1,0:T(8,128)(2,1)} %all_to_all.26.y_ref.field_ref), custom_call_target="tpu_custom_call" | custom-call | flops 2684354560 | bytes 5242880 | tf_op jit(solution)/shard_map/pick_cells/pallas_call | solution.py:281
  224.6 0.0 copy-start.1
  224.6 15.8 %update_xy.1.before_ref = f32[5,16,64,512]{3,2,1,0:T(8,128)} custom-call(bf16[5,16,64,512]{3,2,1,0:T(8,128)(2,1)} %adj_ref.1, bf16[5,16,64,512]{3,2,1,0:T(8,128)(2,1)} %state_ref.3, bf16[3,16,64,512]{3,2,1,0:T(8,128)(2,1)} %metric_ref.3, bf16[512,512]{1,0:T(8,128)(2,1)} %op_ref, bf16[8,5,2,64,512]{4,3,2,1,0:T(8,128)(2,1)} %all_to_all.26.y_ref.field_ref), custom_call_target="tpu_custom_call" | custom-call | flops 7927234560 | bytes 28311552 | tf_op jit(solution)/shard_map/update_xy/pallas_call | solution.py:190
  240.4 39.6 %all-to-all-done.3.z_ref = bf16[16,5,16,16,128]{4,3,2,1,0:T(8,128)(2,1)} async-done(((bf16[16,5,16,16,128]{4,3,2,1,0:T(8,128)(2,1)}), bf16[16,5,16,16,128]{4,3,2,1,0:T(8,128)(2,1)}, u32[]{:S(2)}, u32[]{:S(2)}) %all-to-all-start.3) | async-done | bytes 5242912 | tf_op jit(solution)/shard_map/all_to_all | solution.py:442
  280.0 7.8 %surface_terms.1.after_ref = f32[128,1,256]{2,1,0:T(1,128)} custom-call(s32[512,128]{1,0:T(8,128)S(1)} %broadcast_in_dim.8.cell_ref, bf16[16,5,16,16,128]{4,3,2,1,0:T(8,128)(2,1)} %all-to-all-done.3.z_ref, f32[8,512]{1,0:T(8,128)S(1)} %get-tuple-element.50.adj_ref, f32[8,512]{1,0:T(8,128)S(1)} %get-tuple-element.51.x_ref, f32[8,512]{1,0:T(8,128)S(1)} %pick_cells.5.y_ref, ...), custom_call_target="tpu_custom_call" | custom-call | flops 2684354560 | bytes 5242880 | tf_op jit(solution)/shard_map/surface_terms/pallas_call | solution.py:383
  287.7 4.8 %all-to-all-start.4 = ((f32[128,1,256]{2,1,0:T(1,128)}), f32[128,1,256]{2,1,0:T(1,128)S(1)}, u32[]{:S(2)}, u32[]{:S(2)}) async-start(f32[128,1,256]{2,1,0:T(1,128)} %surface_terms.1.after_ref), calls=%async_computation.4 | async-start | bytes 262144 | tf_op jit(solution)/shard_map/all_to_all | solution.py:453
  292.6 12.0 %update_z.1 = bf16[5,16,64,512]{3,2,1,0:T(8,128)(2,1)} custom-call(f32[5,16,64,512]{3,2,1,0:T(8,128)} %update_xy.1.before_ref, bf16[5,16,64,512]{3,2,1,0:T(8,128)(2,1)} %state_ref.3, bf16[3,16,64,512]{3,2,1,0:T(8,128)(2,1)} %metric_ref.3, bf16[16,5,16,16,128]{4,3,2,1,0:T(8,128)(2,1)} %all-to-all-done.3.z_ref, f32[128,1,256]{2,1,0:T(1,128)} %surface_terms.1.after_ref), custom_call_target="tpu_custom_call" | custom-call | flops 5242880000 | bytes 27262976 | tf_op jit(solution)/shard_map/update_z/pallas_call | solution.py:225
  304.6 0.0 all-to-all-done.4.terms_ref
  304.6 0.8 normalized.1
  (7 shorter events, 0.0 us)
Async XLA Ops:
  3.6 65.7 %copy-start = (bf16[16,5,16,16,128]{4,3,2,1,0:T(8,128)(2,1)}, bf16[16,5,16,16,128]{4,3,2,1,0:T(8,128)(2,1)S(1)}, u32[]{:S(2)}) copy-start(bf16[16,5,16,16,128]{4,3,2,1,0:T(8,128)(2,1)S(1)} %get-tuple-element.33) | copy-start | bytes 15728644
  69.3 9.7 %copy-start.5 = (bf16[4,3,128]{2,0,1:T(4,128)(2,1)S(1)}, bf16[4,3,128]{2,0,1:T(4,128)(2,1)}, u32[]{:S(2)}) copy-start(bf16[4,3,128]{2,0,1:T(4,128)(2,1)} %param.16) | copy-start | bytes 9220
  69.3 9.7 %copy-start.4 = (bf16[256,256]{1,0:T(8,128)(2,1)S(1)}, bf16[256,256]{1,0:T(8,128)(2,1)}, u32[]{:S(2)}) copy-start(bf16[256,256]{1,0:T(8,128)(2,1)} %param.14) | copy-start | bytes 393220
  69.3 9.8 %copy-start.3 = (bf16[512,512]{1,0:T(8,128)(2,1)S(1)}, bf16[512,512]{1,0:T(8,128)(2,1)}, u32[]{:S(2)}) copy-start(bf16[512,512]{1,0:T(8,128)(2,1)} %param.13) | copy-start | bytes 1572868
  69.3 10.1 %copy-start.2 = (bf16[512,512]{1,0:T(8,128)(2,1)S(1)}, bf16[512,512]{1,0:T(8,128)(2,1)}, u32[]{:S(2)}) copy-start(bf16[512,512]{1,0:T(8,128)(2,1)} %op_ref) | copy-start | bytes 1572868
  69.3 10.3 %copy-start.6 = (s32[4,128]{1,0:T(4,128)S(1)}, s32[4,128]{1,0:T(4,128)}, u32[]{:S(2)}) copy-start(s32[4,128]{1,0:T(4,128)} %param.15) | copy-start | bytes 6148
  69.3 72.0 %all-to-all-start.1 = ((bf16[16,5,16,16,128]{4,3,2,1,0:T(8,128)(2,1)}), bf16[16,5,16,16,128]{4,3,2,1,0:T(8,128)(2,1)}, u32[]{:S(2)}, u32[]{:S(2)}) async-start(bf16[16,5,16,16,128]{4,3,2,1,0:T(8,128)(2,1)} %copy-done), calls=%async_computation.1 | async-start | bytes 10485760 | tf_op jit(solution)/shard_map/all_to_all | solution.py:425
  211.4 68.6 %all-to-all-start.3 = ((bf16[16,5,16,16,128]{4,3,2,1,0:T(8,128)(2,1)}), bf16[16,5,16,16,128]{4,3,2,1,0:T(8,128)(2,1)}, u32[]{:S(2)}, u32[]{:S(2)}) async-start(bf16[16,5,16,16,128]{4,3,2,1,0:T(8,128)(2,1)} %line_z.1), calls=%async_computation.3 | async-start | bytes 10485760 | tf_op jit(solution)/shard_map/all_to_all | solution.py:442
  224.6 55.4 %copy-start.1 = (bf16[512,256]{1,0:T(8,128)(2,1)S(1)}, bf16[512,256]{1,0:T(8,128)(2,1)}, u32[]{:S(2)}) copy-start(bf16[512,256]{1,0:T(8,128)(2,1)} %basis_ref.1) | copy-start | bytes 786436
  287.7 16.9 %all-to-all-start.4 = ((f32[128,1,256]{2,1,0:T(1,128)}), f32[128,1,256]{2,1,0:T(1,128)S(1)}, u32[]{:S(2)}, u32[]{:S(2)}) async-start(f32[128,1,256]{2,1,0:T(1,128)} %surface_terms.1.after_ref), calls=%async_computation.4 | async-start | bytes 262144 | tf_op jit(solution)/shard_map/all_to_all | solution.py:453
